TPU v7x, 32 devices: a whole 2x2x4 slice. The times are simulated.
32 devices in a mesh: groups: 2 (over x), seq: 16 (over z, y, core).
Axes of the slice: x: 2, y: 2, z: 4, core: 2. Of those that a mesh axis runs over, the one named last changes fastest.
Arguments:
- mixer_input: bfloat16 [4096, 6144], P(('groups', 'seq')), parts along dimension 0, may hold values from -6 to 6
- gate_input: bfloat16 [4096, 4096], P(('groups', 'seq')), parts along dimension 0, may hold values from -6 to 6
- step_raw: bfloat16 [4096, 64], P(('groups', 'seq')), parts along dimension 0, may hold values from -4 to 12, as said below
- conv_weight: bfloat16 [4, 6144], replicated, may hold values from -3 to 3
- conv_bias: float32 [6144], replicated, may hold values from -0.7 to -0.3
- step_bias: float32 [128], P('groups'), parts along dimension 0, may hold values from -13 to -2
- decay_log: float32 [128], P('groups'), parts along dimension 0, may hold values from -0.4 to 0.4
- skip_gain: float32 [64], replicated, may hold values from 0.5 to 1.5
- norm_gain: float32 [4096], replicated, may hold values from 0.5 to 1.5
Outputs:
- mixer_out: bfloat16 [4096, 4096], P(('groups', 'seq')), parts along dimension 0
There are 2 independent parts, one for each index of `groups`. A program takes and returns all parts, laid end to end along the dimension named above; an argument that names none is the same for every part. Nothing has to cross between parts.
Inputs may be any that keep to these rules, and one draw needn't show every extreme that they name: `step_raw`: raw step sizes; each head's step sizes change by bounded factors between positions.
All inputs are finite; a program needn't handle non-finite values.
Results may differ from a plain program's by a relative error of at most 0.006.
Values may be sent and summed in bfloat16 or wider, within the bound.
No kernel may reach another device: no remote copies, remote signals or barrier semaphores. Data moves between devices by JAX's collectives and lax.ppermute only.
A program may use at most 64 MiB of HBM per device.

v0:
```python
import jax
import jax.numpy as jnp
from jax import lax
from jax.sharding import PartitionSpec as P

HEADS = 64
HEAD_DIM = 64
STATE = 128
HEAD_GROUPS = 8
SPAN = 128


def from_behind(value, axis, by):
    size = lax.axis_size(axis)
    pairs = [(i, i + by) for i in range(size) if 0 <= i + by < size]
    return lax.ppermute(value, axis, pairs)


def convolve(mixer_input, conv_weight, conv_bias):
    kernel_size = conv_weight.shape[0]
    row_count = mixer_input.shape[0]
    tail_rows = mixer_input[row_count - (kernel_size - 1) :]
    previous = from_behind(tail_rows, "seq", 1)
    extended = jnp.concatenate([previous, mixer_input], axis=0)
    activation = jnp.zeros(mixer_input.shape, jnp.float32) + conv_bias[None, :]
    for offset in range(kernel_size):
        activation = activation + conv_weight[offset][None, :].astype(jnp.float32) * extended[
            offset : offset + row_count
        ].astype(jnp.float32)
    return jax.nn.silu(activation).astype(jnp.bfloat16)


def span_terms(values, write_keys, read_keys, step_sizes, decay_rates):
    span_len = values.shape[1]
    cumulative = jnp.cumsum(step_sizes * decay_rates[None, None], axis=1)
    totals = cumulative[:, -1]
    scores = jnp.einsum(
        "nqgk,nsgk->ngqs", read_keys, write_keys, preferred_element_type=jnp.float32
    )
    along_time = jnp.transpose(cumulative, (0, 2, 3, 1))
    log_gap = along_time[..., :, None] - along_time[..., None, :]
    causal = lax.broadcasted_iota(jnp.int32, (span_len, span_len), 0) >= lax.broadcasted_iota(
        jnp.int32, (span_len, span_len), 1
    )
    decays = jnp.exp(jnp.where(causal, log_gap, 0.0))
    steps_last = jnp.transpose(step_sizes, (0, 2, 3, 1))
    weights = jnp.where(causal, scores[:, :, None] * decays * steps_last[..., None, :], 0.0).astype(
        jnp.bfloat16
    )
    inside = jnp.einsum("nghqs,nsghp->nqghp", weights, values, preferred_element_type=jnp.float32)
    tail_weights = jnp.exp(totals[:, None] - cumulative) * step_sizes
    written = (write_keys[:, :, :, None, :].astype(jnp.float32) * tail_weights[..., None]).astype(
        jnp.bfloat16
    )
    increment = jnp.einsum(
        "nsghp,nsghk->nghpk", values, written, preferred_element_type=jnp.float32
    )
    return (cumulative, totals, inside, increment)


def read_out(values, read_keys, cumulative, inside, starts, skip_terms):
    carried_part = jnp.einsum(
        "nqgk,nghpk->nqghp",
        read_keys,
        starts.astype(jnp.bfloat16),
        preferred_element_type=jnp.float32,
    )
    return (
        inside
        + carried_part * jnp.exp(cumulative)[..., None]
        + skip_terms[None, None, :, :, None] * values.astype(jnp.float32)
    )


def combine(earlier, later):
    return (earlier[0] + later[0], jnp.exp(later[0])[..., None, None] * earlier[1] + later[1])


def shards(
    mixer_input,
    gate_input,
    step_raw,
    conv_weight,
    conv_bias,
    step_bias,
    decay_log,
    skip_gain,
    norm_gain,
):
    convolved = convolve(mixer_input, conv_weight, conv_bias)
    row_count = convolved.shape[0]
    inner_width = HEADS * HEAD_DIM
    key_width = HEAD_GROUPS * STATE
    devices = lax.axis_size("seq")
    local_heads = HEADS // devices
    slot_count = devices // HEAD_GROUPS
    write_slots = jnp.broadcast_to(
        convolved[:, inner_width : inner_width + key_width].reshape(
            row_count, HEAD_GROUPS, 1, STATE
        ),
        (row_count, HEAD_GROUPS, slot_count, STATE),
    )
    read_slots = jnp.broadcast_to(
        convolved[:, inner_width + key_width :].reshape(row_count, HEAD_GROUPS, 1, STATE),
        (row_count, HEAD_GROUPS, slot_count, STATE),
    )
    paired = jnp.concatenate([write_slots, read_slots], axis=3).reshape(
        row_count, devices * 2 * STATE
    )
    own_values, own_keys, own_steps = (
        lax.all_to_all(convolved[:, :inner_width], "seq", split_axis=1, concat_axis=0, tiled=True),
        lax.all_to_all(paired, "seq", split_axis=1, concat_axis=0, tiled=True),
        lax.all_to_all(step_raw, "seq", split_axis=1, concat_axis=0, tiled=True),
    )
    first_head = lax.axis_index("seq") * local_heads
    bias_here = lax.dynamic_slice_in_dim(step_bias, first_head, local_heads)
    decay_rates = -jnp.exp(lax.dynamic_slice_in_dim(decay_log, first_head, local_heads)).reshape(
        1, local_heads
    )
    skip_terms = lax.dynamic_slice_in_dim(skip_gain, first_head, local_heads).reshape(
        1, local_heads
    )
    full_rows = own_values.shape[0]
    span_count = full_rows // SPAN
    values = own_values.reshape(span_count, SPAN, 1, local_heads, HEAD_DIM)
    write_keys = own_keys[:, :STATE].reshape(span_count, SPAN, 1, STATE)
    read_keys = own_keys[:, STATE:].reshape(span_count, SPAN, 1, STATE)
    step_sizes = jax.nn.softplus(own_steps.astype(jnp.float32) + bias_here[None, :]).reshape(
        span_count, SPAN, 1, local_heads
    )
    cumulative, totals, inside, increment = span_terms(
        values, write_keys, read_keys, step_sizes, decay_rates
    )
    _, running = lax.associative_scan(combine, (totals, increment), axis=0)
    starts = jnp.concatenate([jnp.zeros_like(running[:1]), running[:-1]], axis=0)
    outputs = read_out(values, read_keys, cumulative, inside, starts, skip_terms).reshape(
        full_rows, local_heads * HEAD_DIM
    )
    merged = lax.all_to_all(outputs, "seq", split_axis=0, concat_axis=1, tiled=True)
    gated_rows = merged * jax.nn.silu(gate_input.astype(jnp.float32))
    grouped = gated_rows.reshape(row_count, HEAD_GROUPS, inner_width // HEAD_GROUPS)
    inverse_rms = lax.rsqrt(jnp.mean(grouped * grouped, axis=-1, keepdims=True) + 1e-05)
    normed = (grouped * inverse_rms).reshape(row_count, inner_width) * norm_gain[None, :]
    return normed.astype(jnp.bfloat16)


def solution(mesh):
    in_specs = (
        P(("groups", "seq"), None),
        P(("groups", "seq"), None),
        P(("groups", "seq"), None),
        P(),
        P(),
        P("groups"),
        P("groups"),
        P(),
        P(),
    )
    out_specs = P(("groups", "seq"), None)
    return jax.shard_map(shards, mesh=mesh, in_specs=in_specs, out_specs=out_specs, check_vma=False)
```

profile of v0, /device:TPU:0, one launch (start us, length us, event | category | flops | bytes accessed | tf_op | source)
XLA Modules:
  0.0 213.9 jit_solution(14222437705074875251)
XLA Ops:
  0.0 7.4 %all-to-all-start.2 = ((bf16[128,16,4]{0,2,1:T(4,128)(2,1)}), bf16[128,16,4]{0,2,1:T(4,128)(2,1)S(1)}, u32[]{:S(2)}, u32[]{:S(2)}) async-start(bf16[128,16,4]{0,2,1:T(4,128)(2,1)} %bitcast.137), calls=%async_computation.2 | async-start | bytes 32768 | tf_op jit(solution)/shard_map/all_to_all | solution.py:113
  7.4 0.9 slice.137
  8.3 2.3 %collective-permute-start = (bf16[3,6144]{1,0:T(4,128)(2,1)S(1)}, bf16[3,6144]{1,0:T(4,128)(2,1)S(1)}, u32[]{:S(2)}, u32[]{:S(2)}) collective-permute-start(bf16[3,6144]{1,0:T(4,128)(2,1)S(1)} %slice.137), channel_id=1, source_target_pairs={{0,1},{1,2},{2,3},{3,4},{4,5},{5,6},{6,7},{7,8},{8,9},{9,10},{10,1... | collective-permute-start | bytes 110600 | tf_op jit(solution)/shard_map/ppermute | solution.py:16
  10.6 1.0 slice_convert_fusion.3
  11.7 4.6 %multiply_convert_fusion.1 = bf16[128,6144]{1,0:T(8,128)(2,1)S(1)} fusion(bf16[128,6144]{1,0:T(8,128)(2,1)} %param.9, bf16[3,6144]{1,0:T(4,128)(2,1)S(1)} %collective-permute-done, f32[6144]{0:T(1024)S(1)} %bitcast.131, f32[6144]{0:T(1024)S(1)} %bitcast.132, f32[6144]{0:T(1024)S(1)} %bitcast.130, f32[6144]{0:T(1024)S(1)} %bitcast.129, f32[6144]{0:T(1024)} %param.13), kind=kLoop, calls=%fused_computation.2 | loop fusion | flops 20447232 | bytes 3305472 | tf_op jit(solution)/shard_map/convert_element_type | solution.py:30
  16.3 1.2 copy-done.3
  17.5 0.1 copy_bitcast_fusion
  17.7 0.1 broadcast_in_dim.24
  17.8 0.1 broadcast_in_dim.22
  17.9 1.1 pad_maximum_fusion.1
  19.0 8.0 %all-to-all-start.1 = ((bf16[128,16,256]{2,0,1:T(8,128)(2,1)}), bf16[128,16,256]{2,0,1:T(8,128)(2,1)S(1)}, u32[]{:S(2)}, u32[]{:S(2)}) async-start(bf16[128,16,256]{2,0,1:T(8,128)(2,1)} %bitcast.7), calls=%async_computation.1 | async-start | bytes 2097152 | tf_op jit(solution)/shard_map/all_to_all | solution.py:112
  27.2 0.6 dynamic_slice.11
  28.0 1.4 copy.89
  29.4 1.4 fusion.41
  30.9 0.1 slice.157
  31.0 0.1 slice.153
  31.1 1.3 copy.107
  32.4 17.6 %all-to-all-done.1 = bf16[128,16,256]{2,0,1:T(8,128)(2,1)S(1)} async-done(((bf16[128,16,256]{2,0,1:T(8,128)(2,1)}), bf16[128,16,256]{2,0,1:T(8,128)(2,1)S(1)}, u32[]{:S(2)}, u32[]{:S(2)}) %all-to-all-start.1) | async-done | bytes 1048608 | tf_op jit(solution)/shard_map/all_to_all | solution.py:112
  50.0 6.9 %all-to-all-start = ((bf16[128,16,256]{0,2,1:T(8,128)(2,1)}), bf16[128,16,256]{0,2,1:T(8,128)(2,1)S(1)}, u32[]{:S(2)}, u32[]{:S(2)}) async-start(bf16[128,16,256]{0,2,1:T(8,128)(2,1)} %bitcast.128), calls=%async_computation | async-start | bytes 2097152 | tf_op jit(solution)/shard_map/all_to_all | solution.py:111
  57.2 0.1 slice.169
  57.5 0.5 copy.94
  58.0 0.7 copy.99
  58.8 0.1 copy.101
  58.9 0.7 copy.97
  59.6 1.0 copy.90
  60.6 0.1 fusion.26
  60.8 0.6 copy.102
  61.4 0.6 copy.92
  62.0 0.8 exponential_reduce_fusion.1
  62.8 0.2 exponential_reduce_fusion
  63.1 1.2 convert_element_type.75
  64.2 1.5 fusion.42
  65.7 14.2 %all-to-all-done = bf16[128,16,256]{0,2,1:T(8,128)(2,1)S(1)} async-done(((bf16[128,16,256]{0,2,1:T(8,128)(2,1)}), bf16[128,16,256]{0,2,1:T(8,128)(2,1)S(1)}, u32[]{:S(2)}, u32[]{:S(2)}) %all-to-all-start) | async-done | bytes 1048608 | tf_op jit(solution)/shard_map/all_to_all | solution.py:111
  79.8 3.5 %fusion.5 = f32[16,4,64,128]{3,2,1,0:T(8,128)S(1)} fusion(bf16[16,128,4,64]{1,3,2,0:T(8,128)(2,1)S(1)} %bitcast.114, f32[16,128,4]{1,2,0:T(4,128)S(1)} %copy.95, f32[16,128,128]{2,1,0:T(8,128)} %convert_element_type.75), kind=kOutput, calls=%fused_computation.12 | convolution fusion | flops 136314880 | bytes 4227072 | tf_op jit(solution)/shard_map/nsghp,nsghk->nghpk/dot_general | solution.py:55
  83.3 0.7 slice_bitcast_fusion.2
  84.0 0.2 slice_add_fusion
  84.2 0.1 slice_add_fusion.1
  84.5 0.3 copy-done.14
  84.9 0.2 copy-done.2
  85.1 0.7 pad_maximum_fusion.4
  85.9 5.1 %pad.29 = f32[4,1,4,64,128]{4,3,2,0,1:T(8,128)} pad(f32[2,1,4,64,128]{4,3,2,0,1:T(8,128)} %pad_maximum_fusion.4, f32[]{:T(128)} %constant.26.clone.1), padding=0_1_1x0_0_0x0_0_0x0_0_0x0_0_0 | pad | bytes 786436 | tf_op jit(solution)/shard_map/pad | solution.py:134
  91.0 3.3 %pad.30 = f32[4,1,4,64,128]{4,3,2,0,1:T(8,128)} pad(f32[2,1,4,64,128]{4,3,2,0,1:T(8,128)S(1)} %pad_add_fusion, f32[]{:T(128)} %constant.26.clone.1), padding=1_0_1x0_0_0x0_0_0x0_0_0x0_0_0 | pad | bytes 786436 | tf_op jit(solution)/shard_map/pad | solution.py:134
  94.3 2.1 add.150
  96.3 1.3 fusion.21
  97.7 0.8 pad_maximum_fusion.3
  98.5 9.2 %pad.31 = f32[8,1,4,64,128]{4,3,2,0,1:T(8,128)} pad(f32[4,1,4,64,128]{4,3,2,0,1:T(8,128)} %pad_maximum_fusion.3, f32[]{:T(128)} %constant.26.clone.1), padding=0_1_1x0_0_0x0_0_0x0_0_0x0_0_0 | pad | bytes 1572868 | tf_op jit(solution)/shard_map/pad | solution.py:134
  107.8 9.2 %pad.32 = f32[8,1,4,64,128]{4,3,2,0,1:T(8,128)} pad(f32[4,1,4,64,128]{4,3,2,0,1:T(8,128)} %add.150, f32[]{:T(128)} %constant.26.clone.1), padding=1_0_1x0_0_0x0_0_0x0_0_0x0_0_0 | pad | bytes 1572868 | tf_op jit(solution)/shard_map/pad | solution.py:134
  117.0 2.9 %add.152 = f32[8,1,4,64,128]{4,3,2,0,1:T(8,128)} add(f32[8,1,4,64,128]{4,3,2,0,1:T(8,128)} %pad.31, f32[8,1,4,64,128]{4,3,2,0,1:T(8,128)} %pad.32) | non-fusion elementwise | flops 262144 | bytes 3145728 | tf_op jit(solution)/shard_map/add | solution.py:134
  119.9 0.2 fusion.20
  120.1 0.7 copy-done.8
  120.8 11.1 %pad.48 = f32[15,1,4,64,128]{4,3,2,0,1:T(8,128)} pad(f32[8,1,4,64,128]{4,3,2,0,1:T(8,128)S(1)} %pad_maximum_fusion.2, f32[]{:T(128)} %constant.26.clone.1), padding=0_0_1x0_0_0x0_0_0x0_0_0x0_0_0 | pad | bytes 3014660 | tf_op jit(solution)/shard_map/slice | solution.py:135
  132.0 12.4 %pad.85 = f32[16,1,4,64,128]{4,3,2,0,1:T(8,128)S(1)} pad(f32[8,1,4,64,128]{4,3,2,0,1:T(8,128)} %add.152, f32[]{:T(128)} %constant.26.clone.1), padding=1_0_1x0_0_0x0_0_0x0_0_0x0_0_0 | pad | bytes 3145732
  144.3 2.0 add_convert_fusion
  146.4 1.6 fusion
  148.1 0.6 fusion.6
  148.6 54.1 %all_to_all.67 = f32[16,128,256]{1,2,0:T(8,128)} all-to-all(f32[16,128,256]{1,2,0:T(8,128)S(1)} %bitcast.118), channel_id=1, replica_groups=mesh['groups'=2,'seq'=16] {'seq'}, dimensions={0} | all-to-all | bytes 4194304 | tf_op jit(solution)/shard_map/all_to_all | solution.py:139
  202.7 2.0 copy.108
  204.7 0.6 fusion.34
  205.3 3.0 %copy.111 = f32[16,8,8,512]{3,2,1,0:T(8,128)} copy(f32[16,8,8,512]{3,1,2,0:T(8,128)S(1)} %bitcast.122) | data formatting | bytes 4194304
  208.3 1.8 reduce_sum.9
  210.2 0.1 copy.105
  210.3 0.2 mul.299
  210.5 1.6 copy.112
  212.2 1.7 multiply_convert_fusion.3
  (68 shorter events, 1.6 us)
Async XLA Ops:
  0.0 19.0 %all-to-all-start.2 = ((bf16[128,16,4]{0,2,1:T(4,128)(2,1)}), bf16[128,16,4]{0,2,1:T(4,128)(2,1)S(1)}, u32[]{:S(2)}, u32[]{:S(2)}) async-start(bf16[128,16,4]{0,2,1:T(4,128)(2,1)} %bitcast.137), calls=%async_computation.2 | async-start | bytes 32768 | tf_op jit(solution)/shard_map/all_to_all | solution.py:113
  8.3 3.4 %collective-permute-start = (bf16[3,6144]{1,0:T(4,128)(2,1)S(1)}, bf16[3,6144]{1,0:T(4,128)(2,1)S(1)}, u32[]{:S(2)}, u32[]{:S(2)}) collective-permute-start(bf16[3,6144]{1,0:T(4,128)(2,1)S(1)} %slice.137), channel_id=1, source_target_pairs={{0,1},{1,2},{2,3},{3,4},{4,5},{5,6},{6,7},{7,8},{8,9},{9,10},{10,1... | collective-permute-start | bytes 110600 | tf_op jit(solution)/shard_map/ppermute | solution.py:16
  16.3 1.2 copy-start.3
  17.9 9.2 %copy-start.16 = (f32[64]{0:T(128)S(1)}, f32[64]{0:T(128)}, u32[]{:S(2)}) copy-start(f32[64]{0:T(128)} %param.14) | copy-start | bytes 772
  17.9 9.3 %copy-start.17 = (f32[64]{0:T(128)S(1)}, f32[64]{0:T(128)}, u32[]{:S(2)}) copy-start(f32[64]{0:T(128)} %param.16) | copy-start | bytes 772
  17.9 9.9 %copy-start.18 = (f32[64]{0:T(128)S(1)}, f32[64]{0:T(128)}, u32[]{:S(2)}) copy-start(f32[64]{0:T(128)} %param.15) | copy-start | bytes 772
  19.0 31.0 %all-to-all-start.1 = ((bf16[128,16,256]{2,0,1:T(8,128)(2,1)}), bf16[128,16,256]{2,0,1:T(8,128)(2,1)S(1)}, u32[]{:S(2)}, u32[]{:S(2)}) async-start(bf16[128,16,256]{2,0,1:T(8,128)(2,1)} %bitcast.7), calls=%async_computation.1 | async-start | bytes 2097152 | tf_op jit(solution)/shard_map/all_to_all | solution.py:112
  29.4 1.7 slice-start.1
  50.0 29.8 %all-to-all-start = ((bf16[128,16,256]{0,2,1:T(8,128)(2,1)}), bf16[128,16,256]{0,2,1:T(8,128)(2,1)S(1)}, u32[]{:S(2)}, u32[]{:S(2)}) async-start(bf16[128,16,256]{0,2,1:T(8,128)(2,1)} %bitcast.128), calls=%async_computation | async-start | bytes 2097152 | tf_op jit(solution)/shard_map/all_to_all | solution.py:111
  63.0 1.2 copy-start.4
  84.2 1.0 copy-start.2
  84.2 0.7 copy-start.14
  91.0 6.7 %slice-start = ((f32[8,1,4,64,128]{4,3,2,0,1:T(8,128)}), f32[1,1,4,64,128]{4,3,2,0,1:T(8,128)S(1)}, s32[]{:S(2)}) async-start(f32[8,1,4,64,128]{4,3,2,0,1:T(8,128)} %copy-done.2), calls=%async_computation.4 | async-start | bytes 262144 | tf_op jit(solution)/shard_map/slice | solution.py:134
  107.7 12.1 %copy-start.13 = (f32[7,4]{1,0:T(8,128)S(1)}, f32[7,4]{1,0:T(8,128)}, u32[]{:S(2)}) copy-start(f32[7,4]{1,0:T(8,128)} %copy.97) | copy-start | bytes 340
  117.0 2.9 %copy-start = (f32[8,1,4,64,128]{4,3,2,0,1:T(8,128)S(1)}, f32[8,1,4,64,128]{4,3,2,0,1:T(8,128)}, u32[]{:S(2)}) copy-start(f32[8,1,4,64,128]{4,3,2,0,1:T(8,128)} %pad.31) | copy-start | bytes 3145732
  117.0 2.9 %copy-start.1 = (f32[8,1,4,64,128]{4,3,2,0,1:T(8,128)S(1)}, f32[8,1,4,64,128]{4,3,2,0,1:T(8,128)}, u32[]{:S(2)}) copy-start(f32[8,1,4,64,128]{4,3,2,0,1:T(8,128)} %pad.32) | copy-start | bytes 3145732
  119.8 0.9 copy-start.8
  144.3 2.0 copy-start.7
  144.3 2.1 copy-start.10
  144.3 2.1 copy-start.11
  146.4 1.6 copy-start.5
  146.4 1.6 copy-start.9
  146.4 1.6 copy-start.15
  202.7 2.0 copy-start.6
  210.5 1.7 copy-start.12
where the time goes:
time: 218 us; the launch traced here: 214 us
  local copies, waits for them, and re-layouts  71.4 us (33%)
  blocking collectives  54.1 us (25%)
  waiting for transfers between devices  31.7 us (15%)
  starting transfers between devices  24.6 us (11%)
  other arithmetic  24.5 us (11%)
  matrix products  7.12 us (3%)
    all_to_all x1, blocking collectives, shards(): lax.all_to_all(outputs, 'seq', split_axis=0, concat_axis=1, tiled=True)  54.1 us
    pad x4, local copies, waits for them, and re-layouts, shards(): _, running = lax.associative_scan(combine, (totals, increment), axis=0)  26.8 us
    unnamed x42, local copies, waits for them, and re-layouts  19.5 us
    all_to_all x1, waiting for transfers between devices, shards(): lax.all_to_all(paired, 'seq', split_axis=1, concat_axis=0, tiled=True)  17.6 us
    all_to_all x1, waiting for transfers between devices, shards(): lax.all_to_all(convolved[:, :inner_width], 'seq', split_axis=1, concat_ax...  14.2 us
    slice x1, local copies, waits for them, and re-layouts, shards(): running[:-1]  11.1 us
    all_to_all x1, starting transfers between devices, shards(): lax.all_to_all(paired, 'seq', split_axis=1, concat_axis=0, tiled=True)  8.03 us
    all_to_all x1, starting transfers between devices, shards(): lax.all_to_all(step_raw, 'seq', split_axis=1, concat_axis=0, tiled=True)  7.39 us
  transfers between devices with their start and end apart: 4, of which 2 were waited for; matrix products, arithmetic and copies ran while one was open for 10% of the time, Pallas kernels for 0%

commit v1 on v0

v1 whole, which is shorter than its diff:
```python
import functools

import jax
import jax.numpy as jnp
from jax import lax
from jax.experimental import pallas as pl
from jax.experimental.pallas import tpu as pltpu
from jax.sharding import PartitionSpec as P

HEADS = 64
HEAD_DIM = 64
STATE = 128
GROUPS = 8
PER_GROUP = HEADS // GROUPS
GROUP_COLS = PER_GROUP * HEAD_DIM
INNER = HEADS * HEAD_DIM
KEYS = GROUPS * STATE
CONV_COLS = INNER + 2 * KEYS
SPAN = 128
LANES = 128
TILES = GROUP_COLS // LANES
PARTS = 2
PART_GROUPS = GROUPS // PARTS
HALF_GROUPS = PART_GROUPS // 2
QUARTER_GROUPS = HALF_GROUPS // 2
HALF_TILES = HALF_GROUPS * TILES
QUARTER_TILES = QUARTER_GROUPS * TILES
HALF_ROWS = HALF_TILES * STATE
QUARTER_ROWS = QUARTER_TILES * STATE
F32 = jnp.float32
BF16 = jnp.bfloat16
VMEM_LIMIT = 24 * 1024 * 1024


def extra_rows(tiles):
    return -(-2 * tiles // 16) * 16


def decay_rows(tiles):
    return -(-tiles // 8) * 8


def call(body, outs, *args, scratch=(), cost=None):
    specs = [pl.BlockSpec(memory_space=pltpu.VMEM) for _ in args]
    flops, transcendentals = cost or (100000, 0)
    moved = sum(a.size * a.dtype.itemsize for a in args) + sum(
        o[0][0] * o[0][1] * jnp.dtype(o[1]).itemsize for o in outs
    )
    return pl.pallas_call(
        body,
        out_shape=[jax.ShapeDtypeStruct(shape, kind) for shape, kind in outs],
        in_specs=specs,
        out_specs=[pl.BlockSpec(memory_space=pltpu.VMEM) for _ in outs],
        scratch_shapes=list(scratch),
        compiler_params=pltpu.CompilerParams(vmem_limit_bytes=VMEM_LIMIT),
        cost_estimate=pl.CostEstimate(
            flops=flops, bytes_accessed=moved, transcendentals=transcendentals
        ),
    )(*args)


def dot(a, b, dims=((1,), (0,))):
    return lax.dot_general(a, b, (dims, ((), ())), preferred_element_type=F32)


def silu(v):
    return v / (1.0 + jnp.exp(-v))


def pieces(v, count):
    found = []
    for _ in range(count):
        piece = v.astype(BF16)
        found.append(piece)
        v = v - piece.astype(F32)
    return found


def spread(group):
    row = lax.broadcasted_iota(jnp.int32, (2 * HEADS, GROUP_COLS), 0)
    lane = lax.broadcasted_iota(jnp.int32, (2 * HEADS, GROUP_COLS), 1)
    head = group * PER_GROUP + lane // HEAD_DIM
    return ((row == head) | (row == head + HEADS)).astype(BF16)


def columns(group, width, start=0):
    return pl.ds(pl.multiple_of(start + group * width, LANES), width)


def convolve_into(rows, padded, weight_ref, bias_ref, cols):
    total = bias_ref[:, cols]
    for tap in range(4):
        total = total + weight_ref[tap : tap + 1, cols].astype(F32) * padded[5 + tap : 5 + tap + rows, :]
    return silu(total).astype(BF16)


def prepare(x, step, decay_log, weight, bias, conv, both, both_t, tail_pair, carry_pair, total_pair, padded):
    @pl.loop(0, CONV_COLS // 512)
    def _(i):
        cols = columns(i, 512)
        padded[0:8, :] = jnp.zeros((8, 512), F32)
        padded[8 : 8 + SPAN, :] = x[:, cols].astype(F32)
        conv[:, cols] = convolve_into(SPAN, padded, weight, bias, cols)

    sizes = step[...]
    log_decay = sizes * -jnp.exp(decay_log[...])
    row = lax.broadcasted_iota(jnp.int32, (SPAN, SPAN), 0)
    lane = lax.broadcasted_iota(jnp.int32, (SPAN, SPAN), 1)
    lower = (row >= lane).astype(BF16)
    cumulative = sum(dot(lower, piece) for piece in pieces(log_decay, 3))
    total = cumulative[SPAN - 1 : SPAN, :]
    tail = jnp.exp(total - cumulative) * sizes
    joined = jnp.concatenate([cumulative, sizes], axis=1)
    both[...] = joined
    both_t[...] = joined.T
    tail_pair[...] = jnp.concatenate(pieces(tail, 2), axis=1)
    carry_pair[...] = jnp.concatenate(pieces(jnp.exp(cumulative), 2), axis=1)
    total_pair[...] = jnp.concatenate(
        pieces(jnp.broadcast_to(jnp.exp(total), (16, HEADS)), 2), axis=1
    )


def load_fixed(conv, fix, cols):
    return jnp.concatenate([fix[:, cols], conv[16:, cols]], axis=0)


def put_decays(send, tiles, decays):
    high = [d.astype(BF16).astype(F32) for d in decays]
    low = [d - h for d, h in zip(decays, high)]
    rows = high + low
    spare = extra_rows(tiles) - len(rows)
    block = jnp.concatenate(rows + [jnp.zeros((spare, LANES), F32)] * (spare > 0), axis=0)
    send[tiles * STATE : tiles * STATE + extra_rows(tiles), :] = block.astype(BF16)


def increments(part, *refs):
    first = part == 0
    if first:
        (x, halo, weight, bias, conv, tail_pair, total_pair, send, keep, keep_decay, fix, padded) = refs

        @pl.loop(0, CONV_COLS // 512)
        def _(i):
            cols = columns(i, 512)
            padded[0:8, :] = jnp.zeros((8, 512), F32)
            padded[5:8, :] = halo[:, cols].astype(F32)
            padded[8:24, :] = x[0:16, cols].astype(F32)
            fix[:, cols] = convolve_into(16, padded, weight, bias, cols)
    else:
        conv, fix, tail_pair, total_pair, send, keep, keep_decay = refs
    core = lax.axis_index("seq") & 1
    for target, side in ((send, 1 - core), (keep, core)):
        decays = []
        for j in range(HALF_GROUPS):
            group = part * PART_GROUPS + side * HALF_GROUPS + j
            to_channels = spread(group)
            scale = dot(tail_pair[...], to_channels)
            values = load_fixed(conv, fix, columns(group, GROUP_COLS)).astype(F32)
            keys = load_fixed(conv, fix, columns(group, STATE, INNER))
            grown = dot(keys, (values * scale).astype(BF16), ((0,), (0,)))
            decay = dot(total_pair[...], to_channels)
            for t in range(TILES):
                at = (j * TILES + t) * STATE
                target[at : at + STATE, :] = grown[:, t * LANES : (t + 1) * LANES].astype(target.dtype)
                decays.append(decay[0:1, t * LANES : (t + 1) * LANES])
        if target is send:
            put_decays(send, HALF_TILES, decays)
        else:
            for t, d in enumerate(decays):
                keep_decay[t : t + 1, :] = d


def tile_rows(t):
    return pl.ds(pl.multiple_of(t * STATE, STATE), STATE)


def received_decays(recv, tiles, scratch):
    rows = recv[tiles * STATE : tiles * STATE + extra_rows(tiles), :].astype(F32)
    scratch[0:tiles, :] = rows[0:tiles] + rows[tiles : 2 * tiles]


def join_cores(keep, keep_decay, recv, send, own, own_decay, other):
    me = lax.axis_index("seq")
    first = (me & 1) == 0
    y = (me >> 1) & 1
    received_decays(recv, HALF_TILES, other)

    def joined(t):
        mine, theirs = keep[tile_rows(t), :], recv[tile_rows(t), :].astype(F32)
        decay_mine, decay_theirs = keep_decay[pl.ds(t, 1), :], other[pl.ds(t, 1), :]
        early, late = jnp.where(first, mine, theirs), jnp.where(first, theirs, mine)
        return jnp.where(first, decay_theirs, decay_mine) * early + late, decay_mine * decay_theirs

    decays = []
    for t in range(QUARTER_TILES):
        state, decay = joined((1 - y) * QUARTER_TILES + t)
        send[t * STATE : (t + 1) * STATE, :] = state.astype(BF16)
        decays.append(decay)
    put_decays(send, QUARTER_TILES, decays)
    for t in range(QUARTER_TILES):
        state, decay = joined(y * QUARTER_TILES + t)
        own[t * STATE : (t + 1) * STATE, :] = state
        own_decay[t : t + 1, :] = decay


def join_pair(bit, carried, last, *refs):
    state, decay, recv = refs[:3]
    refs = refs[3:]
    if carried:
        before, before_decay = refs[:2]
        refs = refs[2:]
    send, new_state, new_decay = refs[:3]
    refs = refs[3:]
    if bit >= 2:
        new_before, new_before_decay = refs[:2]
        refs = refs[2:]
    (other,) = refs
    upper = ((lax.axis_index("seq") >> bit) & 1) == 1
    received_decays(recv, QUARTER_TILES, other)
    decays = []
    for t in range(QUARTER_TILES):
        rows = slice(t * STATE, (t + 1) * STATE)
        mine, theirs = state[rows, :], recv[rows, :].astype(F32)
        d_mine, d_theirs = decay[t : t + 1, :], other[t : t + 1, :]
        early, late = jnp.where(upper, theirs, mine), jnp.where(upper, mine, theirs)
        total = jnp.where(upper, d_mine, d_theirs) * early + late
        new_state[rows, :] = total
        send[rows, :] = total.astype(BF16)
        new_decay[t : t + 1, :] = d_mine * d_theirs
        decays.append(d_mine * d_theirs)
        if bit >= 2:
            if carried:
                b, bd = before[rows, :], before_decay[t : t + 1, :]
                new_before[rows, :] = jnp.where(upper, b + bd * theirs, b)
                new_before_decay[t : t + 1, :] = jnp.where(upper, bd * d_theirs, bd)
            else:
                new_before[rows, :] = jnp.where(upper, theirs, 0.0)
                new_before_decay[t : t + 1, :] = jnp.where(upper, d_theirs, 1.0)
    put_decays(send, QUARTER_TILES, decays)


def to_planes(bit, carried, *refs):
    recv = refs[0]
    refs = refs[1:]
    if carried:
        before, before_decay = refs[:2]
        refs = refs[2:]
    own, own_decay, recv_pair, send, start, other = refs
    me = lax.axis_index("seq")
    upper = ((me >> bit) & 1) == 1
    y = ((me >> 1) & 1) == 1
    received_decays(recv_pair, QUARTER_TILES, other)
    for t in range(QUARTER_TILES):
        rows = slice(t * STATE, (t + 1) * STATE)
        theirs = recv[rows, :].astype(F32)
        if carried:
            b = before[rows, :]
            plane = jnp.where(upper, b + before_decay[t : t + 1, :] * theirs, b)
        else:
            plane = jnp.where(upper, theirs, 0.0)
        d = jnp.where(y, other[t : t + 1, :], own_decay[t : t + 1, :])
        grown = jnp.where(y, recv_pair[rows, :].astype(F32), own[rows, :])
        later = d * plane + grown
        send[rows, :] = jnp.where(y, plane, later).astype(BF16)
        start[rows, :] = jnp.where(y, later, plane)


def to_cores(start, recv_start, keep, keep_decay, recv, send, own, other):
    me = lax.axis_index("seq")
    first = (me & 1) == 0
    y = (me >> 1) & 1
    received_decays(recv, HALF_TILES, other)
    for side in range(2):
        for t in range(QUARTER_TILES):
            rows = slice(t * STATE, (t + 1) * STATE)
            at = (y if side == 0 else 1 - y) * QUARTER_TILES + t
            chip = start[rows, :] if side == 0 else recv_start[rows, :].astype(F32)
            d = jnp.where(first, keep_decay[pl.ds(at, 1), :], other[pl.ds(at, 1), :])
            grown = jnp.where(first, keep[tile_rows(at), :], recv[tile_rows(at), :].astype(F32))
            later = d * chip + grown
            send[tile_rows(at), :] = jnp.where(first, later, chip).astype(BF16)
            own[tile_rows(at), :] = jnp.where(first, chip, later).astype(BF16)


def inside(conv, fix, both, both_t, carry_pair, gate, skip, base, slope):
    row = lax.broadcasted_iota(jnp.int32, (SPAN, SPAN), 0)
    lane = lax.broadcasted_iota(jnp.int32, (SPAN, SPAN), 1)
    causal = row >= lane
    for group in range(GROUPS):
        cols = slice(group * GROUP_COLS, (group + 1) * GROUP_COLS)
        values = load_fixed(conv, fix, cols)
        writes = load_fixed(conv, fix, slice(INNER + group * STATE, INNER + (group + 1) * STATE))
        reads = load_fixed(
            conv, fix, slice(INNER + KEYS + group * STATE, INNER + KEYS + (group + 1) * STATE)
        )
        scores = dot(reads, writes, ((1,), (1,)))
        found = []
        for h in range(group * PER_GROUP, (group + 1) * PER_GROUP):
            gap = both[:, h : h + 1] - both_t[h : h + 1, :]
            weights = scores * jnp.exp(jnp.where(causal, gap, -jnp.inf)) * both_t[HEADS + h : HEADS + h + 1, :]
            at = (h - group * PER_GROUP) * HEAD_DIM
            found.append(dot(weights.astype(BF16), values[:, at : at + HEAD_DIM]))
        within = jnp.concatenate(found, axis=1)
        opened = silu(gate[:, cols].astype(F32))
        base[:, cols] = (within + skip[:, cols] * values.astype(F32)) * opened
        slope[:, cols] = dot(carry_pair[...], spread(group)) * opened


def finish(part, *refs):
    conv, fix, own, recv, base, slope, gain = refs[:7]
    out = refs[-1]
    core = lax.axis_index("seq") & 1
    for source, side in ((own, core), (recv, 1 - core)):
        for j in range(HALF_GROUPS):
            group = part * PART_GROUPS + side * HALF_GROUPS + j
            cols = columns(group, GROUP_COLS)
            reads = load_fixed(conv, fix, columns(group, STATE, INNER + KEYS))
            starts = jnp.concatenate(
                [source[(j * TILES + t) * STATE : (j * TILES + t + 1) * STATE, :] for t in range(TILES)], axis=1
            )
            gated = base[:, cols] + slope[:, cols] * dot(reads, starts)
            mean = jnp.mean(gated * gated, axis=1, keepdims=True)
            local = columns(side * HALF_GROUPS + j, GROUP_COLS)
            out[:, local] = (gated * lax.rsqrt(mean + 1e-5) * gain[:, cols]).astype(BF16)


def shards(mixer_input, gate_input, step_raw, conv_weight, conv_bias, step_bias, decay_log, skip_gain, norm_gain):
    devices = lax.axis_size("seq")
    bits = devices.bit_length() - 1

    def across(value, bit):
        return lax.ppermute(value, "seq", [(i, i ^ (1 << bit)) for i in range(devices)])

    halo = lax.ppermute(mixer_input[SPAN - 3 :], "seq", [(i, i + 1) for i in range(devices - 1)])
    step = jax.nn.softplus(step_raw.astype(F32) + step_bias[None, :])
    bias = conv_bias[None, :]
    skip = jnp.broadcast_to(skip_gain[:, None], (HEADS, HEAD_DIM)).reshape(1, INNER)
    conv, both, both_t, tail_pair, carry_pair, total_pair = call(
        prepare,
        [
            ((SPAN, CONV_COLS), BF16),
            ((SPAN, 2 * HEADS), F32),
            ((2 * HEADS, SPAN), F32),
            ((SPAN, 2 * HEADS), BF16),
            ((SPAN, 2 * HEADS), BF16),
            ((16, 2 * HEADS), BF16),
        ],
        mixer_input, step, decay_log[None, :], conv_weight, bias,
        scratch=[pltpu.VMEM((8 + SPAN, 512), F32)],
    )
    half_send = ((HALF_ROWS + extra_rows(HALF_TILES), LANES), BF16)
    quarter_send = ((QUARTER_ROWS + extra_rows(QUARTER_TILES), LANES), BF16)
    quarter = ((QUARTER_ROWS, LANES), F32)
    quarter_decay = ((decay_rows(QUARTER_TILES), LANES), F32)
    half_keep = [half_send, ((HALF_ROWS, LANES), F32), ((decay_rows(HALF_TILES), LANES), F32)]
    half_scratch = [pltpu.VMEM((decay_rows(HALF_TILES), LANES), F32)]
    quarter_scratch = [pltpu.VMEM((decay_rows(QUARTER_TILES), LANES), F32)]
    grown = []
    fix = None
    for part in range(PARTS):
        if part == 0:
            send, keep, keep_decay, fix = call(
                functools.partial(increments, part), half_keep + [((16, CONV_COLS), BF16)],
                mixer_input, halo, conv_weight, bias, conv, tail_pair, total_pair,
                scratch=[pltpu.VMEM((24, 512), F32)],
            )
        else:
            send, keep, keep_decay = call(
                functools.partial(increments, part), half_keep, conv, fix, tail_pair, total_pair
            )
        grown.append((send, keep, keep_decay))
    starts = []
    for send, keep, keep_decay in grown:
        recv = across(send, 0)
        send_pair, own, own_decay = call(
            join_cores, [quarter_send, quarter, quarter_decay], keep, keep_decay, recv, scratch=half_scratch
        )
        recv_pair = across(send_pair, 1)
        send_plane, state, decay = call(
            functools.partial(join_pair, 1, False, False), [quarter_send, quarter, quarter_decay],
            own, own_decay, recv_pair, scratch=quarter_scratch,
        )
        carried = ()
        for bit in range(2, bits - 1):
            outs = call(
                functools.partial(join_pair, bit, bool(carried), False),
                [quarter_send, quarter, quarter_decay, quarter, quarter_decay],
                state, decay, across(send_plane, bit), *carried, scratch=quarter_scratch,
            )
            send_plane, state, decay = outs[:3]
            carried = tuple(outs[3:])
        send_start, start = call(
            functools.partial(to_planes, bits - 1, bool(carried)), [((QUARTER_ROWS, LANES), BF16), quarter],
            across(send_plane, bits - 1), *carried, own, own_decay, recv_pair, scratch=quarter_scratch,
        )
        send_core, own_start = call(
            to_cores, [((HALF_ROWS, LANES), BF16)] * 2,
            start, across(send_start, 1), keep, keep_decay, recv, scratch=half_scratch,
        )
        starts.append((own_start, across(send_core, 0)))
    base, slope = call(
        inside, [((SPAN, INNER), F32)] * 2,
        conv, fix, both, both_t, carry_pair, gate_input, skip,
        cost=(2 * 64 * 128 * 128 * 64, 64 * 128 * 128),
    )
    gain = norm_gain[None, :]
    finished = [
        call(
            functools.partial(finish, part), [((SPAN, INNER // PARTS), BF16)],
            conv, fix, own_start, recv_start, base, slope, gain,
        )[0]
        for part, (own_start, recv_start) in enumerate(starts)
    ]
    return jnp.concatenate(finished, axis=1)


def solution(mesh):
    in_specs = (
        P(("groups", "seq"), None),
        P(("groups", "seq"), None),
        P(("groups", "seq"), None),
        P(),
        P(),
        P("groups"),
        P("groups"),
        P(),
        P(),
    )
    return jax.shard_map(
        shards, mesh=mesh, in_specs=in_specs, out_specs=P(("groups", "seq"), None), check_vma=False
    )
```

time: 218 us -> 63.4 us (0.29); the launches traced: 214 us -> 62.8 us
  local copies, waits for them, and re-layouts: 71.4 us -> 7.67 us
  blocking collectives: 54.1 us -> 0 us
  other arithmetic: 24.5 us -> 1.77 us
  Pallas kernels: 0 us -> 17.4 us
  waiting for transfers between devices: 31.7 us -> 17.4 us
  matrix products: 7.12 us -> 0 us
  starting transfers between devices: 24.6 us -> 18.3 us
    all_to_all x1 -> x0, blocking collectives: 54.1 us -> none  [shards(): lax.all_to_all(outputs, 'seq', split_axis=0, concat_axis=1, tiled=True)]
    all_to_all x3 -> x0, waiting for transfers between devices: 31.7 us -> none  [the longest x1 17.6 us: shards(): lax.all_to_all(paired, 'seq', split_axis=1, concat_axis=0, tiled=True)]
    pad x4 -> x0, local copies, waits for them, and re-layouts: 26.8 us -> none  [shards(): _, running = lax.associative_scan(combine, (totals, increment), axis=0)]
    all_to_all x3 -> x0, starting transfers between devices: 22.3 us -> none  [the longest x1 8.03 us: shards(): lax.all_to_all(paired, 'seq', split_axis=1, concat_axis=0, tiled=True)]
    ppermute x1 -> x13, waiting for transfers between devices: 0.01 us -> 17.4 us  [the longest x12 17.4 us: across(): lax.ppermute(value, 'seq', [(i, i ^ 1 << bit) for i in range(devices)])]
    pallas_call x0 -> x16, Pallas kernels: none -> 17.4 us  [call(): pl.pallas_call(body, out_shape=[jax.ShapeDtypeStruct(shape, kind) for sha...]
    ppermute x1 -> x13, starting transfers between devices: 2.31 us -> 18.3 us  [the longest x12 16 us: across(): lax.ppermute(value, 'seq', [(i, i ^ 1 << bit) for i in range(devices)])]
    unnamed x42 -> x17, local copies, waits for them, and re-layouts: 19.5 us -> 5.22 us
  transfers between devices with their start and end apart: 4 -> 13, of which waited for: 2 -> 8; matrix products, arithmetic and copies ran while one was open for 10% -> 5% of each run, Pallas kernels for 0% -> 21%
where the time goes in v1:
time: 63.4 us; the launch traced here: 62.8 us
  starting transfers between devices  18.3 us (29%)
  Pallas kernels  17.4 us (27%)
  waiting for transfers between devices  17.4 us (27%)
  local copies, waits for them, and re-layouts  7.67 us (12%)
  other arithmetic  1.77 us (3%)
    ppermute x12, waiting for transfers between devices, across(): lax.ppermute(value, 'seq', [(i, i ^ 1 << bit) for i in range(devices)])  17.4 us
    pallas_call x16, Pallas kernels, call(): pl.pallas_call(body, out_shape=[jax.ShapeDtypeStruct(shape, kind) for sha...  17.4 us
    ppermute x12, starting transfers between devices, across(): lax.ppermute(value, 'seq', [(i, i ^ 1 << bit) for i in range(devices)])  16 us
    unnamed x17, local copies, waits for them, and re-layouts  5.22 us
    ppermute x1, starting transfers between devices, shards(): lax.ppermute(mixer_input[SPAN - 3:], 'seq', [(i, i + 1) for i in range(de...  2.36 us
  transfers between devices with their start and end apart: 13, of which 8 were waited for; matrix products, arithmetic and copies ran while one was open for 5% of the time, Pallas kernels for 21%

profile of v1, /device:TPU:0, one launch (start us, length us, event | category | flops | bytes accessed | tf_op | source)
XLA Modules:
  0.0 62.8 jit_solution(4295520107163592612)
XLA Ops:
  0.0 0.9 %slice.3 = bf16[3,6144]{1,0:T(4,128)(2,1)S(1)} slice(bf16[128,6144]{1,0:T(8,128)(2,1)} %refs_0_.1), slice={[125:128], [0:6144]} | slice | bytes 73728 | tf_op jit(solution)/shard_map/slice | solution.py:333
  0.9 2.4 %collective-permute-start = (bf16[3,6144]{1,0:T(4,128)(2,1)S(1)}, bf16[3,6144]{1,0:T(4,128)(2,1)S(1)}, u32[]{:S(2)}, u32[]{:S(2)}) collective-permute-start(bf16[3,6144]{1,0:T(4,128)(2,1)S(1)} %slice.3), channel_id=1, source_target_pairs={{0,1},{1,2},{2,3},{3,4},{4,5},{5,6},{6,7},{7,8},{8,9},{9,10},{10,1... | collective-permute-start | bytes 110600 | tf_op jit(solution)/shard_map/ppermute | solution.py:333
  3.3 0.8 %copy.10 = bf16[128,64]{1,0:T(8,128)(2,1)S(1)} copy(bf16[128,64]{0,1:T(8,128)(2,1)} %param.11) | data formatting | bytes 32768 | tf_op args[2]
  4.1 0.7 %compare_select_fusion.step = f32[128,64]{1,0:T(8,128)S(1)} fusion(bf16[128,64]{1,0:T(8,128)(2,1)S(1)} %copy.10, f32[64]{0:T(128)} %param.14), kind=kLoop, calls=%fused_computation.1 | loop fusion | flops 65536 | bytes 49408 | tf_op jit(solution)/shard_map/jit(softplus)/select_n | solution.py:334
  4.8 0.0 copy-start
  4.8 1.4 %copy-done = bf16[128,6144]{1,0:T(8,128)(2,1)S(1)} copy-done((bf16[128,6144]{1,0:T(8,128)(2,1)S(1)}, bf16[128,6144]{1,0:T(8,128)(2,1)}, u32[]{:S(2)}) %copy-start) | copy-done | bytes 1572888
  6.2 0.0 copy-start.2
  6.2 0.8 %copy-done.2 = bf16[4,6144]{1,0:T(4,128)(2,1)S(1)} copy-done((bf16[4,6144]{1,0:T(4,128)(2,1)S(1)}, bf16[4,6144]{1,0:T(4,128)(2,1)}, u32[]{:S(2)}) %copy-start.2) | copy-done | bytes 49176
  7.0 0.0 copy-start.4
  7.0 0.7 %copy-done.4 = f32[6144]{0:T(1024)S(1)} copy-done((f32[6144]{0:T(1024)S(1)}, f32[6144]{0:T(1024)}, u32[]{:S(2)}) %copy-start.4) | copy-done | bytes 24600
  7.8 0.0 copy-start.6
  7.8 0.7 %copy-done.6 = f32[64]{0:T(128)S(1)} copy-done((f32[64]{0:T(128)S(1)}, f32[64]{0:T(128)}, u32[]{:S(2)}) %copy-start.6) | copy-done | bytes 280
  8.4 4.2 %shard_map.91 = (bf16[128,6144]{1,0:T(8,128)(2,1)S(1)}, f32[128,128]{1,0:T(8,128)S(1)}, f32[128,128]{1,0:T(8,128)S(1)}, bf16[128,128]{1,0:T(8,128)(2,1)S(1)}, bf...) custom-call(bf16[128,6144]{1,0:T(8,128)(2,1)S(1)} %copy-done, f32[128,64]{1,0:T(8,128)S(1)} %compare_select_fusion.step, ...), custom_call_target="tpu_custom_call" | custom-call | flops 100000 | bytes 3453184 | tf_op jit(solution)/shard_map/pallas_call | solution.py:49
  12.7 0.0 collective-permute-done.refs_1_
  12.7 0.0 copy-start.3
  12.7 0.8 %copy-done.3 = bf16[4,6144]{1,0:T(4,128)(2,1)S(1)} copy-done((bf16[4,6144]{1,0:T(4,128)(2,1)S(1)}, bf16[4,6144]{1,0:T(4,128)(2,1)}, u32[]{:S(2)}) %copy-start.3) | copy-done | bytes 49176
  13.5 1.9 %shard_map.92 = (bf16[1040,128]{1,0:T(8,128)(2,1)S(1)}, f32[1024,128]{1,0:T(8,128)S(1)}, f32[8,128]{1,0:T(8,128)S(1)}, bf16[16,6144]{1,0:T(8,128)(2,1)S(1)}) custom-call(bf16[128,6144]{1,0:T(8,128)(2,1)S(1)} %copy-done, bf16[3,6144]{1,0:T(4,128)(2,1)S(1)} %collective-permute-done.refs_1_, bf16[4,6144]{1,0:T(4,128)(2,1)S(1)} %copy-done.3, ...), custom_call_target="tpu_custom_call" | custom-call | flops 100000 | bytes 4284416 | tf_op jit(solution)/shard_map/pallas_call | solution.py:49
  15.4 1.2 %shard_map.100 = (bf16[1040,128]{1,0:T(8,128)(2,1)S(1)}, f32[1024,128]{1,0:T(8,128)S(1)}, f32[8,128]{1,0:T(8,128)S(1)}) custom-call(bf16[128,6144]{1,0:T(8,128)(2,1)S(1)} %get-tuple-element.46.refs_4_.conv.refs_0_, bf16[16,6144]{1,0:T(8,128)(2,1)S(1)} %get-tuple-element.49.fix.refs_1_, bf16[128,128]{1,0:T(8,128)(2,1)S(1)} %get-tuple-element.47.refs_5_.refs_2_, ...), custom_call_target="tpu_custom_call" | custom-call | flops 100000 | bytes 2600960 | tf_op jit(solution)/shard_map/pallas_call | solution.py:49
  16.6 2.7 %collective-permute-start.7 = (bf16[1040,128]{1,0:T(8,128)(2,1)S(1)}, bf16[1040,128]{1,0:T(8,128)(2,1)S(1)}, u32[]{:S(2)}, u32[]{:S(2)}) collective-permute-start(bf16[1040,128]{1,0:T(8,128)(2,1)S(1)} %get-tuple-element.73), channel_id=1, source_target_pairs={{0,1},{1,0},{2,3},{3,2},{4,5},{5,4},{6,7},{7,6},{8,9},{9,8},{10,11... | collective-permute-start | bytes 798728 | tf_op jit(solution)/shard_map/ppermute | solution.py:331
  19.3 0.1 collective-permute-start.1
  19.4 1.1 %collective-permute-done.7.recv = bf16[1040,128]{1,0:T(8,128)(2,1)S(1)} collective-permute-done((bf16[1040,128]{1,0:T(8,128)(2,1)S(1)}, bf16[1040,128]{1,0:T(8,128)(2,1)S(1)}, u32[]{:S(2)}, u32[]{:S(2)}) %collective-permute-start.7) | collective-permute-done | bytes 266272 | tf_op jit(solution)/shard_map/ppermute | solution.py:331
  20.5 0.1 shard_map.101
  20.6 1.6 %collective-permute-start.8 = (bf16[528,128]{1,0:T(8,128)(2,1)S(1)}, bf16[528,128]{1,0:T(8,128)(2,1)S(1)}, u32[]{:S(2)}, u32[]{:S(2)}) collective-permute-start(bf16[528,128]{1,0:T(8,128)(2,1)S(1)} %get-tuple-element.76), channel_id=1, source_target_pairs={{0,2},{1,3},{2,0},{3,1},{4,6},{5,7},{6,4},{7,5},{8,10},{9,11},{10,... | collective-permute-start | bytes 405512 | tf_op jit(solution)/shard_map/ppermute | solution.py:331
  22.2 0.0 collective-permute-done.1.recv
  22.2 0.1 shard_map.93
  22.3 0.6 collective-permute-start.2
  22.9 4.2 %collective-permute-done.8.refs_2_.refs_5_ = bf16[528,128]{1,0:T(8,128)(2,1)S(1)} collective-permute-done((bf16[528,128]{1,0:T(8,128)(2,1)S(1)}, bf16[528,128]{1,0:T(8,128)(2,1)S(1)}, u32[]{:S(2)}, u32[]{:S(2)}) %collective-permute-start.8) | collective-permute-done | bytes 135200 | tf_op jit(solution)/shard_map/ppermute | solution.py:331
  27.1 0.1 shard_map.102
  27.2 1.6 %collective-permute-start.9 = (bf16[528,128]{1,0:T(8,128)(2,1)S(1)}, bf16[528,128]{1,0:T(8,128)(2,1)S(1)}, u32[]{:S(2)}, u32[]{:S(2)}) collective-permute-start(bf16[528,128]{1,0:T(8,128)(2,1)S(1)} %get-tuple-element.79), channel_id=1, source_target_pairs={{0,4},{1,5},{2,6},{3,7},{4,0},{5,1},{6,2},{7,3},{8,12},{9,13},{10,... | collective-permute-start | bytes 405512 | tf_op jit(solution)/shard_map/ppermute | solution.py:331
  28.8 0.6 collective-permute-done.2.refs_2_.refs_5_
  29.4 0.1 shard_map.94
  29.5 1.6 %collective-permute-start.3 = (bf16[528,128]{1,0:T(8,128)(2,1)S(1)}, bf16[528,128]{1,0:T(8,128)(2,1)S(1)}, u32[]{:S(2)}, u32[]{:S(2)}) collective-permute-start(bf16[528,128]{1,0:T(8,128)(2,1)S(1)} %get-tuple-element.58), channel_id=1, source_target_pairs={{0,4},{1,5},{2,6},{3,7},{4,0},{5,1},{6,2},{7,3},{8,12},{9,13},{10,... | collective-permute-start | bytes 405512 | tf_op jit(solution)/shard_map/ppermute | solution.py:331
  31.2 1.6 %collective-permute-done.9.refs_2_ = bf16[528,128]{1,0:T(8,128)(2,1)S(1)} collective-permute-done((bf16[528,128]{1,0:T(8,128)(2,1)S(1)}, bf16[528,128]{1,0:T(8,128)(2,1)S(1)}, u32[]{:S(2)}, u32[]{:S(2)}) %collective-permute-start.9) | collective-permute-done | bytes 135200 | tf_op jit(solution)/shard_map/ppermute | solution.py:331
  32.8 0.8 %shard_map.103 = (bf16[528,128]{1,0:T(8,128)(2,1)S(1)}, f32[512,128]{1,0:T(8,128)}, f32[8,128]{1,0:T(8,128)}, f32[512,128]{1,0:T(8,128)S(1)}, f32[8,128]{1,0:T(8,128)S(1)}) custom-call(f32[512,128]{1,0:T(8,128)S(1)} %get-tuple-element.77.refs_0_, f32[8,128]{1,0:T(8,128)S(1)} %get-tuple-element.78.refs_1_, bf16[528,128]{1,0:T(8,128)(2,1)S(1)} %collective-permute-done.9.refs_2_), custom_call_target="tpu_custom_call" | custom-call | flops 100000 | bytes 1069056 | tf_op jit(solution)/shard_map/pallas_call | solution.py:49
  33.5 2.6 %collective-permute-start.10 = (bf16[528,128]{1,0:T(8,128)(2,1)S(1)}, bf16[528,128]{1,0:T(8,128)(2,1)S(1)}, u32[]{:S(2)}, u32[]{:S(2)}) collective-permute-start(bf16[528,128]{1,0:T(8,128)(2,1)S(1)} %get-tuple-element.80), channel_id=1, source_target_pairs={{0,8},{1,9},{2,10},{3,11},{4,12},{5,13},{6,14},{7,15},{8,0},{9,1},... | collective-permute-start | bytes 405512 | tf_op jit(solution)/shard_map/ppermute | solution.py:331
  36.1 0.5 collective-permute-done.3.refs_2_
  36.6 0.8 %shard_map.95 = (bf16[528,128]{1,0:T(8,128)(2,1)S(1)}, f32[512,128]{1,0:T(8,128)}, f32[8,128]{1,0:T(8,128)}, f32[512,128]{1,0:T(8,128)S(1)}, f32[8,128]{1,0:T(8,128)S(1)}) custom-call(f32[512,128]{1,0:T(8,128)S(1)} %get-tuple-element.56.refs_0_, f32[8,128]{1,0:T(8,128)S(1)} %get-tuple-element.57.refs_1_, bf16[528,128]{1,0:T(8,128)(2,1)S(1)} %collective-permute-done.3.refs_2_), custom_call_target="tpu_custom_call" | custom-call | flops 100000 | bytes 1069056 | tf_op jit(solution)/shard_map/pallas_call | solution.py:49
  37.4 0.0 copy-start.7
  37.4 0.0 copy-start.1
  37.4 2.1 %collective-permute-start.4 = (bf16[528,128]{1,0:T(8,128)(2,1)S(1)}, bf16[528,128]{1,0:T(8,128)(2,1)S(1)}, u32[]{:S(2)}, u32[]{:S(2)}) collective-permute-start(bf16[528,128]{1,0:T(8,128)(2,1)S(1)} %get-tuple-element.59), channel_id=1, source_target_pairs={{0,8},{1,9},{2,10},{3,11},{4,12},{5,13},{6,14},{7,15},{8,0},{9,1},... | collective-permute-start | bytes 405512 | tf_op jit(solution)/shard_map/ppermute | solution.py:331
  39.5 6.2 %collective-permute-done.10.refs_0_ = bf16[528,128]{1,0:T(8,128)(2,1)S(1)} collective-permute-done((bf16[528,128]{1,0:T(8,128)(2,1)S(1)}, bf16[528,128]{1,0:T(8,128)(2,1)S(1)}, u32[]{:S(2)}, u32[]{:S(2)}) %collective-permute-start.10) | collective-permute-done | bytes 135200 | tf_op jit(solution)/shard_map/ppermute | solution.py:331
  45.7 0.1 shard_map.104
  45.8 1.6 %collective-permute-start.11 = (bf16[512,128]{1,0:T(8,128)(2,1)S(1)}, bf16[512,128]{1,0:T(8,128)(2,1)S(1)}, u32[]{:S(2)}, u32[]{:S(2)}) collective-permute-start(bf16[512,128]{1,0:T(8,128)(2,1)S(1)} %get-tuple-element.84), channel_id=1, source_target_pairs={{0,2},{1,3},{2,0},{3,1},{4,6},{5,7},{6,4},{7,5},{8,10},{9,11},{10,... | collective-permute-start | bytes 393224 | tf_op jit(solution)/shard_map/ppermute | solution.py:331
  47.3 0.0 collective-permute-done.4.refs_0_
  47.3 0.1 shard_map.96
  47.5 1.5 %collective-permute-start.5 = (bf16[512,128]{1,0:T(8,128)(2,1)S(1)}, bf16[512,128]{1,0:T(8,128)(2,1)S(1)}, u32[]{:S(2)}, u32[]{:S(2)}) collective-permute-start(bf16[512,128]{1,0:T(8,128)(2,1)S(1)} %get-tuple-element.63), channel_id=1, source_target_pairs={{0,2},{1,3},{2,0},{3,1},{4,6},{5,7},{6,4},{7,5},{8,10},{9,11},{10,... | collective-permute-start | bytes 393224 | tf_op jit(solution)/shard_map/ppermute | solution.py:331
  48.9 2.7 %collective-permute-done.11.recv_start = bf16[512,128]{1,0:T(8,128)(2,1)S(1)} collective-permute-done((bf16[512,128]{1,0:T(8,128)(2,1)S(1)}, bf16[512,128]{1,0:T(8,128)(2,1)S(1)}, u32[]{:S(2)}, u32[]{:S(2)}) %collective-permute-start.11) | collective-permute-done | bytes 131104 | tf_op jit(solution)/shard_map/ppermute | solution.py:331
  51.7 0.9 %shard_map.105 = (bf16[1024,128]{1,0:T(8,128)(2,1)}, bf16[1024,128]{1,0:T(8,128)(2,1)S(1)}) custom-call(f32[512,128]{1,0:T(8,128)S(1)} %get-tuple-element.83.start, bf16[512,128]{1,0:T(8,128)(2,1)S(1)} %collective-permute-done.11.recv_start, f32[1024,128]{1,0:T(8,128)S(1)} %get-tuple-element.71.keep, f32[8,128]{1,0:T(8,128)S(1)} %get-tuple-element.72.keep_decay, ...), custom_call_target="tpu_custom_call" | custom-call | flops 100000 | bytes 1712128 | tf_op jit(solution)/shard_map/pallas_call | solution.py:49
  52.5 0.0 collective-permute-start.12
  52.5 0.5 collective-permute-done.5.recv_start
  53.1 0.0 copy-start.5
  53.1 0.9 %shard_map.97 = (bf16[1024,128]{1,0:T(8,128)(2,1)}, bf16[1024,128]{1,0:T(8,128)(2,1)S(1)}) custom-call(f32[512,128]{1,0:T(8,128)S(1)} %get-tuple-element.62.start, bf16[512,128]{1,0:T(8,128)(2,1)S(1)} %collective-permute-done.5.recv_start, f32[1024,128]{1,0:T(8,128)S(1)} %get-tuple-element.50.keep, f32[8,128]{1,0:T(8,128)S(1)} %get-tuple-element.51.keep_decay, ...), custom_call_target="tpu_custom_call" | custom-call | flops 100000 | bytes 1712128 | tf_op jit(solution)/shard_map/pallas_call | solution.py:49
  53.9 0.0 collective-permute-start.6
  53.9 0.0 copy-done.7
  53.9 0.7 %broadcast_in_dim.18 = f32[64,64]{1,0:T(8,128)} broadcast(f32[64]{0:T(128)S(1)} %copy-done.7), dimensions={0} | broadcast | bytes 16640 | tf_op jit(solution)/shard_map/broadcast_in_dim | solution.py:336
  54.6 0.8 %reshape.5.skip = f32[1,4096]{1,0:T(1,128)S(1)} reshape(f32[64,64]{1,0:T(8,128)} %broadcast_in_dim.18) | data formatting | bytes 32768 | tf_op jit(solution)/shard_map/reshape | solution.py:336
  55.5 0.0 copy-done.1
  55.5 3.4 %shard_map.98 = (f32[128,4096]{1,0:T(8,128)S(1)}, f32[128,4096]{1,0:T(8,128)S(1)}) custom-call(bf16[128,6144]{1,0:T(8,128)(2,1)S(1)} %get-tuple-element.46.refs_4_.conv.refs_0_, bf16[16,6144]{1,0:T(8,128)(2,1)S(1)} %get-tuple-element.49.fix.refs_1_, f32[128,128]{1,0:T(8,128)S(1)} %get-tuple-element.66.both, f32[128,128]{1,0:T(8,128)S(1)} %get-tuple-element.67.both_t, ...), custom_call_target="tpu_custom_call" | custom-call | flops 134217728 | bytes 7192576 | tf_op jit(solution)/shard_map/pallas_call | solution.py:49
  58.9 0.0 collective-permute-done.12.refs_3_
  58.9 0.0 copy-done.5
  58.9 1.4 %shard_map.106 = bf16[128,2048]{1,0:T(8,128)(2,1)S(1)} custom-call(bf16[128,6144]{1,0:T(8,128)(2,1)S(1)} %get-tuple-element.46.refs_4_.conv.refs_0_, bf16[16,6144]{1,0:T(8,128)(2,1)S(1)} %get-tuple-element.49.fix.refs_1_, bf16[1024,128]{1,0:T(8,128)(2,1)S(1)} %get-tuple-element.85.refs_2_, bf16[1024,128]{1,0:T(8,128)(2,1)} %collective-permute-done.12.refs_3_, ...), custom_call_target="tpu_custom_call" | custom-call | flops 100000 | bytes 7028736 | tf_op jit(solution)/shard_map/pallas_call | solution.py:49
  60.3 0.0 collective-permute-done.6.refs_3_
  60.3 1.4 %shard_map.99 = bf16[128,2048]{1,0:T(8,128)(2,1)S(1)} custom-call(bf16[128,6144]{1,0:T(8,128)(2,1)S(1)} %get-tuple-element.46.refs_4_.conv.refs_0_, bf16[16,6144]{1,0:T(8,128)(2,1)S(1)} %get-tuple-element.49.fix.refs_1_, bf16[1024,128]{1,0:T(8,128)(2,1)S(1)} %get-tuple-element.64.refs_2_, bf16[1024,128]{1,0:T(8,128)(2,1)} %collective-permute-done.6.refs_3_, ...), custom_call_target="tpu_custom_call" | custom-call | flops 100000 | bytes 7028736 | tf_op jit(solution)/shard_map/pallas_call | solution.py:49
  61.7 1.1 %pad_maximum_fusion = bf16[128,4096]{1,0:T(8,128)(2,1)} fusion(bf16[128,2048]{1,0:T(8,128)(2,1)S(1)} %shard_map.106, bf16[128,2048]{1,0:T(8,128)(2,1)S(1)} %shard_map.99), kind=kLoop, calls=%fused_computation | loop fusion | flops 2097152 | bytes 2097152 | tf_op jit(solution)/shard_map/concatenate | solution.py:413
Async XLA Ops:
  0.9 11.8 %collective-permute-start = (bf16[3,6144]{1,0:T(4,128)(2,1)S(1)}, bf16[3,6144]{1,0:T(4,128)(2,1)S(1)}, u32[]{:S(2)}, u32[]{:S(2)}) collective-permute-start(bf16[3,6144]{1,0:T(4,128)(2,1)S(1)} %slice.3), channel_id=1, source_target_pairs={{0,1},{1,2},{2,3},{3,4},{4,5},{5,6},{6,7},{7,8},{8,9},{9,10},{10,1... | collective-permute-start | bytes 110600 | tf_op jit(solution)/shard_map/ppermute | solution.py:333
  4.8 1.4 %copy-start = (bf16[128,6144]{1,0:T(8,128)(2,1)S(1)}, bf16[128,6144]{1,0:T(8,128)(2,1)}, u32[]{:S(2)}) copy-start(bf16[128,6144]{1,0:T(8,128)(2,1)} %refs_0_.1) | copy-start | bytes 4718596
  6.2 0.8 %copy-start.2 = (bf16[4,6144]{1,0:T(4,128)(2,1)S(1)}, bf16[4,6144]{1,0:T(4,128)(2,1)}, u32[]{:S(2)}) copy-start(bf16[4,6144]{1,0:T(4,128)(2,1)} %refs_2_.1) | copy-start | bytes 147460
  7.0 0.7 %copy-start.4 = (f32[6144]{0:T(1024)S(1)}, f32[6144]{0:T(1024)}, u32[]{:S(2)}) copy-start(f32[6144]{0:T(1024)} %param.13) | copy-start | bytes 73732
  7.8 0.7 %copy-start.6 = (f32[64]{0:T(128)S(1)}, f32[64]{0:T(128)}, u32[]{:S(2)}) copy-start(f32[64]{0:T(128)} %param.15) | copy-start | bytes 772
  12.7 0.8 %copy-start.3 = (bf16[4,6144]{1,0:T(4,128)(2,1)S(1)}, bf16[4,6144]{1,0:T(4,128)(2,1)}, u32[]{:S(2)}) copy-start(bf16[4,6144]{1,0:T(4,128)(2,1)} %refs_2_.1) | copy-start | bytes 147460
  16.6 3.9 %collective-permute-start.7 = (bf16[1040,128]{1,0:T(8,128)(2,1)S(1)}, bf16[1040,128]{1,0:T(8,128)(2,1)S(1)}, u32[]{:S(2)}, u32[]{:S(2)}) collective-permute-start(bf16[1040,128]{1,0:T(8,128)(2,1)S(1)} %get-tuple-element.73), channel_id=1, source_target_pairs={{0,1},{1,0},{2,3},{3,2},{4,5},{5,4},{6,7},{7,6},{8,9},{9,8},{10,11... | collective-permute-start | bytes 798728 | tf_op jit(solution)/shard_map/ppermute | solution.py:331
  19.3 2.9 %collective-permute-start.1 = (bf16[1040,128]{1,0:T(8,128)(2,1)S(1)}, bf16[1040,128]{1,0:T(8,128)(2,1)S(1)}, u32[]{:S(2)}, u32[]{:S(2)}) collective-permute-start(bf16[1040,128]{1,0:T(8,128)(2,1)S(1)} %get-tuple-element.52), channel_id=1, source_target_pairs={{0,1},{1,0},{2,3},{3,2},{4,5},{5,4},{6,7},{7,6},{8,9},{9,8},{10,11... | collective-permute-start | bytes 798728 | tf_op jit(solution)/shard_map/ppermute | solution.py:331
  20.6 6.5 %collective-permute-start.8 = (bf16[528,128]{1,0:T(8,128)(2,1)S(1)}, bf16[528,128]{1,0:T(8,128)(2,1)S(1)}, u32[]{:S(2)}, u32[]{:S(2)}) collective-permute-start(bf16[528,128]{1,0:T(8,128)(2,1)S(1)} %get-tuple-element.76), channel_id=1, source_target_pairs={{0,2},{1,3},{2,0},{3,1},{4,6},{5,7},{6,4},{7,5},{8,10},{9,11},{10,... | collective-permute-start | bytes 405512 | tf_op jit(solution)/shard_map/ppermute | solution.py:331
  22.3 7.1 %collective-permute-start.2 = (bf16[528,128]{1,0:T(8,128)(2,1)S(1)}, bf16[528,128]{1,0:T(8,128)(2,1)S(1)}, u32[]{:S(2)}, u32[]{:S(2)}) collective-permute-start(bf16[528,128]{1,0:T(8,128)(2,1)S(1)} %get-tuple-element.55), channel_id=1, source_target_pairs={{0,2},{1,3},{2,0},{3,1},{4,6},{5,7},{6,4},{7,5},{8,10},{9,11},{10,... | collective-permute-start | bytes 405512 | tf_op jit(solution)/shard_map/ppermute | solution.py:331
  27.2 5.6 %collective-permute-start.9 = (bf16[528,128]{1,0:T(8,128)(2,1)S(1)}, bf16[528,128]{1,0:T(8,128)(2,1)S(1)}, u32[]{:S(2)}, u32[]{:S(2)}) collective-permute-start(bf16[528,128]{1,0:T(8,128)(2,1)S(1)} %get-tuple-element.79), channel_id=1, source_target_pairs={{0,4},{1,5},{2,6},{3,7},{4,0},{5,1},{6,2},{7,3},{8,12},{9,13},{10,... | collective-permute-start | bytes 405512 | tf_op jit(solution)/shard_map/ppermute | solution.py:331
  29.5 7.1 %collective-permute-start.3 = (bf16[528,128]{1,0:T(8,128)(2,1)S(1)}, bf16[528,128]{1,0:T(8,128)(2,1)S(1)}, u32[]{:S(2)}, u32[]{:S(2)}) collective-permute-start(bf16[528,128]{1,0:T(8,128)(2,1)S(1)} %get-tuple-element.58), channel_id=1, source_target_pairs={{0,4},{1,5},{2,6},{3,7},{4,0},{5,1},{6,2},{7,3},{8,12},{9,13},{10,... | collective-permute-start | bytes 405512 | tf_op jit(solution)/shard_map/ppermute | solution.py:331
  33.5 12.1 %collective-permute-start.10 = (bf16[528,128]{1,0:T(8,128)(2,1)S(1)}, bf16[528,128]{1,0:T(8,128)(2,1)S(1)}, u32[]{:S(2)}, u32[]{:S(2)}) collective-permute-start(bf16[528,128]{1,0:T(8,128)(2,1)S(1)} %get-tuple-element.80), channel_id=1, source_target_pairs={{0,8},{1,9},{2,10},{3,11},{4,12},{5,13},{6,14},{7,15},{8,0},{9,1},... | collective-permute-start | bytes 405512 | tf_op jit(solution)/shard_map/ppermute | solution.py:331
  37.4 16.6 %copy-start.7 = (f32[64]{0:T(128)S(1)}, f32[64]{0:T(128)}, u32[]{:S(2)}) copy-start(f32[64]{0:T(128)} %param.16) | copy-start | bytes 772
  37.4 18.1 %copy-start.1 = (bf16[128,4096]{1,0:T(8,128)(2,1)S(1)}, bf16[128,4096]{1,0:T(8,128)(2,1)}, u32[]{:S(2)}) copy-start(bf16[128,4096]{1,0:T(8,128)(2,1)} %gate.1) | copy-start | bytes 3145732
  37.4 10.0 %collective-permute-start.4 = (bf16[528,128]{1,0:T(8,128)(2,1)S(1)}, bf16[528,128]{1,0:T(8,128)(2,1)S(1)}, u32[]{:S(2)}, u32[]{:S(2)}) collective-permute-start(bf16[528,128]{1,0:T(8,128)(2,1)S(1)} %get-tuple-element.59), channel_id=1, source_target_pairs={{0,8},{1,9},{2,10},{3,11},{4,12},{5,13},{6,14},{7,15},{8,0},{9,1},... | collective-permute-start | bytes 405512 | tf_op jit(solution)/shard_map/ppermute | solution.py:331
  45.8 5.9 %collective-permute-start.11 = (bf16[512,128]{1,0:T(8,128)(2,1)S(1)}, bf16[512,128]{1,0:T(8,128)(2,1)S(1)}, u32[]{:S(2)}, u32[]{:S(2)}) collective-permute-start(bf16[512,128]{1,0:T(8,128)(2,1)S(1)} %get-tuple-element.84), channel_id=1, source_target_pairs={{0,2},{1,3},{2,0},{3,1},{4,6},{5,7},{6,4},{7,5},{8,10},{9,11},{10,... | collective-permute-start | bytes 393224 | tf_op jit(solution)/shard_map/ppermute | solution.py:331
  47.5 5.6 %collective-permute-start.5 = (bf16[512,128]{1,0:T(8,128)(2,1)S(1)}, bf16[512,128]{1,0:T(8,128)(2,1)S(1)}, u32[]{:S(2)}, u32[]{:S(2)}) collective-permute-start(bf16[512,128]{1,0:T(8,128)(2,1)S(1)} %get-tuple-element.63), channel_id=1, source_target_pairs={{0,2},{1,3},{2,0},{3,1},{4,6},{5,7},{6,4},{7,5},{8,10},{9,11},{10,... | collective-permute-start | bytes 393224 | tf_op jit(solution)/shard_map/ppermute | solution.py:331
  52.5 6.4 %collective-permute-start.12 = (bf16[1024,128]{1,0:T(8,128)(2,1)}, bf16[1024,128]{1,0:T(8,128)(2,1)}, u32[]{:S(2)}, u32[]{:S(2)}) collective-permute-start(bf16[1024,128]{1,0:T(8,128)(2,1)} %get-tuple-element.86), channel_id=1, source_target_pairs={{0,1},{1,0},{2,3},{3,2},{4,5},{5,4},{6,7},{7,6},{8,9},{9,8},{10,11... | collective-permute-start | bytes 786440 | tf_op jit(solution)/shard_map/ppermute | solution.py:331
  53.1 5.9 %copy-start.5 = (f32[4096]{0:T(1024)S(1)}, f32[4096]{0:T(1024)}, u32[]{:S(2)}) copy-start(f32[4096]{0:T(1024)} %param.17) | copy-start | bytes 49156
  53.9 6.4 %collective-permute-start.6 = (bf16[1024,128]{1,0:T(8,128)(2,1)}, bf16[1024,128]{1,0:T(8,128)(2,1)}, u32[]{:S(2)}, u32[]{:S(2)}) collective-permute-start(bf16[1024,128]{1,0:T(8,128)(2,1)} %get-tuple-element.65), channel_id=1, source_target_pairs={{0,1},{1,0},{2,3},{3,2},{4,5},{5,4},{6,7},{7,6},{8,9},{9,8},{10,11... | collective-permute-start | bytes 786440 | tf_op jit(solution)/shard_map/ppermute | solution.py:331

commit v2 on v1

v2 whole, which is shorter than its diff:
```python
import functools

import jax
import jax.numpy as jnp
from jax import lax
from jax.experimental import pallas as pl
from jax.experimental.pallas import tpu as pltpu
from jax.sharding import PartitionSpec as P

HEADS = 64
HEAD_DIM = 64
STATE = 128
GROUPS = 8
PER_GROUP = HEADS // GROUPS
GROUP_COLS = PER_GROUP * HEAD_DIM
INNER = HEADS * HEAD_DIM
KEYS = GROUPS * STATE
CONV_COLS = INNER + 2 * KEYS
SPAN = 128
LANES = 128
TILES = GROUP_COLS // LANES
PARTS = 2
PART_GROUPS = GROUPS // PARTS
HALF_GROUPS = PART_GROUPS // 2
QUARTER_GROUPS = HALF_GROUPS // 2
HALF_TILES = HALF_GROUPS * TILES
QUARTER_TILES = QUARTER_GROUPS * TILES
HALF_ROWS = HALF_TILES * STATE
QUARTER_ROWS = QUARTER_TILES * STATE
F32 = jnp.float32
BF16 = jnp.bfloat16
VMEM_LIMIT = 24 * 1024 * 1024


def extra_rows(tiles):
    return -(-2 * tiles // 16) * 16


def decay_rows(tiles):
    return -(-tiles // 8) * 8


def call(body, outs, *args, after=(), hbm=(), aliases=None, scratch=()):
    count = len(args)
    args = [pltpu.with_memory_space_constraint(a, pltpu.HBM) if i in hbm else a for i, a in enumerate(args)]
    specs = [pl.BlockSpec(memory_space=pltpu.HBM if i in hbm else pltpu.VMEM) for i in range(count)]
    specs += [pl.BlockSpec(memory_space=pl.ANY) for _ in after]

    def kernel(*refs):
        body(*refs[:count], *refs[count + len(after) :])

    return pl.pallas_call(
        kernel,
        out_shape=[space(shape, kind) for shape, kind, space in outs],
        in_specs=specs,
        out_specs=[pl.BlockSpec(memory_space=space) for _, _, space in outs],
        scratch_shapes=list(scratch),
        input_output_aliases=aliases or {},
        compiler_params=pltpu.CompilerParams(vmem_limit_bytes=VMEM_LIMIT),
    )(*args, *after)


def vmem(rows, cols, kind):
    return ((rows, cols), kind, pltpu.VMEM)


def dot(a, b, dims=((1,), (0,))):
    return lax.dot_general(a, b, (dims, ((), ())), preferred_element_type=F32)


def silu(v):
    return v / (1.0 + jnp.exp(-v))


def pieces(v, count):
    found = []
    for _ in range(count):
        piece = v.astype(BF16)
        found.append(piece)
        v = v - piece.astype(F32)
    return found


def spread(group):
    row = lax.broadcasted_iota(jnp.int32, (2 * HEADS, GROUP_COLS), 0)
    lane = lax.broadcasted_iota(jnp.int32, (2 * HEADS, GROUP_COLS), 1)
    head = group * PER_GROUP + lane // HEAD_DIM
    return ((row == head) | (row == head + HEADS)).astype(BF16)


def columns(group, width, start=0):
    return pl.ds(pl.multiple_of(start + group * width, LANES), width)


def convolve_into(rows, padded, weight_ref, bias_ref, cols):
    total = bias_ref[:, cols]
    for tap in range(4):
        total = total + weight_ref[tap : tap + 1, cols].astype(F32) * padded[5 + tap : 5 + tap + rows, :]
    return silu(total).astype(BF16)


def accurate_log1p(u):
    w = 1.0 + u
    return jnp.where(w == 1.0, u, jnp.log(w) * (u / jnp.where(w == 1.0, 1.0, w - 1.0)))


def part_columns(part):
    return (
        (part * PART_GROUPS * GROUP_COLS, PART_GROUPS * GROUP_COLS),
        (INNER + part * PART_GROUPS * STATE, PART_GROUPS * STATE),
    )


def convolve_part(source, halo, weight, bias, padded, spans, outs, rows=SPAN):
    for (start, width), out in zip(spans, outs):

        @pl.loop(0, width // 512)
        def _(i, start=start, out=out):
            cols = columns(i, 512, start)
            padded[0:8, :] = jnp.zeros((8, 512), F32)
            if halo is not None:
                padded[5:8, :] = halo[:, cols].astype(F32)
            padded[8 : 8 + rows, :] = source[0:rows, cols].astype(F32)
            out[0:rows, columns(i, 512)] = convolve_into(rows, padded, weight, bias, cols)


def prepare(
    x, raw_t, step_bias, decay_log, skip, weight_in, bias_in,
    held, weight, bias, values, keys, both, both_t, tail_pair, carry_pair, row_pair,
    padded, raw_here, small, sems,
):
    first = part_columns(0)
    pieces_of_x = list(first)
    at = 0
    for start, width in sorted(first) + [(CONV_COLS, 0)]:
        if start > at:
            pieces_of_x.append((at, start - at))
        at = start + width
    copies = [
        pltpu.make_async_copy(raw_t, raw_here, sems.at[0]),
        pltpu.make_async_copy(step_bias, small.at[0:1], sems.at[1]),
        pltpu.make_async_copy(decay_log, small.at[8:9], sems.at[2]),
        pltpu.make_async_copy(skip, small.at[16:17], sems.at[3]),
        pltpu.make_async_copy(weight_in, weight, sems.at[4]),
        pltpu.make_async_copy(bias_in, bias, sems.at[5]),
    ]
    for i, (start, width) in enumerate(pieces_of_x):
        cols = slice(start, start + width)
        copies.append(pltpu.make_async_copy(x.at[:, cols], held.at[:, cols], sems.at[6 + i]))
    for copy in copies:
        copy.start()
    for copy in copies[:4]:
        copy.wait()
    raw = raw_here[...].astype(F32)
    raw = jnp.concatenate([raw, raw], axis=0).T[:, :HEADS] + small[0:1, :]
    sizes = jnp.maximum(raw, 0.0) + accurate_log1p(jnp.exp(-jnp.abs(raw)))
    log_decay = sizes * -jnp.exp(small[8:9, :])
    row = lax.broadcasted_iota(jnp.int32, (SPAN, SPAN), 0)
    lane = lax.broadcasted_iota(jnp.int32, (SPAN, SPAN), 1)
    lower = (row >= lane).astype(BF16)
    cumulative = sum(dot(lower, piece) for piece in pieces(log_decay, 3))
    total = cumulative[SPAN - 1 : SPAN, :]
    tail = jnp.exp(total - cumulative) * sizes
    joined = jnp.concatenate([cumulative, sizes], axis=1)
    both[...] = joined
    both_t[...] = joined.T
    tail_pair[...] = jnp.concatenate(pieces(tail, 2), axis=1)
    carry_pair[...] = jnp.concatenate(pieces(jnp.exp(cumulative), 2), axis=1)
    rows = jnp.concatenate(
        [jnp.broadcast_to(jnp.exp(total), (8, HEADS)), jnp.broadcast_to(small[16:17, :], (8, HEADS))], axis=0
    )
    row_pair[...] = jnp.concatenate(pieces(rows, 2), axis=1)
    for copy in copies[4:8]:
        copy.wait()
    convolve_part(held, None, weight, bias, padded, first, (values, keys))
    for copy in copies[8:]:
        copy.wait()


def prepare_rest(held, halo, weight, bias, *refs):
    spans = [span for part in range(1, PARTS) for span in part_columns(part)] + [(INNER + KEYS, KEYS)]
    convolve_part(held, halo, weight, bias, refs[-1], spans, refs[:-1])


def put_decays(send, tiles, decays):
    high = [d.astype(BF16).astype(F32) for d in decays]
    low = [d - h for d, h in zip(decays, high)]
    rows = high + low
    spare = extra_rows(tiles) - len(rows)
    block = jnp.concatenate(rows + [jnp.zeros((spare, LANES), F32)] * (spare > 0), axis=0)
    send[tiles * STATE : tiles * STATE + extra_rows(tiles), :] = block.astype(BF16)


def increments(first, *refs):
    if first:
        held, halo, weight, bias, raw_values, raw_keys = refs[:6]
        tail_pair, row_pair, send, keep, keep_decay, values_ref, keys_ref, padded, value_fix, key_fix = refs[6:]
        convolve_part(held, halo, weight, bias, padded, part_columns(0), (value_fix, key_fix), 16)
    else:
        values_ref, keys_ref, tail_pair, row_pair, send, keep, keep_decay = refs
    part = 0 if first else 1
    core = lax.axis_index("seq") & 1
    for target, side in ((send, 1 - core), (keep, core)):
        decays = []
        for j in range(HALF_GROUPS):
            local = side * HALF_GROUPS + j
            value_cols, key_cols = columns(local, GROUP_COLS), columns(local, STATE)
            to_channels = spread(part * PART_GROUPS + local)
            scale = dot(tail_pair[...], to_channels)
            if first:
                values = jnp.concatenate([value_fix[:, value_cols], raw_values[16:, value_cols]], axis=0)
                keys = jnp.concatenate([key_fix[:, key_cols], raw_keys[16:, key_cols]], axis=0)
                values_ref[:, value_cols] = values
                keys_ref[:, key_cols] = keys
            else:
                values, keys = values_ref[:, value_cols], keys_ref[:, key_cols]
            grown = dot(keys, (values.astype(F32) * scale).astype(BF16), ((0,), (0,)))
            decay = dot(row_pair[...], to_channels)
            for t in range(TILES):
                at = (j * TILES + t) * STATE
                target[at : at + STATE, :] = grown[:, t * LANES : (t + 1) * LANES].astype(target.dtype)
                decays.append(decay[0:1, t * LANES : (t + 1) * LANES])
        if target is send:
            put_decays(send, HALF_TILES, decays)
        else:
            for t, d in enumerate(decays):
                keep_decay[t : t + 1, :] = d


def tile_rows(t):
    return pl.ds(pl.multiple_of(t * STATE, STATE), STATE)


def received_decays(recv, tiles, scratch):
    rows = recv[tiles * STATE : tiles * STATE + extra_rows(tiles), :].astype(F32)
    scratch[0:tiles, :] = rows[0:tiles] + rows[tiles : 2 * tiles]


def join_cores(keep, keep_decay, recv, send, own, own_decay, other):
    me = lax.axis_index("seq")
    first = (me & 1) == 0
    y = (me >> 1) & 1
    received_decays(recv, HALF_TILES, other)

    def joined(t):
        mine, theirs = keep[tile_rows(t), :], recv[tile_rows(t), :].astype(F32)
        decay_mine, decay_theirs = keep_decay[pl.ds(t, 1), :], other[pl.ds(t, 1), :]
        early, late = jnp.where(first, mine, theirs), jnp.where(first, theirs, mine)
        return jnp.where(first, decay_theirs, decay_mine) * early + late, decay_mine * decay_theirs

    decays = []
    for t in range(QUARTER_TILES):
        state, decay = joined((1 - y) * QUARTER_TILES + t)
        send[t * STATE : (t + 1) * STATE, :] = state.astype(BF16)
        decays.append(decay)
    put_decays(send, QUARTER_TILES, decays)
    for t in range(QUARTER_TILES):
        state, decay = joined(y * QUARTER_TILES + t)
        own[t * STATE : (t + 1) * STATE, :] = state
        own_decay[t : t + 1, :] = decay


def join_pair(bit, carried, totals, *refs):
    state, decay, recv = refs[:3]
    refs = refs[3:]
    if carried:
        before, before_decay = refs[:2]
        refs = refs[2:]
    send = refs[0]
    refs = refs[1:]
    if totals:
        new_state, new_decay = refs[:2]
        refs = refs[2:]
    if bit >= 2:
        new_before, new_before_decay = refs[:2]
        refs = refs[2:]
    (other,) = refs
    upper = ((lax.axis_index("seq") >> bit) & 1) == 1
    received_decays(recv, QUARTER_TILES, other)
    decays = []
    for t in range(QUARTER_TILES):
        rows = slice(t * STATE, (t + 1) * STATE)
        mine, theirs = state[rows, :], recv[rows, :].astype(F32)
        d_mine, d_theirs = decay[t : t + 1, :], other[t : t + 1, :]
        early, late = jnp.where(upper, theirs, mine), jnp.where(upper, mine, theirs)
        total = jnp.where(upper, d_mine, d_theirs) * early + late
        send[rows, :] = total.astype(BF16)
        if totals:
            new_state[rows, :] = total
            new_decay[t : t + 1, :] = d_mine * d_theirs
        decays.append(d_mine * d_theirs)
        if bit >= 2:
            if carried:
                b, bd = before[rows, :], before_decay[t : t + 1, :]
                new_before[rows, :] = jnp.where(upper, b + bd * theirs, b)
                new_before_decay[t : t + 1, :] = jnp.where(upper, bd * d_theirs, bd)
            else:
                new_before[rows, :] = jnp.where(upper, theirs, 0.0)
                new_before_decay[t : t + 1, :] = jnp.where(upper, d_theirs, 1.0)
    put_decays(send, QUARTER_TILES, decays)


def to_planes(bit, carried, *refs):
    recv = refs[0]
    refs = refs[1:]
    if carried:
        before, before_decay = refs[:2]
        refs = refs[2:]
    own, own_decay, recv_pair, send, start, other = refs
    me = lax.axis_index("seq")
    upper = ((me >> bit) & 1) == 1
    y = ((me >> 1) & 1) == 1
    received_decays(recv_pair, QUARTER_TILES, other)
    for t in range(QUARTER_TILES):
        rows = slice(t * STATE, (t + 1) * STATE)
        theirs = recv[rows, :].astype(F32)
        if carried:
            b = before[rows, :]
            plane = jnp.where(upper, b + before_decay[t : t + 1, :] * theirs, b)
        else:
            plane = jnp.where(upper, theirs, 0.0)
        d = jnp.where(y, other[t : t + 1, :], own_decay[t : t + 1, :])
        grown = jnp.where(y, recv_pair[rows, :].astype(F32), own[rows, :])
        later = d * plane + grown
        send[rows, :] = jnp.where(y, plane, later).astype(BF16)
        start[rows, :] = jnp.where(y, later, plane)


def to_cores(start, recv_start, keep, keep_decay, recv, send, own, other):
    me = lax.axis_index("seq")
    first = (me & 1) == 0
    y = (me >> 1) & 1
    received_decays(recv, HALF_TILES, other)
    for side in range(2):
        for t in range(QUARTER_TILES):
            rows = slice(t * STATE, (t + 1) * STATE)
            at = (y if side == 0 else 1 - y) * QUARTER_TILES + t
            chip = start[rows, :] if side == 0 else recv_start[rows, :].astype(F32)
            d = jnp.where(first, keep_decay[pl.ds(at, 1), :], other[pl.ds(at, 1), :])
            grown = jnp.where(first, keep[tile_rows(at), :], recv[tile_rows(at), :].astype(F32))
            later = d * chip + grown
            send[tile_rows(at), :] = jnp.where(first, later, chip).astype(BF16)
            own[tile_rows(at), :] = jnp.where(first, chip, later).astype(BF16)


def inside(part, values_ref, keys_ref, reads_ref, both, both_t, carry_pair, row_pair, gate, base, slope):
    row = lax.broadcasted_iota(jnp.int32, (SPAN, SPAN), 0)
    lane = lax.broadcasted_iota(jnp.int32, (SPAN, SPAN), 1)
    causal = row >= lane
    for j in range(PART_GROUPS):
        group = part * PART_GROUPS + j
        cols = slice(j * GROUP_COLS, (j + 1) * GROUP_COLS)
        values = values_ref[:, cols]
        writes = keys_ref[:, j * STATE : (j + 1) * STATE]
        reads = reads_ref[:, group * STATE : (group + 1) * STATE]
        scores = dot(reads, writes, ((1,), (1,)))
        found = []
        for i in range(PER_GROUP):
            h = group * PER_GROUP + i
            gap = both[:, h : h + 1] - both_t[h : h + 1, :]
            weights = scores * jnp.exp(jnp.where(causal, gap, -jnp.inf)) * both_t[HEADS + h : HEADS + h + 1, :]
            found.append(dot(weights.astype(BF16), values[:, i * HEAD_DIM : (i + 1) * HEAD_DIM]))
        within = jnp.concatenate(found, axis=1)
        to_channels = spread(group)
        skip = dot(row_pair[...], to_channels)[8:9, :]
        opened = silu(gate[:, group * GROUP_COLS : (group + 1) * GROUP_COLS].astype(F32))
        base[:, cols] = (within + skip * values.astype(F32)) * opened
        slope[:, cols] = dot(carry_pair[...], to_channels) * opened


def finish(part, mine, chained, *refs):
    reads_ref, source, base, slope, gain = refs[:5]
    out, made, sems = refs[-3:]
    core = lax.axis_index("seq") & 1
    side = core if mine else 1 - core
    copies = []
    for j in range(HALF_GROUPS):
        local = side * HALF_GROUPS + j
        group = part * PART_GROUPS + local
        cols = columns(local, GROUP_COLS)
        starts = jnp.concatenate(
            [source[(j * TILES + t) * STATE : (j * TILES + t + 1) * STATE, :] for t in range(TILES)], axis=1
        )
        gated = base[:, cols] + slope[:, cols] * dot(reads_ref[:, columns(group, STATE)], starts)
        mean = jnp.mean(gated * gated, axis=1, keepdims=True)
        made[j] = (gated * lax.rsqrt(mean + 1e-5) * gain[:, columns(group, GROUP_COLS)]).astype(BF16)
        copy = pltpu.make_async_copy(made.at[j], out.at[:, columns(group, GROUP_COLS)], sems.at[j])
        copy.start()
        copies.append(copy)
    for copy in copies:
        copy.wait()


def shards(mixer_input, gate_input, step_raw, conv_weight, conv_bias, step_bias, decay_log, skip_gain, norm_gain):
    devices = lax.axis_size("seq")
    bits = devices.bit_length() - 1

    def across(value, bit):
        return lax.ppermute(value, "seq", [(i, i ^ (1 << bit)) for i in range(devices)])

    part_values = vmem(SPAN, PART_GROUPS * GROUP_COLS, BF16)
    part_keys = vmem(SPAN, PART_GROUPS * STATE, BF16)
    half_send = vmem(HALF_ROWS + extra_rows(HALF_TILES), LANES, BF16)
    quarter_send = vmem(QUARTER_ROWS + extra_rows(QUARTER_TILES), LANES, BF16)
    quarter = vmem(QUARTER_ROWS, LANES, F32)
    quarter_decay = vmem(decay_rows(QUARTER_TILES), LANES, F32)
    half_keep = [half_send, vmem(HALF_ROWS, LANES, F32), vmem(decay_rows(HALF_TILES), LANES, F32)]
    half_scratch = [pltpu.VMEM((decay_rows(HALF_TILES), LANES), F32)]
    quarter_scratch = [pltpu.VMEM((decay_rows(QUARTER_TILES), LANES), F32)]

    halo = lax.ppermute(mixer_input[SPAN - 3 :], "seq", [(i, i + 1) for i in range(devices - 1)])
    held, weight, bias, raw_values, raw_keys, both, both_t, tail_pair, carry_pair, row_pair = call(
        prepare,
        [
            vmem(SPAN, CONV_COLS, BF16),
            vmem(4, CONV_COLS, BF16),
            vmem(1, CONV_COLS, F32),
            part_values,
            part_keys,
            vmem(SPAN, 2 * HEADS, F32),
            vmem(2 * HEADS, SPAN, F32),
            vmem(SPAN, 2 * HEADS, BF16),
            vmem(SPAN, 2 * HEADS, BF16),
            vmem(16, 2 * HEADS, BF16),
        ],
        mixer_input, step_raw.T, step_bias[None, :], decay_log[None, :], skip_gain[None, :],
        conv_weight, conv_bias[None, :],
        hbm=range(7),
        scratch=[
            pltpu.VMEM((8 + SPAN, 512), F32),
            pltpu.VMEM((HEADS, SPAN), BF16),
            pltpu.VMEM((24, HEADS), F32),
            pltpu.SemaphoreType.DMA((12,)),
        ],
    )
    send_a, keep_a, keep_decay_a, values_a, keys_a = call(
        functools.partial(increments, True), half_keep + [part_values, part_keys],
        held, halo, weight, bias, raw_values, raw_keys, tail_pair, row_pair,
        scratch=[
            pltpu.VMEM((24, 512), F32),
            pltpu.VMEM((16, PART_GROUPS * GROUP_COLS), BF16),
            pltpu.VMEM((16, PART_GROUPS * STATE), BF16),
        ],
    )
    recv_a = across(send_a, 0)
    values_b, keys_b, reads = call(
        prepare_rest, [part_values, part_keys, vmem(SPAN, KEYS, BF16)],
        held, halo, weight, bias, after=(keep_decay_a,), scratch=[pltpu.VMEM((8 + SPAN, 512), F32)],
    )

    def cores(keep, keep_decay, recv, after):
        return call(
            join_cores, [quarter_send, quarter, quarter_decay], keep, keep_decay, recv,
            after=after, scratch=half_scratch,
        )

    def pair(bit, state, decay, recv, carried, after):
        totals = bit + 1 < bits - 1
        outs = call(
            functools.partial(join_pair, bit, bool(carried), totals),
            [quarter_send] + [quarter, quarter_decay] * totals + [quarter, quarter_decay] * (bit >= 2),
            state, decay, recv, *carried, after=after, scratch=quarter_scratch,
        )
        send = outs[0]
        state, decay = outs[1:3] if totals else (None, None)
        return send, state, decay, tuple(outs[-2:]) if bit >= 2 else ()

    def planes(recv, carried, own, own_decay, recv_pair, after):
        return call(
            functools.partial(to_planes, bits - 1, bool(carried)), [vmem(QUARTER_ROWS, LANES, BF16), quarter],
            recv, *carried, own, own_decay, recv_pair, after=after, scratch=quarter_scratch,
        )

    def split(start, recv_start, keep, keep_decay, recv, after):
        return call(
            to_cores, [vmem(HALF_ROWS, LANES, BF16)] * 2, start, recv_start, keep, keep_decay, recv,
            after=after, scratch=half_scratch,
        )

    def within(part, values, keys, after):
        return call(
            functools.partial(inside, part), [vmem(SPAN, PART_GROUPS * GROUP_COLS, F32)] * 2,
            values, keys, reads, both, both_t, carry_pair, row_pair, gate_input, after=after,
        )

    out = None

    def last(part, mine, source, base, slope):
        args = (reads, source, base, slope, norm_gain[None, :]) + ((out,) if out is not None else ())
        return call(
            functools.partial(finish, part, mine, out is not None),
            [((SPAN, INNER), BF16, pltpu.HBM)],
            *args,
            hbm=(5,) if out is not None else (),
            aliases={5: 0} if out is not None else None,
            scratch=[pltpu.VMEM((HALF_GROUPS, SPAN, GROUP_COLS), BF16), pltpu.SemaphoreType.DMA((HALF_GROUPS,))],
        )[0]

    send_pair_a, own_a, own_decay_a = cores(keep_a, keep_decay_a, recv_a, (reads,))
    recv_pair_a = across(send_pair_a, 1)
    send_b, keep_b, keep_decay_b = call(
        functools.partial(increments, False), half_keep, values_b, keys_b, tail_pair, row_pair,
        after=(own_decay_a,),
    )
    recv_b = across(send_b, 0)
    send_pair_b, own_b, own_decay_b = cores(keep_b, keep_decay_b, recv_b, ())
    recv_pair_b = across(send_pair_b, 1)
    found_a = pair(1, own_a, own_decay_a, recv_pair_a, (), (own_decay_b,))
    base_a, slope_a = within(0, values_a, keys_a, (found_a[0],))
    found_b = pair(1, own_b, own_decay_b, recv_pair_b, (), (base_a,))
    base_b = None
    for bit in range(2, bits - 1):
        send, state, decay, carried = found_a
        found_a = pair(bit, state, decay, across(send, bit), carried, (found_b[0],))
        if base_b is None:
            base_b, slope_b = within(1, values_b, keys_b, (found_a[0],))
        send, state, decay, carried = found_b
        found_b = pair(bit, state, decay, across(send, bit), carried, (found_a[0], base_b))
    start_send_a, start_a = planes(
        across(found_a[0], bits - 1), found_a[3], own_a, own_decay_a, recv_pair_a, (found_b[0],)
    )
    start_send_b, start_b = planes(
        across(found_b[0], bits - 1), found_b[3], own_b, own_decay_b, recv_pair_b, (start_send_a,)
    )
    core_send_a, own_start_a = split(
        start_a, across(start_send_a, 1), keep_a, keep_decay_a, recv_a, (start_send_b,)
    )
    out = last(0, True, own_start_a, base_a, slope_a)
    out = last(0, False, across(core_send_a, 0), base_a, slope_a)
    core_send_b, own_start_b = split(start_b, across(start_send_b, 1), keep_b, keep_decay_b, recv_b, ())
    out = last(1, True, own_start_b, base_b, slope_b)
    return last(1, False, across(core_send_b, 0), base_b, slope_b)


def solution(mesh):
    in_specs = (
        P(("groups", "seq"), None),
        P(("groups", "seq"), None),
        P(("groups", "seq"), None),
        P(),
        P(),
        P("groups"),
        P("groups"),
        P(),
        P(),
    )
    return jax.shard_map(
        shards, mesh=mesh, in_specs=in_specs, out_specs=P(("groups", "seq"), None), check_vma=False
    )
```

time: 63.4 us -> 51.2 us (0.81)
  local copies, waits for them, and re-layouts: 7.67 us -> 0.93 us
  waiting for transfers between devices: 17.4 us -> 14.2 us
  other arithmetic: 1.77 us -> 0 us
  Pallas kernels: 17.4 us -> 16.3 us
  starting transfers between devices: 18.3 us -> 19.3 us
    unnamed x17 -> x4, local copies, waits for them, and re-layouts: 5.22 us -> 0.01 us
    ppermute x12, waiting for transfers between devices: 17.4 us -> 14.2 us  [across(): lax.ppermute(value, 'seq', [(i, i ^ 1 << bit) for i in range(devices)])]
    pallas_call x16 -> x20, Pallas kernels: 17.4 us -> 16.3 us  [call(): pl.pallas_call(kernel, out_shape=[space(shape, kind) for shape, kind, spa...]
    concatenate x1 -> x0, other arithmetic: 1.06 us -> none  [shards(): return jnp.concatenate(finished, axis=1)]
    ppermute x12, starting transfers between devices: 16 us -> 17 us  [across(): lax.ppermute(value, 'seq', [(i, i ^ 1 << bit) for i in range(devices)])]
    reshape x1 -> x0, local copies, waits for them, and re-layouts: 0.84 us -> none  [shards(): jnp.broadcast_to(skip_gain[:, None], (HEADS, HEAD_DIM)).reshape(1, INNER)]
    select_n x1 -> x0, other arithmetic: 0.71 us -> none  [shards(): step = jax.nn.softplus(step_raw.astype(F32) + step_bias[None, :])]
    broadcast_in_dim x1 -> x0, local copies, waits for them, and re-layouts: 0.69 us -> none  [shards(): jnp.broadcast_to(skip_gain[:, None], (HEADS, HEAD_DIM)).reshape(1, INNER)]
  transfers between devices with their start and end apart: 13 -> 13, of which waited for: 8 -> 5; matrix products, arithmetic and copies ran while one was open for 5% -> 0% of each run, Pallas kernels for 21% -> 25%
where the time goes in v2:
time: 51.2 us; the launch traced here: 51 us
  starting transfers between devices  19.3 us (38%)
  Pallas kernels  16.3 us (32%)
  waiting for transfers between devices  14.2 us (28%)
  local copies, waits for them, and re-layouts  0.93 us (2%)
    ppermute x12, starting transfers between devices, across(): lax.ppermute(value, 'seq', [(i, i ^ 1 << bit) for i in range(devices)])  17 us
    pallas_call x20, Pallas kernels, call(): pl.pallas_call(kernel, out_shape=[space(shape, kind) for shape, kind, spa...  16.3 us
    ppermute x12, waiting for transfers between devices, across(): lax.ppermute(value, 'seq', [(i, i ^ 1 << bit) for i in range(devices)])  14.2 us
    ppermute x1, starting transfers between devices, shards(): lax.ppermute(mixer_input[SPAN - 3:], 'seq', [(i, i + 1) for i in range(de...  2.36 us
  transfers between devices with their start and end apart: 13, of which 5 were waited for; matrix products, arithmetic and copies ran while one was open for 0% of the time, Pallas kernels for 25%

profile of v2, /device:TPU:0, one launch (start us, length us, event | category | flops | bytes accessed | tf_op | source)
XLA Modules:
  0.0 51.0 jit_solution(1915380687469734765)
XLA Ops:
  0.0 0.9 %slice.3 = bf16[3,6144]{1,0:T(4,128)(2,1)S(1)} slice(bf16[128,6144]{1,0:T(8,128)(2,1)} %refs_0_.1), slice={[125:128], [0:6144]} | slice | bytes 73728 | tf_op jit(solution)/shard_map/slice | solution.py:411
  0.9 2.4 %collective-permute-start = (bf16[3,6144]{1,0:T(4,128)(2,1)S(1)}, bf16[3,6144]{1,0:T(4,128)(2,1)S(1)}, u32[]{:S(2)}, u32[]{:S(2)}) collective-permute-start(bf16[3,6144]{1,0:T(4,128)(2,1)S(1)} %slice.3), channel_id=1, source_target_pairs={{0,1},{1,2},{2,3},{3,4},{4,5},{5,6},{6,7},{7,8},{8,9},{9,10},{10,1... | collective-permute-start | bytes 110600 | tf_op jit(solution)/shard_map/ppermute | solution.py:411
  3.3 2.9 %shard_map.91 = (bf16[128,6144]{1,0:T(8,128)(2,1)S(1)}, bf16[4,6144]{1,0:T(4,128)(2,1)S(1)}, f32[1,6144]{1,0:T(1,128)S(1)}, bf16[128,2048]{1,0:T(8,128)(2,1)S(1)...) custom-call(bf16[128,6144]{1,0:T(8,128)(2,1)} %refs_0_.1, ...), custom_call_target="tpu_custom_call" | custom-call | tf_op jit(solution)/shard_map/pallas_call | solution.py:52
  6.2 0.0 collective-permute-done.refs_1_
  6.2 1.5 %shard_map.92 = (bf16[1040,128]{1,0:T(8,128)(2,1)S(1)}, f32[1024,128]{1,0:T(8,128)S(1)}, f32[8,128]{1,0:T(8,128)S(1)}, bf16[128,2048]{1,0:T(8,128)(2,1)S(1)}, bf16[128,512]{1,0:T(8,128)(2,1)S(1)}) custom-call(bf16[128,6144]{1,0:T(8,128)(2,1)S(1)} %get-tuple-element.56.refs_0_, bf16[3,6144]{1,0:T(4,128)(2,1)S(1)} %collective-permute-done.refs_1_, ...), custom_call_target="tpu_custom_call" | custom-call | tf_op jit(solution)/shard_map/pallas_call | solution.py:52
  7.7 2.7 %collective-permute-start.1 = (bf16[1040,128]{1,0:T(8,128)(2,1)S(1)}, bf16[1040,128]{1,0:T(8,128)(2,1)S(1)}, u32[]{:S(2)}, u32[]{:S(2)}) collective-permute-start(bf16[1040,128]{1,0:T(8,128)(2,1)S(1)} %get-tuple-element.68), channel_id=1, source_target_pairs={{0,1},{1,0},{2,3},{3,2},{4,5},{5,4},{6,7},{7,6},{8,9},{9,8},{10,11... | collective-permute-start | bytes 798728 | tf_op jit(solution)/shard_map/ppermute | solution.py:399
  10.4 2.3 %shard_map.93 = (bf16[128,2048]{1,0:T(8,128)(2,1)S(1)}, bf16[128,512]{1,0:T(8,128)(2,1)S(1)}, bf16[128,1024]{1,0:T(8,128)(2,1)S(1)}) custom-call(bf16[128,6144]{1,0:T(8,128)(2,1)S(1)} %get-tuple-element.56.refs_0_, bf16[3,6144]{1,0:T(4,128)(2,1)S(1)} %collective-permute-done.refs_1_, bf16[4,6144]{1,0:T(4,128)(2,1)S(1)} %get-tuple-element.57.refs_2_, ...), custom_call_target="tpu_custom_call" | custom-call | tf_op jit(solution)/shard_map/pallas_call | solution.py:52
  12.7 0.0 copy-start
  12.7 0.0 collective-permute-done.1.refs_2_.refs_4_
  12.7 0.1 shard_map.94
  12.8 1.2 %shard_map.95 = (bf16[1040,128]{1,0:T(8,128)(2,1)S(1)}, f32[1024,128]{1,0:T(8,128)S(1)}, f32[8,128]{1,0:T(8,128)S(1)}) custom-call(bf16[128,2048]{1,0:T(8,128)(2,1)S(1)} %get-tuple-element.65.refs_0_, bf16[128,512]{1,0:T(8,128)(2,1)S(1)} %get-tuple-element.66.refs_1_, bf16[128,128]{1,0:T(8,128)(2,1)S(1)} %get-tuple-element.61.refs_6_.refs_2_, ...), custom_call_target="tpu_custom_call" | custom-call | tf_op jit(solution)/shard_map/pallas_call | solution.py:52
  14.0 0.1 collective-permute-start.2
  14.1 1.6 %collective-permute-start.4 = (bf16[528,128]{1,0:T(8,128)(2,1)S(1)}, bf16[528,128]{1,0:T(8,128)(2,1)S(1)}, u32[]{:S(2)}, u32[]{:S(2)}) collective-permute-start(bf16[528,128]{1,0:T(8,128)(2,1)S(1)} %get-tuple-element.82), channel_id=1, source_target_pairs={{0,2},{1,3},{2,0},{3,1},{4,6},{5,7},{6,4},{7,5},{8,10},{9,11},{10,... | collective-permute-start | bytes 405512 | tf_op jit(solution)/shard_map/ppermute | solution.py:399
  15.7 0.0 collective-permute-done.2.refs_2_.refs_4_
  15.7 0.1 shard_map.96
  15.8 1.5 %collective-permute-start.3 = (bf16[528,128]{1,0:T(8,128)(2,1)S(1)}, bf16[528,128]{1,0:T(8,128)(2,1)S(1)}, u32[]{:S(2)}, u32[]{:S(2)}) collective-permute-start(bf16[528,128]{1,0:T(8,128)(2,1)S(1)} %get-tuple-element.75), channel_id=1, source_target_pairs={{0,2},{1,3},{2,0},{3,1},{4,6},{5,7},{6,4},{7,5},{8,10},{9,11},{10,... | collective-permute-start | bytes 405512 | tf_op jit(solution)/shard_map/ppermute | solution.py:399
  17.4 3.2 %collective-permute-done.4.refs_2_.refs_5_ = bf16[528,128]{1,0:T(8,128)(2,1)S(1)} collective-permute-done((bf16[528,128]{1,0:T(8,128)(2,1)S(1)}, bf16[528,128]{1,0:T(8,128)(2,1)S(1)}, u32[]{:S(2)}, u32[]{:S(2)}) %collective-permute-start.4) | collective-permute-done | bytes 135200 | tf_op jit(solution)/shard_map/ppermute | solution.py:399
  20.6 0.1 shard_map.97
  20.6 1.9 %collective-permute-start.6 = (bf16[528,128]{1,0:T(8,128)(2,1)S(1)}, bf16[528,128]{1,0:T(8,128)(2,1)S(1)}, u32[]{:S(2)}, u32[]{:S(2)}) collective-permute-start(bf16[528,128]{1,0:T(8,128)(2,1)S(1)} %get-tuple-element.83.refs_8_), channel_id=1, source_target_pairs={{0,4},{1,5},{2,6},{3,7},{4,0},{5,1},{6,2},{7,3},{8,12},{9,13},{10,... | collective-permute-start | bytes 405512 | tf_op jit(solution)/shard_map/ppermute | solution.py:399
  22.6 0.0 copy-done
  22.6 1.7 %shard_map.98 = (f32[128,2048]{1,0:T(8,128)S(1)}, f32[128,2048]{1,0:T(8,128)S(1)}) custom-call(bf16[128,2048]{1,0:T(8,128)(2,1)S(1)} %get-tuple-element.76.refs_0_, bf16[128,512]{1,0:T(8,128)(2,1)S(1)} %get-tuple-element.77.refs_1_, bf16[128,1024]{1,0:T(8,128)(2,1)S(1)} %get-tuple-element.64.refs_3_.refs_2_.refs_0_, ...), custom_call_target="tpu_custom_call" | custom-call | tf_op jit(solution)/shard_map/pallas_call | solution.py:52
  24.3 0.0 collective-permute-done.3.refs_2_.refs_5_
  24.3 0.1 shard_map.99
  24.3 0.4 collective-permute-start.5
  24.7 1.4 %collective-permute-done.6.refs_2_ = bf16[528,128]{1,0:T(8,128)(2,1)S(1)} collective-permute-done((bf16[528,128]{1,0:T(8,128)(2,1)S(1)}, bf16[528,128]{1,0:T(8,128)(2,1)S(1)}, u32[]{:S(2)}, u32[]{:S(2)}) %collective-permute-start.6) | collective-permute-done | bytes 135200 | tf_op jit(solution)/shard_map/ppermute | solution.py:399
  26.1 0.1 shard_map.100
  26.2 1.7 %shard_map.101 = (f32[128,2048]{1,0:T(8,128)S(1)}, f32[128,2048]{1,0:T(8,128)S(1)}) custom-call(bf16[128,2048]{1,0:T(8,128)(2,1)S(1)} %get-tuple-element.65.refs_0_, bf16[128,512]{1,0:T(8,128)(2,1)S(1)} %get-tuple-element.66.refs_1_, bf16[128,1024]{1,0:T(8,128)(2,1)S(1)} %get-tuple-element.64.refs_3_.refs_2_.refs_0_, ...), custom_call_target="tpu_custom_call" | custom-call | tf_op jit(solution)/shard_map/pallas_call | solution.py:52
  27.9 3.3 %collective-permute-start.8 = (bf16[528,128]{1,0:T(8,128)(2,1)S(1)}, bf16[528,128]{1,0:T(8,128)(2,1)S(1)}, u32[]{:S(2)}, u32[]{:S(2)}) collective-permute-start(bf16[528,128]{1,0:T(8,128)(2,1)S(1)} %get-tuple-element.90.refs_8_.refs_3_), channel_id=1, source_target_pairs={{0,8},{1,9},{2,10},{3,11},{4,12},{5,13},{6,14},{7,15},{8,0},{9,1},... | collective-permute-start | bytes 405512 | tf_op jit(solution)/shard_map/ppermute | solution.py:399
  31.3 0.0 collective-permute-done.5.refs_2_
  31.3 0.1 shard_map.102
  31.4 2.1 %collective-permute-start.7 = (bf16[528,128]{1,0:T(8,128)(2,1)S(1)}, bf16[528,128]{1,0:T(8,128)(2,1)S(1)}, u32[]{:S(2)}, u32[]{:S(2)}) collective-permute-start(bf16[528,128]{1,0:T(8,128)(2,1)S(1)} %get-tuple-element.92.refs_6_), channel_id=1, source_target_pairs={{0,8},{1,9},{2,10},{3,11},{4,12},{5,13},{6,14},{7,15},{8,0},{9,1},... | collective-permute-start | bytes 405512 | tf_op jit(solution)/shard_map/ppermute | solution.py:399
  33.5 5.9 %collective-permute-done.8.refs_0_ = bf16[528,128]{1,0:T(8,128)(2,1)S(1)} collective-permute-done((bf16[528,128]{1,0:T(8,128)(2,1)S(1)}, bf16[528,128]{1,0:T(8,128)(2,1)S(1)}, u32[]{:S(2)}, u32[]{:S(2)}) %collective-permute-start.8) | collective-permute-done | bytes 135200 | tf_op jit(solution)/shard_map/ppermute | solution.py:399
  39.4 0.1 shard_map.103
  39.5 1.7 %collective-permute-start.11 = (bf16[512,128]{1,0:T(8,128)(2,1)S(1)}, bf16[512,128]{1,0:T(8,128)(2,1)S(1)}, u32[]{:S(2)}, u32[]{:S(2)}) collective-permute-start(bf16[512,128]{1,0:T(8,128)(2,1)S(1)} %get-tuple-element.97.refs_6_), channel_id=1, source_target_pairs={{0,2},{1,3},{2,0},{3,1},{4,6},{5,7},{6,4},{7,5},{8,10},{9,11},{10,... | collective-permute-start | bytes 393224 | tf_op jit(solution)/shard_map/ppermute | solution.py:399
  41.2 0.0 collective-permute-done.7.refs_0_
  41.2 0.0 copy-start.1
  41.2 0.1 shard_map.104
  41.3 1.5 %collective-permute-start.9 = (bf16[512,128]{1,0:T(8,128)(2,1)S(1)}, bf16[512,128]{1,0:T(8,128)(2,1)S(1)}, u32[]{:S(2)}, u32[]{:S(2)}) collective-permute-start(bf16[512,128]{1,0:T(8,128)(2,1)S(1)} %get-tuple-element.99.refs_5_), channel_id=1, source_target_pairs={{0,2},{1,3},{2,0},{3,1},{4,6},{5,7},{6,4},{7,5},{8,10},{9,11},{10,... | collective-permute-start | bytes 393224 | tf_op jit(solution)/shard_map/ppermute | solution.py:399
  42.8 2.5 %collective-permute-done.11.refs_1_ = bf16[512,128]{1,0:T(8,128)(2,1)S(1)} collective-permute-done((bf16[512,128]{1,0:T(8,128)(2,1)S(1)}, bf16[512,128]{1,0:T(8,128)(2,1)S(1)}, u32[]{:S(2)}, u32[]{:S(2)}) %collective-permute-start.11) | collective-permute-done | bytes 131104 | tf_op jit(solution)/shard_map/ppermute | solution.py:399
  45.3 0.2 shard_map.106
  45.4 0.1 collective-permute-start.12
  45.5 1.2 %collective-permute-done.9.refs_1_ = bf16[512,128]{1,0:T(8,128)(2,1)S(1)} collective-permute-done((bf16[512,128]{1,0:T(8,128)(2,1)S(1)}, bf16[512,128]{1,0:T(8,128)(2,1)S(1)}, u32[]{:S(2)}, u32[]{:S(2)}) %collective-permute-start.9) | collective-permute-done | bytes 131104 | tf_op jit(solution)/shard_map/ppermute | solution.py:399
  46.7 0.2 shard_map.105
  46.8 0.1 collective-permute-start.10
  46.9 0.0 copy-done.1
  46.9 1.0 %shard_map.107.refs_5_ = bf16[128,4096]{1,0:T(8,128)(2,1)} custom-call(bf16[128,1024]{1,0:T(8,128)(2,1)S(1)} %get-tuple-element.64.refs_3_.refs_2_.refs_0_, bf16[1024,128]{1,0:T(8,128)(2,1)S(1)} %get-tuple-element.106.refs_1_, f32[128,2048]{1,0:T(8,128)S(1)} %get-tuple-element.84.refs_3_.refs_2_, f32[128,2048]{1,0:T(8,128)S(1)} %get-tuple-element.105.refs_3_, ...), custom_call_target="tpu_custom_call" | custom-call | tf_op jit(solution)/shard_map/pallas_call | solution.py:52
  47.9 0.0 collective-permute-done.12.refs_1_
  47.9 1.0 %shard_map.108.refs_5_ = bf16[128,4096]{1,0:T(8,128)(2,1)} custom-call(bf16[128,1024]{1,0:T(8,128)(2,1)S(1)} %get-tuple-element.64.refs_3_.refs_2_.refs_0_, bf16[1024,128]{1,0:T(8,128)(2,1)S(1)} %collective-permute-done.12.refs_1_, f32[128,2048]{1,0:T(8,128)S(1)} %get-tuple-element.84.refs_3_.refs_2_, ...), custom_call_target="tpu_custom_call", output_to_operand_aliasing={{}: (5, {})} | custom-call | tf_op jit(solution)/shard_map/pallas_call | solution.py:52
  48.9 1.0 %shard_map.109.refs_5_ = bf16[128,4096]{1,0:T(8,128)(2,1)} custom-call(bf16[128,1024]{1,0:T(8,128)(2,1)S(1)} %get-tuple-element.64.refs_3_.refs_2_.refs_0_, bf16[1024,128]{1,0:T(8,128)(2,1)S(1)} %get-tuple-element.102.refs_1_, f32[128,2048]{1,0:T(8,128)S(1)} %get-tuple-element.91.refs_4_.refs_2_, ...), custom_call_target="tpu_custom_call", output_to_operand_aliasing={{}: (5, {})} | custom-call | tf_op jit(solution)/shard_map/pallas_call | solution.py:52
  49.9 0.0 collective-permute-done.10.refs_1_
  50.0 1.0 %shard_map.110 = bf16[128,4096]{1,0:T(8,128)(2,1)} custom-call(bf16[128,1024]{1,0:T(8,128)(2,1)S(1)} %get-tuple-element.64.refs_3_.refs_2_.refs_0_, bf16[1024,128]{1,0:T(8,128)(2,1)S(1)} %collective-permute-done.10.refs_1_, f32[128,2048]{1,0:T(8,128)S(1)} %get-tuple-element.91.refs_4_.refs_2_, ...), custom_call_target="tpu_custom_call", output_to_operand_aliasing={{}: (5, {})} | custom-call | tf_op jit(solution)/shard_map/pallas_call | solution.py:52
Async XLA Ops:
  0.9 5.3 %collective-permute-start = (bf16[3,6144]{1,0:T(4,128)(2,1)S(1)}, bf16[3,6144]{1,0:T(4,128)(2,1)S(1)}, u32[]{:S(2)}, u32[]{:S(2)}) collective-permute-start(bf16[3,6144]{1,0:T(4,128)(2,1)S(1)} %slice.3), channel_id=1, source_target_pairs={{0,1},{1,2},{2,3},{3,4},{4,5},{5,6},{6,7},{7,8},{8,9},{9,10},{10,1... | collective-permute-start | bytes 110600 | tf_op jit(solution)/shard_map/ppermute | solution.py:411
  7.7 5.0 %collective-permute-start.1 = (bf16[1040,128]{1,0:T(8,128)(2,1)S(1)}, bf16[1040,128]{1,0:T(8,128)(2,1)S(1)}, u32[]{:S(2)}, u32[]{:S(2)}) collective-permute-start(bf16[1040,128]{1,0:T(8,128)(2,1)S(1)} %get-tuple-element.68), channel_id=1, source_target_pairs={{0,1},{1,0},{2,3},{3,2},{4,5},{5,4},{6,7},{7,6},{8,9},{9,8},{10,11... | collective-permute-start | bytes 798728 | tf_op jit(solution)/shard_map/ppermute | solution.py:399
  12.7 9.9 %copy-start = (bf16[128,4096]{1,0:T(8,128)(2,1)S(1)}, bf16[128,4096]{1,0:T(8,128)(2,1)}, u32[]{:S(2)}) copy-start(bf16[128,4096]{1,0:T(8,128)(2,1)} %refs_7_.3) | copy-start | bytes 3145732
  14.0 1.7 %collective-permute-start.2 = (bf16[1040,128]{1,0:T(8,128)(2,1)S(1)}, bf16[1040,128]{1,0:T(8,128)(2,1)S(1)}, u32[]{:S(2)}, u32[]{:S(2)}) collective-permute-start(bf16[1040,128]{1,0:T(8,128)(2,1)S(1)} %get-tuple-element.72), channel_id=1, source_target_pairs={{0,1},{1,0},{2,3},{3,2},{4,5},{5,4},{6,7},{7,6},{8,9},{9,8},{10,11... | collective-permute-start | bytes 798728 | tf_op jit(solution)/shard_map/ppermute | solution.py:399
  14.1 6.5 %collective-permute-start.4 = (bf16[528,128]{1,0:T(8,128)(2,1)S(1)}, bf16[528,128]{1,0:T(8,128)(2,1)S(1)}, u32[]{:S(2)}, u32[]{:S(2)}) collective-permute-start(bf16[528,128]{1,0:T(8,128)(2,1)S(1)} %get-tuple-element.82), channel_id=1, source_target_pairs={{0,2},{1,3},{2,0},{3,1},{4,6},{5,7},{6,4},{7,5},{8,10},{9,11},{10,... | collective-permute-start | bytes 405512 | tf_op jit(solution)/shard_map/ppermute | solution.py:399
  15.8 8.4 %collective-permute-start.3 = (bf16[528,128]{1,0:T(8,128)(2,1)S(1)}, bf16[528,128]{1,0:T(8,128)(2,1)S(1)}, u32[]{:S(2)}, u32[]{:S(2)}) collective-permute-start(bf16[528,128]{1,0:T(8,128)(2,1)S(1)} %get-tuple-element.75), channel_id=1, source_target_pairs={{0,2},{1,3},{2,0},{3,1},{4,6},{5,7},{6,4},{7,5},{8,10},{9,11},{10,... | collective-permute-start | bytes 405512 | tf_op jit(solution)/shard_map/ppermute | solution.py:399
  20.6 5.5 %collective-permute-start.6 = (bf16[528,128]{1,0:T(8,128)(2,1)S(1)}, bf16[528,128]{1,0:T(8,128)(2,1)S(1)}, u32[]{:S(2)}, u32[]{:S(2)}) collective-permute-start(bf16[528,128]{1,0:T(8,128)(2,1)S(1)} %get-tuple-element.83.refs_8_), channel_id=1, source_target_pairs={{0,4},{1,5},{2,6},{3,7},{4,0},{5,1},{6,2},{7,3},{8,12},{9,13},{10,... | collective-permute-start | bytes 405512 | tf_op jit(solution)/shard_map/ppermute | solution.py:399
  24.3 6.9 %collective-permute-start.5 = (bf16[528,128]{1,0:T(8,128)(2,1)S(1)}, bf16[528,128]{1,0:T(8,128)(2,1)S(1)}, u32[]{:S(2)}, u32[]{:S(2)}) collective-permute-start(bf16[528,128]{1,0:T(8,128)(2,1)S(1)} %get-tuple-element.87.refs_3_), channel_id=1, source_target_pairs={{0,4},{1,5},{2,6},{3,7},{4,0},{5,1},{6,2},{7,3},{8,12},{9,13},{10,... | collective-permute-start | bytes 405512 | tf_op jit(solution)/shard_map/ppermute | solution.py:399
  27.9 11.4 %collective-permute-start.8 = (bf16[528,128]{1,0:T(8,128)(2,1)S(1)}, bf16[528,128]{1,0:T(8,128)(2,1)S(1)}, u32[]{:S(2)}, u32[]{:S(2)}) collective-permute-start(bf16[528,128]{1,0:T(8,128)(2,1)S(1)} %get-tuple-element.90.refs_8_.refs_3_), channel_id=1, source_target_pairs={{0,8},{1,9},{2,10},{3,11},{4,12},{5,13},{6,14},{7,15},{8,0},{9,1},... | collective-permute-start | bytes 405512 | tf_op jit(solution)/shard_map/ppermute | solution.py:399
  31.4 9.8 %collective-permute-start.7 = (bf16[528,128]{1,0:T(8,128)(2,1)S(1)}, bf16[528,128]{1,0:T(8,128)(2,1)S(1)}, u32[]{:S(2)}, u32[]{:S(2)}) collective-permute-start(bf16[528,128]{1,0:T(8,128)(2,1)S(1)} %get-tuple-element.92.refs_6_), channel_id=1, source_target_pairs={{0,8},{1,9},{2,10},{3,11},{4,12},{5,13},{6,14},{7,15},{8,0},{9,1},... | collective-permute-start | bytes 405512 | tf_op jit(solution)/shard_map/ppermute | solution.py:399
  39.5 5.8 %collective-permute-start.11 = (bf16[512,128]{1,0:T(8,128)(2,1)S(1)}, bf16[512,128]{1,0:T(8,128)(2,1)S(1)}, u32[]{:S(2)}, u32[]{:S(2)}) collective-permute-start(bf16[512,128]{1,0:T(8,128)(2,1)S(1)} %get-tuple-element.97.refs_6_), channel_id=1, source_target_pairs={{0,2},{1,3},{2,0},{3,1},{4,6},{5,7},{6,4},{7,5},{8,10},{9,11},{10,... | collective-permute-start | bytes 393224 | tf_op jit(solution)/shard_map/ppermute | solution.py:399
  41.2 5.7 %copy-start.1 = (f32[4096]{0:T(1024)S(1)}, f32[4096]{0:T(1024)}, u32[]{:S(2)}) copy-start(f32[4096]{0:T(1024)} %param.17) | copy-start | bytes 49156
  41.3 5.4 %collective-permute-start.9 = (bf16[512,128]{1,0:T(8,128)(2,1)S(1)}, bf16[512,128]{1,0:T(8,128)(2,1)S(1)}, u32[]{:S(2)}, u32[]{:S(2)}) collective-permute-start(bf16[512,128]{1,0:T(8,128)(2,1)S(1)} %get-tuple-element.99.refs_5_), channel_id=1, source_target_pairs={{0,2},{1,3},{2,0},{3,1},{4,6},{5,7},{6,4},{7,5},{8,10},{9,11},{10,... | collective-permute-start | bytes 393224 | tf_op jit(solution)/shard_map/ppermute | solution.py:399
  45.4 2.5 %collective-permute-start.12 = (bf16[1024,128]{1,0:T(8,128)(2,1)S(1)}, bf16[1024,128]{1,0:T(8,128)(2,1)S(1)}, u32[]{:S(2)}, u32[]{:S(2)}) collective-permute-start(bf16[1024,128]{1,0:T(8,128)(2,1)S(1)} %get-tuple-element.104), channel_id=1, source_target_pairs={{0,1},{1,0},{2,3},{3,2},{4,5},{5,4},{6,7},{7,6},{8,9},{9,8},{10,11... | collective-permute-start | bytes 786440 | tf_op jit(solution)/shard_map/ppermute | solution.py:399
  46.8 3.1 %collective-permute-start.10 = (bf16[1024,128]{1,0:T(8,128)(2,1)S(1)}, bf16[1024,128]{1,0:T(8,128)(2,1)S(1)}, u32[]{:S(2)}, u32[]{:S(2)}) collective-permute-start(bf16[1024,128]{1,0:T(8,128)(2,1)S(1)} %get-tuple-element.100), channel_id=1, source_target_pairs={{0,1},{1,0},{2,3},{3,2},{4,5},{5,4},{6,7},{7,6},{8,9},{9,8},{10,11... | collective-permute-start | bytes 786440 | tf_op jit(solution)/shard_map/ppermute | solution.py:399

commit v3 on v2

v3 whole, which is shorter than its diff:
```python
import functools

import jax
import jax.numpy as jnp
from jax import lax
from jax.experimental import pallas as pl
from jax.experimental.pallas import tpu as pltpu
from jax.sharding import PartitionSpec as P

HEADS = 64
HEAD_DIM = 64
STATE = 128
GROUPS = 8
PER_GROUP = HEADS // GROUPS
GROUP_COLS = PER_GROUP * HEAD_DIM
INNER = HEADS * HEAD_DIM
KEYS = GROUPS * STATE
CONV_COLS = INNER + 2 * KEYS
SPAN = 128
LANES = 128
TILES = GROUP_COLS // LANES
SIZES = (4, 4)
F32 = jnp.float32
BF16 = jnp.bfloat16


class Part:
    def __init__(self, index):
        self.index = index
        self.first = sum(SIZES[:index])
        self.groups = SIZES[index]
        self.half_groups = self.groups // 2
        self.half_tiles = self.half_groups * TILES
        self.quarter_tiles = self.half_tiles // 2
        self.half_rows = self.half_tiles * STATE
        self.quarter_rows = self.quarter_tiles * STATE
        self.width = self.groups * GROUP_COLS
        self.spans = (
            (self.first * GROUP_COLS, self.width),
            (INNER + self.first * STATE, self.groups * STATE),
        )


VMEM_LIMIT = 24 * 1024 * 1024
FLOPS, BYTES = 1e9, 3e6


def extra_rows(tiles):
    return -(-2 * tiles // 16) * 16


def decay_rows(tiles):
    return -(-tiles // 8) * 8


def call(body, outs, *args, after=(), hbm=(), cost=0.1, scratch=()):
    count = len(args)
    args = [pltpu.with_memory_space_constraint(a, pltpu.HBM) if i in hbm else a for i, a in enumerate(args)]
    specs = [pl.BlockSpec(memory_space=pltpu.HBM if i in hbm else pltpu.VMEM) for i in range(count)]
    specs += [pl.BlockSpec(memory_space=pl.ANY) for _ in after]

    def kernel(*refs):
        body(*refs[:count], *refs[count + len(after) :])

    return pl.pallas_call(
        kernel,
        out_shape=[space(shape, kind) for shape, kind, space in outs],
        in_specs=specs,
        out_specs=[pl.BlockSpec(memory_space=space) for _, _, space in outs],
        scratch_shapes=list(scratch),
        compiler_params=pltpu.CompilerParams(vmem_limit_bytes=VMEM_LIMIT),
        cost_estimate=pl.CostEstimate(flops=int(cost * FLOPS), bytes_accessed=int(cost * BYTES), transcendentals=0),
    )(*args, *after)


def vmem(rows, cols, kind):
    return ((rows, cols), kind, pltpu.VMEM)


def dot(a, b, dims=((1,), (0,))):
    return lax.dot_general(a, b, (dims, ((), ())), preferred_element_type=F32)


def silu(v):
    half = 0.5 * v
    return half + half * jnp.tanh(half)


def pieces(v, count):
    found = []
    for _ in range(count):
        piece = v.astype(BF16)
        found.append(piece)
        v = v - piece.astype(F32)
    return found


def spread(group):
    row = lax.broadcasted_iota(jnp.int32, (2 * HEADS, GROUP_COLS), 0)
    lane = lax.broadcasted_iota(jnp.int32, (2 * HEADS, GROUP_COLS), 1)
    head = group * PER_GROUP + lane // HEAD_DIM
    return ((row == head) | (row == head + HEADS)).astype(BF16)


def columns(group, width, start=0):
    return pl.ds(pl.multiple_of(start + group * width, LANES), width)


def convolve_into(rows, padded, weight_ref, bias_ref, cols):
    total = bias_ref[:, cols]
    for tap in range(4):
        total = total + weight_ref[tap : tap + 1, cols].astype(F32) * padded[5 + tap : 5 + tap + rows, :]
    return silu(total).astype(BF16)


def accurate_log1p(u):
    w = 1.0 + u
    return jnp.where(w == 1.0, u, jnp.log(w) * (u / jnp.where(w == 1.0, 1.0, w - 1.0)))


def convolve_part(source, halo, weight, bias, padded, spans, outs, rows=SPAN):
    for (start, width), out in zip(spans, outs):

        block = min(width, 512)

        @pl.loop(0, width // block)
        def _(i, start=start, out=out, block=block):
            cols = columns(i, block, start)
            here = padded.at[:, 0:block]
            here[0:8, :] = jnp.zeros((8, block), F32)
            if halo is not None:
                here[5:8, :] = halo[:, cols].astype(F32)
            here[8 : 8 + rows, :] = source[0:rows, cols].astype(F32)
            out[0:rows, columns(i, block)] = convolve_into(rows, here, weight, bias, cols)


def prepare(
    part, x, raw_t, step_bias, decay_log, skip, weight_in, bias_in,
    held, weight, bias, values, keys, both, both_t, tail_pair, carry_pair, row_pair,
    padded, raw_here, small, sems,
):
    first = part.spans
    pieces_of_x = list(first)
    at = 0
    for start, width in sorted(first) + [(CONV_COLS, 0)]:
        if start > at:
            pieces_of_x.append((at, start - at))
        at = start + width
    copies = [
        pltpu.make_async_copy(raw_t, raw_here, sems.at[0]),
        pltpu.make_async_copy(step_bias, small.at[0:1], sems.at[1]),
        pltpu.make_async_copy(decay_log, small.at[8:9], sems.at[2]),
        pltpu.make_async_copy(skip, small.at[16:17], sems.at[3]),
        pltpu.make_async_copy(weight_in, weight, sems.at[4]),
        pltpu.make_async_copy(bias_in, bias, sems.at[5]),
    ]
    for i, (start, width) in enumerate(pieces_of_x):
        cols = slice(start, start + width)
        copies.append(pltpu.make_async_copy(x.at[:, cols], held.at[:, cols], sems.at[6 + i]))
    for copy in copies:
        copy.start()
    for copy in copies[:4]:
        copy.wait()
    raw = raw_here[...].astype(F32)
    raw = jnp.concatenate([raw, raw], axis=0).T[:, :HEADS] + small[0:1, :]
    sizes = jnp.maximum(raw, 0.0) + accurate_log1p(jnp.exp(-jnp.abs(raw)))
    log_decay = sizes * -jnp.exp(small[8:9, :])
    row = lax.broadcasted_iota(jnp.int32, (SPAN, SPAN), 0)
    lane = lax.broadcasted_iota(jnp.int32, (SPAN, SPAN), 1)
    lower = (row >= lane).astype(BF16)
    cumulative = sum(dot(lower, piece) for piece in pieces(log_decay, 3))
    total = cumulative[SPAN - 1 : SPAN, :]
    tail = jnp.exp(total - cumulative) * sizes
    joined = jnp.concatenate([cumulative, sizes], axis=1)
    both[...] = joined
    both_t[...] = joined.T
    tail_pair[...] = jnp.concatenate(pieces(tail, 2), axis=1)
    carry_pair[...] = jnp.concatenate(pieces(jnp.exp(cumulative), 2), axis=1)
    rows = jnp.concatenate(
        [jnp.broadcast_to(jnp.exp(total), (8, HEADS)), jnp.broadcast_to(small[16:17, :], (8, HEADS))], axis=0
    )
    row_pair[...] = jnp.concatenate(pieces(rows, 2), axis=1)
    for copy in copies[4:8]:
        copy.wait()
    convolve_part(held, None, weight, bias, padded, first, (values, keys))
    for copy in copies[8:]:
        copy.wait()


def prepare_rest(spans, held, halo, weight, bias, *refs):
    convolve_part(held, halo, weight, bias, refs[-1], spans, refs[:-1])


def put_decays(send, tiles, decays):
    high = [d.astype(BF16).astype(F32) for d in decays]
    low = [d - h for d, h in zip(decays, high)]
    rows = high + low
    spare = extra_rows(tiles) - len(rows)
    block = jnp.concatenate(rows + [jnp.zeros((spare, LANES), F32)] * (spare > 0), axis=0)
    send[tiles * STATE : tiles * STATE + extra_rows(tiles), :] = block.astype(BF16)


def increments(part, *refs):
    first = part.index == 0
    if first:
        held, halo, weight, bias, raw_values, raw_keys = refs[:6]
        tail_pair, row_pair, send, keep, keep_decay, values_ref, keys_ref, padded, value_fix, key_fix = refs[6:]
        convolve_part(held, halo, weight, bias, padded, part.spans, (value_fix, key_fix), 16)
    else:
        values_ref, keys_ref, tail_pair, row_pair, send, keep, keep_decay = refs
    core = lax.axis_index("seq") & 1
    for target, side in ((send, 1 - core), (keep, core)):
        decays = []
        for j in range(part.half_groups):
            local = side * part.half_groups + j
            value_cols, key_cols = columns(local, GROUP_COLS), columns(local, STATE)
            to_channels = spread(part.first + local)
            scale = dot(tail_pair[...], to_channels)
            if first:
                values = jnp.concatenate([value_fix[:, value_cols], raw_values[16:, value_cols]], axis=0)
                keys = jnp.concatenate([key_fix[:, key_cols], raw_keys[16:, key_cols]], axis=0)
                values_ref[:, value_cols] = values
                keys_ref[:, key_cols] = keys
            else:
                values, keys = values_ref[:, value_cols], keys_ref[:, key_cols]
            grown = dot(keys, (values.astype(F32) * scale).astype(BF16), ((0,), (0,)))
            decay = dot(row_pair[...], to_channels)
            for t in range(TILES):
                at = (j * TILES + t) * STATE
                target[at : at + STATE, :] = grown[:, t * LANES : (t + 1) * LANES].astype(target.dtype)
                decays.append(decay[0:1, t * LANES : (t + 1) * LANES])
        if target is send:
            put_decays(send, part.half_tiles, decays)
        else:
            for t, d in enumerate(decays):
                keep_decay[t : t + 1, :] = d


def tile_rows(t):
    return pl.ds(pl.multiple_of(t * STATE, STATE), STATE)


def received_decays(recv, tiles, scratch):
    rows = recv[tiles * STATE : tiles * STATE + extra_rows(tiles), :].astype(F32)
    scratch[0:tiles, :] = rows[0:tiles] + rows[tiles : 2 * tiles]


def join_cores(part, keep, keep_decay, recv, send, own, own_decay, other):
    me = lax.axis_index("seq")
    first = (me & 1) == 0
    y = (me >> 1) & 1
    received_decays(recv, part.half_tiles, other)

    def joined(t):
        mine, theirs = keep[tile_rows(t), :], recv[tile_rows(t), :].astype(F32)
        decay_mine, decay_theirs = keep_decay[pl.ds(t, 1), :], other[pl.ds(t, 1), :]
        early, late = jnp.where(first, mine, theirs), jnp.where(first, theirs, mine)
        return jnp.where(first, decay_theirs, decay_mine) * early + late, decay_mine * decay_theirs

    decays = []
    for t in range(part.quarter_tiles):
        state, decay = joined((1 - y) * part.quarter_tiles + t)
        send[t * STATE : (t + 1) * STATE, :] = state.astype(BF16)
        decays.append(decay)
    put_decays(send, part.quarter_tiles, decays)
    for t in range(part.quarter_tiles):
        state, decay = joined(y * part.quarter_tiles + t)
        own[t * STATE : (t + 1) * STATE, :] = state
        own_decay[t : t + 1, :] = decay


def join_pair(part, bit, carried, totals, *refs):
    state, decay, recv = refs[:3]
    refs = refs[3:]
    if carried:
        before, before_decay = refs[:2]
        refs = refs[2:]
    send = refs[0]
    refs = refs[1:]
    if totals:
        new_state, new_decay = refs[:2]
        refs = refs[2:]
    if bit >= 2:
        new_before, new_before_decay = refs[:2]
        refs = refs[2:]
    (other,) = refs
    upper = ((lax.axis_index("seq") >> bit) & 1) == 1
    received_decays(recv, part.quarter_tiles, other)
    decays = []
    for t in range(part.quarter_tiles):
        rows = slice(t * STATE, (t + 1) * STATE)
        mine, theirs = state[rows, :], recv[rows, :].astype(F32)
        d_mine, d_theirs = decay[t : t + 1, :], other[t : t + 1, :]
        early, late = jnp.where(upper, theirs, mine), jnp.where(upper, mine, theirs)
        total = jnp.where(upper, d_mine, d_theirs) * early + late
        send[rows, :] = total.astype(BF16)
        if totals:
            new_state[rows, :] = total
            new_decay[t : t + 1, :] = d_mine * d_theirs
        decays.append(d_mine * d_theirs)
        if bit >= 2:
            if carried:
                b, bd = before[rows, :], before_decay[t : t + 1, :]
                new_before[rows, :] = jnp.where(upper, b + bd * theirs, b)
                new_before_decay[t : t + 1, :] = jnp.where(upper, bd * d_theirs, bd)
            else:
                new_before[rows, :] = jnp.where(upper, theirs, 0.0)
                new_before_decay[t : t + 1, :] = jnp.where(upper, d_theirs, 1.0)
    put_decays(send, part.quarter_tiles, decays)


def to_planes(part, bit, carried, *refs):
    recv = refs[0]
    refs = refs[1:]
    if carried:
        before, before_decay = refs[:2]
        refs = refs[2:]
    own, own_decay, recv_pair, send, start, other = refs
    me = lax.axis_index("seq")
    upper = ((me >> bit) & 1) == 1
    y = ((me >> 1) & 1) == 1
    received_decays(recv_pair, part.quarter_tiles, other)
    for t in range(part.quarter_tiles):
        rows = slice(t * STATE, (t + 1) * STATE)
        theirs = recv[rows, :].astype(F32)
        if carried:
            b = before[rows, :]
            plane = jnp.where(upper, b + before_decay[t : t + 1, :] * theirs, b)
        else:
            plane = jnp.where(upper, theirs, 0.0)
        d = jnp.where(y, other[t : t + 1, :], own_decay[t : t + 1, :])
        grown = jnp.where(y, recv_pair[rows, :].astype(F32), own[rows, :])
        later = d * plane + grown
        send[rows, :] = jnp.where(y, plane, later).astype(BF16)
        start[rows, :] = jnp.where(y, later, plane)


def to_cores(part, start, recv_start, keep, keep_decay, recv, send, own, other):
    me = lax.axis_index("seq")
    first = (me & 1) == 0
    y = (me >> 1) & 1
    received_decays(recv, part.half_tiles, other)
    for side in range(2):
        for t in range(part.quarter_tiles):
            rows = slice(t * STATE, (t + 1) * STATE)
            at = (y if side == 0 else 1 - y) * part.quarter_tiles + t
            chip = start[rows, :] if side == 0 else recv_start[rows, :].astype(F32)
            d = jnp.where(first, keep_decay[pl.ds(at, 1), :], other[pl.ds(at, 1), :])
            grown = jnp.where(first, keep[tile_rows(at), :], recv[tile_rows(at), :].astype(F32))
            later = d * chip + grown
            send[tile_rows(at), :] = jnp.where(first, later, chip).astype(BF16)
            own[tile_rows(at), :] = jnp.where(first, chip, later).astype(BF16)


def inside(part, values_ref, keys_ref, reads_ref, both, both_t, carry_pair, row_pair, gate, base, slope):
    row = lax.broadcasted_iota(jnp.int32, (SPAN, SPAN), 0)
    lane = lax.broadcasted_iota(jnp.int32, (SPAN, SPAN), 1)
    causal = row >= lane
    for j in range(part.groups):
        group = part.first + j
        cols = slice(j * GROUP_COLS, (j + 1) * GROUP_COLS)
        values = values_ref[:, cols]
        writes = keys_ref[:, j * STATE : (j + 1) * STATE]
        reads = reads_ref[:, group * STATE : (group + 1) * STATE]
        scores = dot(reads, writes, ((1,), (1,)))
        found = []
        for i in range(PER_GROUP):
            h = group * PER_GROUP + i
            gap = both[:, h : h + 1] - both_t[h : h + 1, :]
            weights = scores * jnp.exp(jnp.where(causal, gap, -jnp.inf)) * both_t[HEADS + h : HEADS + h + 1, :]
            found.append(dot(weights.astype(BF16), values[:, i * HEAD_DIM : (i + 1) * HEAD_DIM]))
        within = jnp.concatenate(found, axis=1)
        to_channels = spread(group)
        skip = dot(row_pair[...], to_channels)[8:9, :]
        opened = silu(gate[:, group * GROUP_COLS : (group + 1) * GROUP_COLS].astype(F32))
        base[:, cols] = (within + skip * values.astype(F32)) * opened
        slope[:, cols] = dot(carry_pair[...], to_channels) * opened


def finish(part, mine, reads_ref, source, base, slope, gain, made):
    core = lax.axis_index("seq") & 1
    side = core if mine else 1 - core
    for j in range(part.half_groups):
        local = side * part.half_groups + j
        group = part.first + local
        cols = columns(local, GROUP_COLS)
        starts = jnp.concatenate(
            [source[(j * TILES + t) * STATE : (j * TILES + t + 1) * STATE, :] for t in range(TILES)], axis=1
        )
        gated = base[:, cols] + slope[:, cols] * dot(reads_ref[:, columns(group, STATE)], starts)
        mean = jnp.mean(gated * gated, axis=1, keepdims=True)
        normed = gated * lax.rsqrt(mean + 1e-5) * gain[:, columns(group, GROUP_COLS)]
        made[:, j * GROUP_COLS : (j + 1) * GROUP_COLS] = normed.astype(BF16)


def finish_last(part, others, *refs):
    count = len(others)
    arrays, out, made, sems = refs[:count], refs[-3], refs[-2], refs[-1]
    core = lax.axis_index("seq") & 1

    def copy_out(i, other, mine, array):
        group = other.first + (core if mine else 1 - core) * other.half_groups
        return pltpu.make_async_copy(
            array, out.at[:, pl.ds(pl.multiple_of(group * GROUP_COLS, GROUP_COLS), other.width // 2)], sems.at[i]
        )

    copies = [copy_out(i, *other, array) for i, (other, array) in enumerate(zip(others, arrays))]
    for copy in copies:
        copy.start()
    finish(part, False, *refs[count:-3], made)
    copies.append(copy_out(count, part, False, made))
    copies[-1].start()
    for copy in copies:
        copy.wait()


ORDER = "I0 P1 I1 A0 A1 R0 B0 B1 C0 C1 W0 W1 S0 S1 H0 H1 E0 F0 E1 F1"


def shards(mixer_input, gate_input, step_raw, conv_weight, conv_bias, step_bias, decay_log, skip_gain, norm_gain):
    devices = lax.axis_size("seq")
    bits = devices.bit_length() - 1
    parts = [Part(i) for i in range(len(SIZES))]

    def across(value, bit):
        return lax.ppermute(value, "seq", [(i, i ^ (1 << bit)) for i in range(devices)])

    def padded(rows):
        return pltpu.VMEM((8 + rows, 512), F32)

    def decays_of(tiles):
        return vmem(decay_rows(tiles), LANES, F32)

    def decay_scratch(tiles):
        return [pltpu.VMEM((decay_rows(tiles), LANES), F32)]

    def rows_of(p):
        return [vmem(SPAN, p.width, BF16), vmem(SPAN, p.groups * STATE, BF16)]

    def half_send(p):
        return vmem(p.half_rows + extra_rows(p.half_tiles), LANES, BF16)

    def quarter_send(p):
        return vmem(p.quarter_rows + extra_rows(p.quarter_tiles), LANES, BF16)

    def quarter(p):
        return [vmem(p.quarter_rows, LANES, F32), decays_of(p.quarter_tiles)]

    halo = lax.ppermute(mixer_input[SPAN - 3 :], "seq", [(i, i + 1) for i in range(devices - 1)])
    p = parts[0]
    held, weight, bias, raw_values, raw_keys, both, both_t, tail_pair, carry_pair, row_pair = call(
        functools.partial(prepare, p),
        [
            vmem(SPAN, CONV_COLS, BF16),
            vmem(4, CONV_COLS, BF16),
            vmem(1, CONV_COLS, F32),
            *rows_of(p),
            vmem(SPAN, 2 * HEADS, F32),
            vmem(2 * HEADS, SPAN, F32),
            vmem(SPAN, 2 * HEADS, BF16),
            vmem(SPAN, 2 * HEADS, BF16),
            vmem(16, 2 * HEADS, BF16),
        ],
        mixer_input, step_raw.T, step_bias[None, :], decay_log[None, :], skip_gain[None, :],
        conv_weight, conv_bias[None, :],
        hbm=range(7),
        cost=2.5,
        scratch=[
            padded(SPAN),
            pltpu.VMEM((HEADS, SPAN), BF16),
            pltpu.VMEM((24, HEADS), F32),
            pltpu.SemaphoreType.DMA((12,)),
        ],
    )
    gain = norm_gain[None, :]
    have = {}
    token = ()
    results = []
    for stage in ORDER.split():
        kind, p = stage[0], parts[int(stage[1:])]
        n = p.index
        get = lambda name: have[name, n]

        def put(**values):
            have.update({(name, n): value for name, value in values.items()})

        if kind == "P":
            values, keys = call(
                functools.partial(prepare_rest, p.spans), rows_of(p), held, halo, weight, bias,
                after=token, cost=0.4 * p.groups, scratch=[padded(SPAN)],
            )
            put(values=values, keys=keys)
            token = (keys,)
        elif kind == "R":
            (reads,) = call(
                functools.partial(prepare_rest, [(INNER + KEYS, KEYS)]), [vmem(SPAN, KEYS, BF16)],
                held, halo, weight, bias, after=token, cost=0.6, scratch=[padded(SPAN)],
            )
            token = (reads,)
        elif kind == "I":
            outs = [half_send(p), vmem(p.half_rows, LANES, F32), decays_of(p.half_tiles)]
            if n == 0:
                send, keep, keep_decay, values, keys = call(
                    functools.partial(increments, p), outs + rows_of(p),
                    held, halo, weight, bias, raw_values, raw_keys, tail_pair, row_pair,
                    cost=0.3 * p.groups,
                    scratch=[
                        padded(16),
                        pltpu.VMEM((16, p.width), BF16),
                        pltpu.VMEM((16, p.groups * STATE), BF16),
                    ],
                )
                put(values=values, keys=keys)
            else:
                send, keep, keep_decay = call(
                    functools.partial(increments, p), outs, get("values"), get("keys"), tail_pair, row_pair,
                    after=token, cost=0.3 * p.groups,
                )
            put(kept=(keep, keep_decay, across(send, 0)))
            token = (keep_decay,)
        elif kind == "A":
            send, own, own_decay = call(
                functools.partial(join_cores, p), [quarter_send(p), *quarter(p)], *get("kept"),
                after=token, scratch=decay_scratch(p.half_tiles),
            )
            put(own=(own, own_decay, across(send, 1)), bit=1, carried=())
            have["state", n] = have["own", n]
            token = (own_decay,)
        elif kind in "BC":
            for bit in range(1, 2) if kind == "B" else range(2, bits - 1):
                totals, carried = bit + 1 < bits - 1, get("carried")
                outs = call(
                    functools.partial(join_pair, p, bit, bool(carried), totals),
                    [quarter_send(p)] + quarter(p) * totals + quarter(p) * (bit >= 2),
                    *get("state"), *carried, after=token, scratch=decay_scratch(p.quarter_tiles),
                )
                recv = across(outs[0], bit + 1)
                put(
                    state=(*(outs[1:3] if totals else (None, None)), recv),
                    carried=tuple(outs[-2:]) if bit >= 2 else (),
                )
                token = (outs[-1],) if len(outs) > 1 else (outs[0],)
        elif kind == "S":
            send, start = call(
                functools.partial(to_planes, p, bits - 1, bool(get("carried"))),
                [vmem(p.quarter_rows, LANES, BF16), quarter(p)[0]],
                get("state")[2], *get("carried"), *get("own"),
                after=token, scratch=decay_scratch(p.quarter_tiles),
            )
            put(start=(start, across(send, 1)))
            token = (start,)
        elif kind == "H":
            send, own_start = call(
                functools.partial(to_cores, p), [vmem(p.half_rows, LANES, BF16)] * 2, *get("start"), *get("kept"),
                after=token, scratch=decay_scratch(p.half_tiles),
            )
            put(own_start=own_start, recv_start=across(send, 0))
            token = (own_start,)
        elif kind == "W":
            put(
                mixed=call(
                    functools.partial(inside, p), [vmem(SPAN, p.width, F32)] * 2,
                    get("values"), get("keys"), reads, both, both_t, carry_pair, row_pair, gate_input,
                    after=token, cost=0.42 * p.groups,
                )
            )
            token = (get("mixed")[0],)
        elif kind in "EF" and len(results) < 2 * len(SIZES) - 1:
            name = "own_start" if kind == "E" else "recv_start"
            (made,) = call(
                functools.partial(finish, p, kind == "E"), [vmem(SPAN, p.width // 2, BF16)],
                reads, get(name), *get("mixed"), gain, after=token, cost=0.2 * p.half_groups,
            )
            results.append(((p, kind == "E"), made))
            token = (made,)
        else:
            (out,) = call(
                functools.partial(finish_last, p, [where for where, _ in results]),
                [((SPAN, INNER), BF16, pltpu.HBM)],
                *[made for _, made in results], reads, get("recv_start"), *get("mixed"), gain,
                after=token, cost=0.2 * p.half_groups,
                scratch=[pltpu.VMEM((SPAN, p.width // 2), BF16), pltpu.SemaphoreType.DMA((2 * len(SIZES),))],
            )
    return out


def solution(mesh):
    in_specs = (
        P(("groups", "seq"), None),
        P(("groups", "seq"), None),
        P(("groups", "seq"), None),
        P(),
        P(),
        P("groups"),
        P("groups"),
        P(),
        P(),
    )
    return jax.shard_map(
        shards, mesh=mesh, in_specs=in_specs, out_specs=P(("groups", "seq"), None), check_vma=False
    )
```

time: 51.2 us -> 48.9 us (0.955)
  Pallas kernels: 16.3 us -> 14.2 us
  waiting for transfers between devices: 14.2 us -> 13.6 us
    pallas_call x20 -> x21, Pallas kernels: 16.3 us -> 14.2 us  [call(): pl.pallas_call(kernel, out_shape=[space(shape, kind) for shape, kind, spa...]
    ppermute x12, waiting for transfers between devices: 14.2 us -> 13.6 us  [across(): lax.ppermute(value, 'seq', [(i, i ^ 1 << bit) for i in range(devices)])]
  transfers between devices with their start and end apart: 13 -> 13, of which waited for: 5 -> 8; matrix products, arithmetic and copies ran while one was open for 0% -> 0% of each run, Pallas kernels for 25% -> 24%
where the time goes in v3:
time: 48.9 us; the launch traced here: 48.7 us
  starting transfers between devices  19.8 us (40%)
  Pallas kernels  14.2 us (29%)
  waiting for transfers between devices  13.6 us (28%)
  local copies, waits for them, and re-layouts  0.93 us (2%)
    ppermute x12, starting transfers between devices, across(): lax.ppermute(value, 'seq', [(i, i ^ 1 << bit) for i in range(devices)])  17.4 us
    pallas_call x21, Pallas kernels, call(): pl.pallas_call(kernel, out_shape=[space(shape, kind) for shape, kind, spa...  14.2 us
    ppermute x12, waiting for transfers between devices, across(): lax.ppermute(value, 'seq', [(i, i ^ 1 << bit) for i in range(devices)])  13.6 us
    ppermute x1, starting transfers between devices, shards(): lax.ppermute(mixer_input[SPAN - 3:], 'seq', [(i, i + 1) for i in range(de...  2.36 us
  transfers between devices with their start and end apart: 13, of which 8 were waited for; matrix products, arithmetic and copies ran while one was open for 0% of the time, Pallas kernels for 24%

profile of v3, /device:TPU:0, one launch (start us, length us, event | category | flops | bytes accessed | tf_op | source)
XLA Modules:
  0.0 48.7 jit_solution(5037309686498226802)
XLA Ops:
  0.0 0.9 %slice.3 = bf16[3,6144]{1,0:T(4,128)(2,1)S(1)} slice(bf16[128,6144]{1,0:T(8,128)(2,1)} %refs_0_.1), slice={[125:128], [0:6144]} | slice | bytes 73728 | tf_op jit(solution)/shard_map/slice | solution.py:449
  0.9 2.4 %collective-permute-start = (bf16[3,6144]{1,0:T(4,128)(2,1)S(1)}, bf16[3,6144]{1,0:T(4,128)(2,1)S(1)}, u32[]{:S(2)}, u32[]{:S(2)}) collective-permute-start(bf16[3,6144]{1,0:T(4,128)(2,1)S(1)} %slice.3), channel_id=1, source_target_pairs={{0,1},{1,2},{2,3},{3,4},{4,5},{5,6},{6,7},{7,8},{8,9},{9,10},{10,1... | collective-permute-start | bytes 110600 | tf_op jit(solution)/shard_map/ppermute | solution.py:449
  3.3 2.8 %shard_map.91 = (bf16[128,6144]{1,0:T(8,128)(2,1)S(1)}, bf16[4,6144]{1,0:T(4,128)(2,1)S(1)}, f32[1,6144]{1,0:T(1,128)S(1)}, bf16[128,2048]{1,0:T(8,128)(2,1)S(1)...) custom-call(bf16[128,6144]{1,0:T(8,128)(2,1)} %refs_0_.1, ...), custom_call_target="tpu_custom_call" | custom-call | flops 2500000000 | bytes 7500000 | tf_op jit(solution)/shard_map/pallas_call | solution.py:65
  6.1 0.0 collective-permute-done.refs_1_
  6.2 1.5 %shard_map.92 = (bf16[1040,128]{1,0:T(8,128)(2,1)S(1)}, f32[1024,128]{1,0:T(8,128)S(1)}, f32[8,128]{1,0:T(8,128)S(1)}, bf16[128,2048]{1,0:T(8,128)(2,1)S(1)}, bf16[128,512]{1,0:T(8,128)(2,1)S(1)}) custom-call(bf16[128,6144]{1,0:T(8,128)(2,1)S(1)} %get-tuple-element.55.refs_0_, bf16[3,6144]{1,0:T(4,128)(2,1)S(1)} %collective-permute-done.refs_1_, ...), custom_call_target="tpu_custom_call" | custom-call | flops 1200000000 | bytes 3600000 | tf_op jit(solution)/shard_map/pallas_call | solution.py:65
  7.6 2.7 %collective-permute-start.2 = (bf16[1040,128]{1,0:T(8,128)(2,1)S(1)}, bf16[1040,128]{1,0:T(8,128)(2,1)S(1)}, u32[]{:S(2)}, u32[]{:S(2)}) collective-permute-start(bf16[1040,128]{1,0:T(8,128)(2,1)S(1)} %get-tuple-element.69), channel_id=1, source_target_pairs={{0,1},{1,0},{2,3},{3,2},{4,5},{5,4},{6,7},{7,6},{8,9},{9,8},{10,11... | collective-permute-start | bytes 798728 | tf_op jit(solution)/shard_map/ppermute | solution.py:426
  10.3 1.6 %shard_map.93 = (bf16[128,2048]{1,0:T(8,128)(2,1)S(1)}, bf16[128,512]{1,0:T(8,128)(2,1)S(1)}) custom-call(bf16[128,6144]{1,0:T(8,128)(2,1)S(1)} %get-tuple-element.55.refs_0_, bf16[3,6144]{1,0:T(4,128)(2,1)S(1)} %collective-permute-done.refs_1_, bf16[4,6144]{1,0:T(4,128)(2,1)S(1)} %get-tuple-element.56.refs_2_, f32[1,6144]{1,0:T(1,128)S(1)} %get-tuple-element.57.refs_3_, ...), custom_call_target="tpu_custom_call" | custom-call | flops 1600000000 | bytes 4800000 | tf_op jit(solution)/shard_map/pallas_call | solution.py:65
  11.9 1.2 %shard_map.94 = (bf16[1040,128]{1,0:T(8,128)(2,1)S(1)}, f32[1024,128]{1,0:T(8,128)S(1)}, f32[8,128]{1,0:T(8,128)S(1)}) custom-call(bf16[128,2048]{1,0:T(8,128)(2,1)S(1)} %get-tuple-element.63.refs_0_, bf16[128,512]{1,0:T(8,128)(2,1)S(1)} %get-tuple-element.64.refs_1_.refs_4_, bf16[128,128]{1,0:T(8,128)(2,1)S(1)} %get-tuple-element.60.refs_6_.refs_2_, ...), custom_call_target="tpu_custom_call" | custom-call | flops 1200000000 | bytes 3600000 | tf_op jit(solution)/shard_map/pallas_call | solution.py:65
  13.1 0.1 collective-permute-start.1
  13.2 0.0 collective-permute-done.2.refs_2_.refs_4_
  13.2 0.1 shard_map.95
  13.3 1.6 %collective-permute-start.3 = (bf16[528,128]{1,0:T(8,128)(2,1)S(1)}, bf16[528,128]{1,0:T(8,128)(2,1)S(1)}, u32[]{:S(2)}, u32[]{:S(2)}) collective-permute-start(bf16[528,128]{1,0:T(8,128)(2,1)S(1)} %get-tuple-element.73), channel_id=1, source_target_pairs={{0,2},{1,3},{2,0},{3,1},{4,6},{5,7},{6,4},{7,5},{8,10},{9,11},{10,... | collective-permute-start | bytes 405512 | tf_op jit(solution)/shard_map/ppermute | solution.py:426
  14.9 0.0 collective-permute-done.1.refs_2_.refs_4_
  14.9 0.1 shard_map.96
  15.0 1.4 %collective-permute-start.5 = (bf16[528,128]{1,0:T(8,128)(2,1)S(1)}, bf16[528,128]{1,0:T(8,128)(2,1)S(1)}, u32[]{:S(2)}, u32[]{:S(2)}) collective-permute-start(bf16[528,128]{1,0:T(8,128)(2,1)S(1)} %get-tuple-element.78), channel_id=1, source_target_pairs={{0,2},{1,3},{2,0},{3,1},{4,6},{5,7},{6,4},{7,5},{8,10},{9,11},{10,... | collective-permute-start | bytes 405512 | tf_op jit(solution)/shard_map/ppermute | solution.py:426
  16.4 0.0 copy-start.1
  16.4 0.6 %shard_map.97.refs_3_.refs_2_.refs_0_ = bf16[128,1024]{1,0:T(8,128)(2,1)S(1)} custom-call(bf16[128,6144]{1,0:T(8,128)(2,1)S(1)} %get-tuple-element.55.refs_0_, bf16[3,6144]{1,0:T(4,128)(2,1)S(1)} %collective-permute-done.refs_1_, bf16[4,6144]{1,0:T(4,128)(2,1)S(1)} %get-tuple-element.56.refs_2_, f32[1,6144]{1,0:T(1,128)S(1)} %get-tuple-element.57.refs_3_, ...), custom_call_target="tpu_custom_call" | custom-call | flops 600000000 | bytes 1800000 | tf_op jit(solution)/shard_map/pallas_call | solution.py:65
  17.0 2.7 %collective-permute-done.3.refs_2_.refs_5_ = bf16[528,128]{1,0:T(8,128)(2,1)S(1)} collective-permute-done((bf16[528,128]{1,0:T(8,128)(2,1)S(1)}, bf16[528,128]{1,0:T(8,128)(2,1)S(1)}, u32[]{:S(2)}, u32[]{:S(2)}) %collective-permute-start.3) | collective-permute-done | bytes 135200 | tf_op jit(solution)/shard_map/ppermute | solution.py:426
  19.8 0.1 shard_map.98
  19.8 2.1 %collective-permute-start.4 = (bf16[528,128]{1,0:T(8,128)(2,1)S(1)}, bf16[528,128]{1,0:T(8,128)(2,1)S(1)}, u32[]{:S(2)}, u32[]{:S(2)}) collective-permute-start(bf16[528,128]{1,0:T(8,128)(2,1)S(1)} %get-tuple-element.76), channel_id=1, source_target_pairs={{0,4},{1,5},{2,6},{3,7},{4,0},{5,1},{6,2},{7,3},{8,12},{9,13},{10,... | collective-permute-start | bytes 405512 | tf_op jit(solution)/shard_map/ppermute | solution.py:426
  21.9 0.3 collective-permute-done.5.refs_2_.refs_5_
  22.2 0.1 shard_map.99
  22.3 1.6 %collective-permute-start.7 = (bf16[528,128]{1,0:T(8,128)(2,1)S(1)}, bf16[528,128]{1,0:T(8,128)(2,1)S(1)}, u32[]{:S(2)}, u32[]{:S(2)}) collective-permute-start(bf16[528,128]{1,0:T(8,128)(2,1)S(1)} %get-tuple-element.89), channel_id=1, source_target_pairs={{0,4},{1,5},{2,6},{3,7},{4,0},{5,1},{6,2},{7,3},{8,12},{9,13},{10,... | collective-permute-start | bytes 405512 | tf_op jit(solution)/shard_map/ppermute | solution.py:426
  24.0 1.6 %collective-permute-done.4.refs_2_ = bf16[528,128]{1,0:T(8,128)(2,1)S(1)} collective-permute-done((bf16[528,128]{1,0:T(8,128)(2,1)S(1)}, bf16[528,128]{1,0:T(8,128)(2,1)S(1)}, u32[]{:S(2)}, u32[]{:S(2)}) %collective-permute-start.4) | collective-permute-done | bytes 135200 | tf_op jit(solution)/shard_map/ppermute | solution.py:426
  25.6 0.1 shard_map.100
  25.7 3.6 %collective-permute-start.6 = (bf16[528,128]{1,0:T(8,128)(2,1)S(1)}, bf16[528,128]{1,0:T(8,128)(2,1)S(1)}, u32[]{:S(2)}, u32[]{:S(2)}) collective-permute-start(bf16[528,128]{1,0:T(8,128)(2,1)S(1)} %get-tuple-element.80), channel_id=1, source_target_pairs={{0,8},{1,9},{2,10},{3,11},{4,12},{5,13},{6,14},{7,15},{8,0},{9,1},... | collective-permute-start | bytes 405512 | tf_op jit(solution)/shard_map/ppermute | solution.py:426
  29.2 0.0 collective-permute-done.7.refs_2_
  29.3 0.1 shard_map.101
  29.3 2.8 %collective-permute-start.9 = (bf16[528,128]{1,0:T(8,128)(2,1)S(1)}, bf16[528,128]{1,0:T(8,128)(2,1)S(1)}, u32[]{:S(2)}, u32[]{:S(2)}) collective-permute-start(bf16[528,128]{1,0:T(8,128)(2,1)S(1)} %get-tuple-element.95), channel_id=1, source_target_pairs={{0,8},{1,9},{2,10},{3,11},{4,12},{5,13},{6,14},{7,15},{8,0},{9,1},... | collective-permute-start | bytes 405512 | tf_op jit(solution)/shard_map/ppermute | solution.py:426
  32.1 0.0 copy-done.1
  32.1 1.6 %shard_map.102 = (f32[128,2048]{1,0:T(8,128)S(1)}, f32[128,2048]{1,0:T(8,128)S(1)}) custom-call(bf16[128,2048]{1,0:T(8,128)(2,1)S(1)} %get-tuple-element.86.refs_0_, bf16[128,512]{1,0:T(8,128)(2,1)S(1)} %get-tuple-element.87.refs_1_, bf16[128,1024]{1,0:T(8,128)(2,1)S(1)} %shard_map.97.refs_3_.refs_2_.refs_0_, f32[128,128]{1,0:T(8,128)S(1)} %get-tuple-element.83.refs_3_, ...), custom_call_target="tpu_custom_call" | custom-call | flops 1680000000 | bytes 5040000 | tf_op jit(solution)/shard_map/pallas_call | solution.py:65
  33.8 1.7 %shard_map.103 = (f32[128,2048]{1,0:T(8,128)S(1)}, f32[128,2048]{1,0:T(8,128)S(1)}) custom-call(bf16[128,2048]{1,0:T(8,128)(2,1)S(1)} %get-tuple-element.63.refs_0_, bf16[128,512]{1,0:T(8,128)(2,1)S(1)} %get-tuple-element.64.refs_1_.refs_4_, bf16[128,1024]{1,0:T(8,128)(2,1)S(1)} %shard_map.97.refs_3_.refs_2_.refs_0_, ...), custom_call_target="tpu_custom_call" | custom-call | flops 1680000000 | bytes 5040000 | tf_op jit(solution)/shard_map/pallas_call | solution.py:65
  35.5 3.1 %collective-permute-done.6.refs_0_ = bf16[528,128]{1,0:T(8,128)(2,1)S(1)} collective-permute-done((bf16[528,128]{1,0:T(8,128)(2,1)S(1)}, bf16[528,128]{1,0:T(8,128)(2,1)S(1)}, u32[]{:S(2)}, u32[]{:S(2)}) %collective-permute-start.6) | collective-permute-done | bytes 135200 | tf_op jit(solution)/shard_map/ppermute | solution.py:426
  38.6 0.1 shard_map.104
  38.7 0.6 %collective-permute-start.8 = (bf16[512,128]{1,0:T(8,128)(2,1)S(1)}, bf16[512,128]{1,0:T(8,128)(2,1)S(1)}, u32[]{:S(2)}, u32[]{:S(2)}) collective-permute-start(bf16[512,128]{1,0:T(8,128)(2,1)S(1)} %get-tuple-element.94), channel_id=1, source_target_pairs={{0,2},{1,3},{2,0},{3,1},{4,6},{5,7},{6,4},{7,5},{8,10},{9,11},{10,... | collective-permute-start | bytes 393224 | tf_op jit(solution)/shard_map/ppermute | solution.py:426
  39.3 0.8 %collective-permute-done.9.refs_0_ = bf16[528,128]{1,0:T(8,128)(2,1)S(1)} collective-permute-done((bf16[528,128]{1,0:T(8,128)(2,1)S(1)}, bf16[528,128]{1,0:T(8,128)(2,1)S(1)}, u32[]{:S(2)}, u32[]{:S(2)}) %collective-permute-start.9) | collective-permute-done | bytes 135200 | tf_op jit(solution)/shard_map/ppermute | solution.py:426
  40.1 0.1 shard_map.105
  40.2 0.0 copy-start
  40.2 0.9 %collective-permute-start.10 = (bf16[512,128]{1,0:T(8,128)(2,1)S(1)}, bf16[512,128]{1,0:T(8,128)(2,1)S(1)}, u32[]{:S(2)}, u32[]{:S(2)}) collective-permute-start(bf16[512,128]{1,0:T(8,128)(2,1)S(1)} %get-tuple-element.100), channel_id=1, source_target_pairs={{0,2},{1,3},{2,0},{3,1},{4,6},{5,7},{6,4},{7,5},{8,10},{9,11},{10,... | collective-permute-start | bytes 393224 | tf_op jit(solution)/shard_map/ppermute | solution.py:426
  41.1 3.2 %collective-permute-done.8.refs_1_ = bf16[512,128]{1,0:T(8,128)(2,1)S(1)} collective-permute-done((bf16[512,128]{1,0:T(8,128)(2,1)S(1)}, bf16[512,128]{1,0:T(8,128)(2,1)S(1)}, u32[]{:S(2)}, u32[]{:S(2)}) %collective-permute-start.8) | collective-permute-done | bytes 131104 | tf_op jit(solution)/shard_map/ppermute | solution.py:426
  44.3 0.2 shard_map.106
  44.5 0.1 collective-permute-start.11
  44.6 1.2 %collective-permute-done.10.refs_1_ = bf16[512,128]{1,0:T(8,128)(2,1)S(1)} collective-permute-done((bf16[512,128]{1,0:T(8,128)(2,1)S(1)}, bf16[512,128]{1,0:T(8,128)(2,1)S(1)}, u32[]{:S(2)}, u32[]{:S(2)}) %collective-permute-start.10) | collective-permute-done | bytes 131104 | tf_op jit(solution)/shard_map/ppermute | solution.py:426
  45.7 0.2 shard_map.107
  45.9 0.1 collective-permute-start.12
  46.0 0.0 copy-done
  46.0 0.3 shard_map.108.refs_5_.refs_0_
  46.3 0.0 collective-permute-done.11.refs_1_
  46.3 0.3 shard_map.109.refs_5_.refs_1_
  46.6 0.3 shard_map.110.refs_2_.refs_8_
  47.0 0.5 %collective-permute-done.12.refs_4_ = bf16[1024,128]{1,0:T(8,128)(2,1)S(1)} collective-permute-done((bf16[1024,128]{1,0:T(8,128)(2,1)S(1)}, bf16[1024,128]{1,0:T(8,128)(2,1)S(1)}, u32[]{:S(2)}, u32[]{:S(2)}) %collective-permute-start.12) | collective-permute-done | bytes 262176 | tf_op jit(solution)/shard_map/ppermute | solution.py:426
  47.5 1.2 %shard_map.111 = bf16[128,4096]{1,0:T(8,128)(2,1)} custom-call(bf16[128,1024]{1,0:T(8,128)(2,1)S(1)} %shard_map.108.refs_5_.refs_0_, bf16[128,1024]{1,0:T(8,128)(2,1)S(1)} %shard_map.109.refs_5_.refs_1_, bf16[128,1024]{1,0:T(8,128)(2,1)S(1)} %shard_map.110.refs_2_.refs_8_, bf16[128,1024]{1,0:T(8,128)(2,1)S(1)} %shard_map.97.refs_3_.refs_2_.refs_0_, ...), custom_call_target="tpu_custom_call" | custom-call | flops 400000000 | bytes 1200000 | tf_op jit(solution)/shard_map/pallas_call | solution.py:65
Async XLA Ops:
  0.9 5.2 %collective-permute-start = (bf16[3,6144]{1,0:T(4,128)(2,1)S(1)}, bf16[3,6144]{1,0:T(4,128)(2,1)S(1)}, u32[]{:S(2)}, u32[]{:S(2)}) collective-permute-start(bf16[3,6144]{1,0:T(4,128)(2,1)S(1)} %slice.3), channel_id=1, source_target_pairs={{0,1},{1,2},{2,3},{3,4},{4,5},{5,6},{6,7},{7,8},{8,9},{9,10},{10,1... | collective-permute-start | bytes 110600 | tf_op jit(solution)/shard_map/ppermute | solution.py:449
  7.6 5.6 %collective-permute-start.2 = (bf16[1040,128]{1,0:T(8,128)(2,1)S(1)}, bf16[1040,128]{1,0:T(8,128)(2,1)S(1)}, u32[]{:S(2)}, u32[]{:S(2)}) collective-permute-start(bf16[1040,128]{1,0:T(8,128)(2,1)S(1)} %get-tuple-element.69), channel_id=1, source_target_pairs={{0,1},{1,0},{2,3},{3,2},{4,5},{5,4},{6,7},{7,6},{8,9},{9,8},{10,11... | collective-permute-start | bytes 798728 | tf_op jit(solution)/shard_map/ppermute | solution.py:426
  13.1 1.8 %collective-permute-start.1 = (bf16[1040,128]{1,0:T(8,128)(2,1)S(1)}, bf16[1040,128]{1,0:T(8,128)(2,1)S(1)}, u32[]{:S(2)}, u32[]{:S(2)}) collective-permute-start(bf16[1040,128]{1,0:T(8,128)(2,1)S(1)} %get-tuple-element.67), channel_id=1, source_target_pairs={{0,1},{1,0},{2,3},{3,2},{4,5},{5,4},{6,7},{7,6},{8,9},{9,8},{10,11... | collective-permute-start | bytes 798728 | tf_op jit(solution)/shard_map/ppermute | solution.py:426
  13.3 6.5 %collective-permute-start.3 = (bf16[528,128]{1,0:T(8,128)(2,1)S(1)}, bf16[528,128]{1,0:T(8,128)(2,1)S(1)}, u32[]{:S(2)}, u32[]{:S(2)}) collective-permute-start(bf16[528,128]{1,0:T(8,128)(2,1)S(1)} %get-tuple-element.73), channel_id=1, source_target_pairs={{0,2},{1,3},{2,0},{3,1},{4,6},{5,7},{6,4},{7,5},{8,10},{9,11},{10,... | collective-permute-start | bytes 405512 | tf_op jit(solution)/shard_map/ppermute | solution.py:426
  15.0 7.2 %collective-permute-start.5 = (bf16[528,128]{1,0:T(8,128)(2,1)S(1)}, bf16[528,128]{1,0:T(8,128)(2,1)S(1)}, u32[]{:S(2)}, u32[]{:S(2)}) collective-permute-start(bf16[528,128]{1,0:T(8,128)(2,1)S(1)} %get-tuple-element.78), channel_id=1, source_target_pairs={{0,2},{1,3},{2,0},{3,1},{4,6},{5,7},{6,4},{7,5},{8,10},{9,11},{10,... | collective-permute-start | bytes 405512 | tf_op jit(solution)/shard_map/ppermute | solution.py:426
  16.4 15.7 %copy-start.1 = (bf16[128,4096]{1,0:T(8,128)(2,1)S(1)}, bf16[128,4096]{1,0:T(8,128)(2,1)}, u32[]{:S(2)}) copy-start(bf16[128,4096]{1,0:T(8,128)(2,1)} %refs_7_.3) | copy-start | bytes 3145732
  19.8 5.8 %collective-permute-start.4 = (bf16[528,128]{1,0:T(8,128)(2,1)S(1)}, bf16[528,128]{1,0:T(8,128)(2,1)S(1)}, u32[]{:S(2)}, u32[]{:S(2)}) collective-permute-start(bf16[528,128]{1,0:T(8,128)(2,1)S(1)} %get-tuple-element.76), channel_id=1, source_target_pairs={{0,4},{1,5},{2,6},{3,7},{4,0},{5,1},{6,2},{7,3},{8,12},{9,13},{10,... | collective-permute-start | bytes 405512 | tf_op jit(solution)/shard_map/ppermute | solution.py:426
  22.3 6.9 %collective-permute-start.7 = (bf16[528,128]{1,0:T(8,128)(2,1)S(1)}, bf16[528,128]{1,0:T(8,128)(2,1)S(1)}, u32[]{:S(2)}, u32[]{:S(2)}) collective-permute-start(bf16[528,128]{1,0:T(8,128)(2,1)S(1)} %get-tuple-element.89), channel_id=1, source_target_pairs={{0,4},{1,5},{2,6},{3,7},{4,0},{5,1},{6,2},{7,3},{8,12},{9,13},{10,... | collective-permute-start | bytes 405512 | tf_op jit(solution)/shard_map/ppermute | solution.py:426
  25.7 12.9 %collective-permute-start.6 = (bf16[528,128]{1,0:T(8,128)(2,1)S(1)}, bf16[528,128]{1,0:T(8,128)(2,1)S(1)}, u32[]{:S(2)}, u32[]{:S(2)}) collective-permute-start(bf16[528,128]{1,0:T(8,128)(2,1)S(1)} %get-tuple-element.80), channel_id=1, source_target_pairs={{0,8},{1,9},{2,10},{3,11},{4,12},{5,13},{6,14},{7,15},{8,0},{9,1},... | collective-permute-start | bytes 405512 | tf_op jit(solution)/shard_map/ppermute | solution.py:426
  29.3 10.7 %collective-permute-start.9 = (bf16[528,128]{1,0:T(8,128)(2,1)S(1)}, bf16[528,128]{1,0:T(8,128)(2,1)S(1)}, u32[]{:S(2)}, u32[]{:S(2)}) collective-permute-start(bf16[528,128]{1,0:T(8,128)(2,1)S(1)} %get-tuple-element.95), channel_id=1, source_target_pairs={{0,8},{1,9},{2,10},{3,11},{4,12},{5,13},{6,14},{7,15},{8,0},{9,1},... | collective-permute-start | bytes 405512 | tf_op jit(solution)/shard_map/ppermute | solution.py:426
  38.7 5.6 %collective-permute-start.8 = (bf16[512,128]{1,0:T(8,128)(2,1)S(1)}, bf16[512,128]{1,0:T(8,128)(2,1)S(1)}, u32[]{:S(2)}, u32[]{:S(2)}) collective-permute-start(bf16[512,128]{1,0:T(8,128)(2,1)S(1)} %get-tuple-element.94), channel_id=1, source_target_pairs={{0,2},{1,3},{2,0},{3,1},{4,6},{5,7},{6,4},{7,5},{8,10},{9,11},{10,... | collective-permute-start | bytes 393224 | tf_op jit(solution)/shard_map/ppermute | solution.py:426
  40.2 5.8 %copy-start = (f32[4096]{0:T(1024)S(1)}, f32[4096]{0:T(1024)}, u32[]{:S(2)}) copy-start(f32[4096]{0:T(1024)} %param.17) | copy-start | bytes 49156
  40.2 5.5 %collective-permute-start.10 = (bf16[512,128]{1,0:T(8,128)(2,1)S(1)}, bf16[512,128]{1,0:T(8,128)(2,1)S(1)}, u32[]{:S(2)}, u32[]{:S(2)}) collective-permute-start(bf16[512,128]{1,0:T(8,128)(2,1)S(1)} %get-tuple-element.100), channel_id=1, source_target_pairs={{0,2},{1,3},{2,0},{3,1},{4,6},{5,7},{6,4},{7,5},{8,10},{9,11},{10,... | collective-permute-start | bytes 393224 | tf_op jit(solution)/shard_map/ppermute | solution.py:426
  44.5 1.8 %collective-permute-start.11 = (bf16[1024,128]{1,0:T(8,128)(2,1)S(1)}, bf16[1024,128]{1,0:T(8,128)(2,1)S(1)}, u32[]{:S(2)}, u32[]{:S(2)}) collective-permute-start(bf16[1024,128]{1,0:T(8,128)(2,1)S(1)} %get-tuple-element.102), channel_id=1, source_target_pairs={{0,1},{1,0},{2,3},{3,2},{4,5},{5,4},{6,7},{7,6},{8,9},{9,8},{10,11... | collective-permute-start | bytes 786440 | tf_op jit(solution)/shard_map/ppermute | solution.py:426
  45.9 1.6 %collective-permute-start.12 = (bf16[1024,128]{1,0:T(8,128)(2,1)S(1)}, bf16[1024,128]{1,0:T(8,128)(2,1)S(1)}, u32[]{:S(2)}, u32[]{:S(2)}) collective-permute-start(bf16[1024,128]{1,0:T(8,128)(2,1)S(1)} %get-tuple-element.104), channel_id=1, source_target_pairs={{0,1},{1,0},{2,3},{3,2},{4,5},{5,4},{6,7},{7,6},{8,9},{9,8},{10,11... | collective-permute-start | bytes 786440 | tf_op jit(solution)/shard_map/ppermute | solution.py:426

commit v4 on v3

--- a/solution.py
+++ b/solution.py
@@ -82,8 +82,7 @@
 
 
 def silu(v):
-    half = 0.5 * v
-    return half + half * jnp.tanh(half)
+    return silu_of_twice(0.5 * v)
 
 
 def pieces(v, count):
@@ -95,22 +94,23 @@
     return found
 
 
-def spread(group):
-    row = lax.broadcasted_iota(jnp.int32, (2 * HEADS, GROUP_COLS), 0)
-    lane = lax.broadcasted_iota(jnp.int32, (2 * HEADS, GROUP_COLS), 1)
-    head = group * PER_GROUP + lane // HEAD_DIM
-    return ((row == head) | (row == head + HEADS)).astype(BF16)
-
-
 def columns(group, width, start=0):
     return pl.ds(pl.multiple_of(start + group * width, LANES), width)
 
 
-def convolve_into(rows, padded, weight_ref, bias_ref, cols):
-    total = bias_ref[:, cols]
+def silu_of_twice(half):
+    return half + half * jnp.tanh(half)
+
+
+def halved_taps(weight, bias, cols):
+    return 0.5 * weight[:, cols].astype(F32), 0.5 * bias[:, cols]
+
+
+def convolve_into(rows, padded, weight, bias, cols):
+    taps, total = halved_taps(weight, bias, cols)
     for tap in range(4):
-        total = total + weight_ref[tap : tap + 1, cols].astype(F32) * padded[5 + tap : 5 + tap + rows, :]
-    return silu(total).astype(BF16)
+        total = total + taps[tap : tap + 1] * padded[5 + tap : 5 + tap + rows, :]
+    return silu_of_twice(total).astype(BF16)
 
 
 def accurate_log1p(u):
@@ -118,9 +118,23 @@
     return jnp.where(w == 1.0, u, jnp.log(w) * (u / jnp.where(w == 1.0, 1.0, w - 1.0)))
 
 
-def convolve_part(source, halo, weight, bias, padded, spans, outs, rows=SPAN):
+def convolve_body(source, weight, bias, spans, outs):
     for (start, width), out in zip(spans, outs):
-
+        block = min(width, 256)
+
+        @pl.loop(0, width // block)
+        def _(i, start=start, out=out, block=block):
+            cols = columns(i, block, start)
+            here = source[:, cols].astype(F32)
+            taps, total = halved_taps(weight, bias, cols)
+            total = total + taps[3:4] * here
+            for back in range(1, 4):
+                total = total + taps[3 - back : 4 - back] * pltpu.roll(here, back, 0)
+            out[:, columns(i, block)] = silu_of_twice(total).astype(BF16)
+
+
+def convolve_head(source, halo, weight, bias, padded, spans, outs):
+    for (start, width), out in zip(spans, outs):
         block = min(width, 512)
 
         @pl.loop(0, width // block)
@@ -128,16 +142,15 @@
             cols = columns(i, block, start)
             here = padded.at[:, 0:block]
             here[0:8, :] = jnp.zeros((8, block), F32)
-            if halo is not None:
-                here[5:8, :] = halo[:, cols].astype(F32)
-            here[8 : 8 + rows, :] = source[0:rows, cols].astype(F32)
-            out[0:rows, columns(i, block)] = convolve_into(rows, here, weight, bias, cols)
+            here[5:8, :] = halo[:, cols].astype(F32)
+            here[8:24, :] = source[0:16, cols].astype(F32)
+            out[0:16, columns(i, block)] = convolve_into(16, here, weight, bias, cols)
 
 
 def prepare(
     part, x, raw_t, step_bias, decay_log, skip, weight_in, bias_in,
-    held, weight, bias, values, keys, both, both_t, tail_pair, carry_pair, row_pair,
-    padded, raw_here, small, sems,
+    held, weight, bias, values, keys, both, both_t, tail_pair, carry_pair, row_pair, spread,
+    raw_here, small, sems,
 ):
     first = part.spans
     pieces_of_x = list(first)
@@ -159,6 +172,10 @@
         copies.append(pltpu.make_async_copy(x.at[:, cols], held.at[:, cols], sems.at[6 + i]))
     for copy in copies:
         copy.start()
+    channel = lax.broadcasted_iota(jnp.int32, (2 * HEADS, GROUP_COLS), 1)
+    head = (lax.broadcasted_iota(jnp.int32, (2 * HEADS, GROUP_COLS), 0) & (HEADS - 1)) - channel // HEAD_DIM
+    for group in range(GROUPS):
+        spread[:, group * GROUP_COLS : (group + 1) * GROUP_COLS] = (head == group * PER_GROUP).astype(BF16)
     for copy in copies[:4]:
         copy.wait()
     raw = raw_here[...].astype(F32)
@@ -182,13 +199,14 @@
     row_pair[...] = jnp.concatenate(pieces(rows, 2), axis=1)
     for copy in copies[4:8]:
         copy.wait()
-    convolve_part(held, None, weight, bias, padded, first, (values, keys))
+    convolve_body(held, weight, bias, first, (values, keys))
     for copy in copies[8:]:
         copy.wait()
 
 
 def prepare_rest(spans, held, halo, weight, bias, *refs):
-    convolve_part(held, halo, weight, bias, refs[-1], spans, refs[:-1])
+    convolve_body(held, weight, bias, spans, refs[:-1])
+    convolve_head(held, halo, weight, bias, refs[-1], spans, refs[:-1])
 
 
 def put_decays(send, tiles, decays):
@@ -201,39 +219,43 @@
 
 
 def increments(part, *refs):
-    first = part.index == 0
-    if first:
+    if part.index == 0:
         held, halo, weight, bias, raw_values, raw_keys = refs[:6]
-        tail_pair, row_pair, send, keep, keep_decay, values_ref, keys_ref, padded, value_fix, key_fix = refs[6:]
-        convolve_part(held, halo, weight, bias, padded, part.spans, (value_fix, key_fix), 16)
+        tail_pair, row_pair, spread, send, keep, keep_decay, values_ref, keys_ref = refs[6:14]
+        scaled, padded, value_fix, key_fix = refs[14:]
+        convolve_head(held, halo, weight, bias, padded, part.spans, (value_fix, key_fix))
+        keys_ref[0:16, :] = key_fix[...]
+        keys_ref[16:, :] = raw_keys[16:, :]
     else:
-        values_ref, keys_ref, tail_pair, row_pair, send, keep, keep_decay = refs
+        values_ref, keys_ref, tail_pair, row_pair, spread, send, keep, keep_decay, scaled = refs
     core = lax.axis_index("seq") & 1
-    for target, side in ((send, 1 - core), (keep, core)):
-        decays = []
-        for j in range(part.half_groups):
-            local = side * part.half_groups + j
-            value_cols, key_cols = columns(local, GROUP_COLS), columns(local, STATE)
-            to_channels = spread(part.first + local)
-            scale = dot(tail_pair[...], to_channels)
-            if first:
-                values = jnp.concatenate([value_fix[:, value_cols], raw_values[16:, value_cols]], axis=0)
-                keys = jnp.concatenate([key_fix[:, key_cols], raw_keys[16:, key_cols]], axis=0)
-                values_ref[:, value_cols] = values
-                keys_ref[:, key_cols] = keys
-            else:
-                values, keys = values_ref[:, value_cols], keys_ref[:, key_cols]
-            grown = dot(keys, (values.astype(F32) * scale).astype(BF16), ((0,), (0,)))
-            decay = dot(row_pair[...], to_channels)
-            for t in range(TILES):
-                at = (j * TILES + t) * STATE
-                target[at : at + STATE, :] = grown[:, t * LANES : (t + 1) * LANES].astype(target.dtype)
-                decays.append(decay[0:1, t * LANES : (t + 1) * LANES])
+    targets = ((send, 1 - core), (keep, core))
+    order = [(target, side * part.half_groups + j, j) for target, side in targets for j in range(part.half_groups)]
+    for i, (_, local, _) in enumerate(order):
+        cols = columns(local, GROUP_COLS)
+        scale = dot(tail_pair[...], spread[:, columns(part.first + local, GROUP_COLS)])
+        if part.index == 0:
+            values = jnp.concatenate([value_fix[:, cols], raw_values[16:, cols]], axis=0)
+            values_ref[:, cols] = values
+        else:
+            values = values_ref[:, cols]
+        scaled[i] = (values.astype(F32) * scale).astype(BF16)
+    for target, side in targets:
+        decay = dot(
+            row_pair[...],
+            spread[:, columns((part.first + side * part.half_groups) // part.half_groups, part.width // 2)],
+        )
+        decays = [decay[0:1, t * LANES : (t + 1) * LANES] for t in range(part.half_tiles)]
         if target is send:
             put_decays(send, part.half_tiles, decays)
         else:
             for t, d in enumerate(decays):
                 keep_decay[t : t + 1, :] = d
+    for i, (target, local, j) in enumerate(order):
+        grown = dot(keys_ref[:, columns(local, STATE)], scaled[i], ((0,), (0,)))
+        for t in range(TILES):
+            at = (j * TILES + t) * STATE
+            target[at : at + STATE, :] = grown[:, t * LANES : (t + 1) * LANES].astype(target.dtype)
 
 
 def tile_rows(t):
@@ -352,7 +374,7 @@
             own[tile_rows(at), :] = jnp.where(first, chip, later).astype(BF16)
 
 
-def inside(part, values_ref, keys_ref, reads_ref, both, both_t, carry_pair, row_pair, gate, base, slope):
+def inside(part, values_ref, keys_ref, reads_ref, both, both_t, carry_pair, row_pair, spread, gate, base, slope):
     row = lax.broadcasted_iota(jnp.int32, (SPAN, SPAN), 0)
     lane = lax.broadcasted_iota(jnp.int32, (SPAN, SPAN), 1)
     causal = row >= lane
@@ -370,7 +392,7 @@
             weights = scores * jnp.exp(jnp.where(causal, gap, -jnp.inf)) * both_t[HEADS + h : HEADS + h + 1, :]
             found.append(dot(weights.astype(BF16), values[:, i * HEAD_DIM : (i + 1) * HEAD_DIM]))
         within = jnp.concatenate(found, axis=1)
-        to_channels = spread(group)
+        to_channels = spread[:, group * GROUP_COLS : (group + 1) * GROUP_COLS]
         skip = dot(row_pair[...], to_channels)[8:9, :]
         opened = silu(gate[:, group * GROUP_COLS : (group + 1) * GROUP_COLS].astype(F32))
         base[:, cols] = (within + skip * values.astype(F32)) * opened
@@ -414,7 +436,10 @@
         copy.wait()
 
 
-ORDER = "I0 P1 I1 A0 A1 R0 B0 B1 C0 C1 W0 W1 S0 S1 H0 H1 E0 F0 E1 F1"
+ORDER = (
+    "I0", "P1", "I1", "A0", "A1", "B0", "B1", "C0", "C1", "R0", "W0", "W1", "S0", "S1",
+    "H0", "H1", "E0", "F0", "E1", "F1",
+)
 
 
 def shards(mixer_input, gate_input, step_raw, conv_weight, conv_bias, step_bias, decay_log, skip_gain, norm_gain):
@@ -423,10 +448,10 @@
     parts = [Part(i) for i in range(len(SIZES))]
 
     def across(value, bit):
-        return lax.ppermute(value, "seq", [(i, i ^ (1 << bit)) for i in range(devices)])
-
-    def padded(rows):
-        return pltpu.VMEM((8 + rows, 512), F32)
+        flipped = 1 << bit if bit < 2 else (2 << bit) - 4
+        return lax.ppermute(value, "seq", [(i, i ^ flipped) for i in range(devices)])
+
+    padded = pltpu.VMEM((24, 512), F32)
 
     def decays_of(tiles):
         return vmem(decay_rows(tiles), LANES, F32)
@@ -448,7 +473,7 @@
 
     halo = lax.ppermute(mixer_input[SPAN - 3 :], "seq", [(i, i + 1) for i in range(devices - 1)])
     p = parts[0]
-    held, weight, bias, raw_values, raw_keys, both, both_t, tail_pair, carry_pair, row_pair = call(
+    held, weight, bias, raw_values, raw_keys, both, both_t, tail_pair, carry_pair, row_pair, spread = call(
         functools.partial(prepare, p),
         [
             vmem(SPAN, CONV_COLS, BF16),
@@ -460,13 +485,13 @@
             vmem(SPAN, 2 * HEADS, BF16),
             vmem(SPAN, 2 * HEADS, BF16),
             vmem(16, 2 * HEADS, BF16),
+            vmem(2 * HEADS, INNER, BF16),
         ],
         mixer_input, step_raw.T, step_bias[None, :], decay_log[None, :], skip_gain[None, :],
         conv_weight, conv_bias[None, :],
         hbm=range(7),
         cost=2.5,
         scratch=[
-            padded(SPAN),
             pltpu.VMEM((HEADS, SPAN), BF16),
             pltpu.VMEM((24, HEADS), F32),
             pltpu.SemaphoreType.DMA((12,)),
@@ -476,7 +501,7 @@
     have = {}
     token = ()
     results = []
-    for stage in ORDER.split():
+    for stage in ORDER:
         kind, p = stage[0], parts[int(stage[1:])]
         n = p.index
         get = lambda name: have[name, n]
@@ -487,25 +512,27 @@
         if kind == "P":
             values, keys = call(
                 functools.partial(prepare_rest, p.spans), rows_of(p), held, halo, weight, bias,
-                after=token, cost=0.4 * p.groups, scratch=[padded(SPAN)],
+                after=token, cost=0.4 * p.groups, scratch=[padded],
             )
             put(values=values, keys=keys)
             token = (keys,)
         elif kind == "R":
             (reads,) = call(
                 functools.partial(prepare_rest, [(INNER + KEYS, KEYS)]), [vmem(SPAN, KEYS, BF16)],
-                held, halo, weight, bias, after=token, cost=0.6, scratch=[padded(SPAN)],
+                held, halo, weight, bias, after=token, cost=0.6, scratch=[padded],
             )
             token = (reads,)
         elif kind == "I":
             outs = [half_send(p), vmem(p.half_rows, LANES, F32), decays_of(p.half_tiles)]
+            scaled = pltpu.VMEM((p.groups, SPAN, GROUP_COLS), BF16)
             if n == 0:
                 send, keep, keep_decay, values, keys = call(
                     functools.partial(increments, p), outs + rows_of(p),
-                    held, halo, weight, bias, raw_values, raw_keys, tail_pair, row_pair,
+                    held, halo, weight, bias, raw_values, raw_keys, tail_pair, row_pair, spread,
                     cost=0.3 * p.groups,
                     scratch=[
-                        padded(16),
+                        scaled,
+                        padded,
                         pltpu.VMEM((16, p.width), BF16),
                         pltpu.VMEM((16, p.groups * STATE), BF16),
                     ],
@@ -513,8 +540,8 @@
                 put(values=values, keys=keys)
             else:
                 send, keep, keep_decay = call(
-                    functools.partial(increments, p), outs, get("values"), get("keys"), tail_pair, row_pair,
-                    after=token, cost=0.3 * p.groups,
+                    functools.partial(increments, p), outs, get("values"), get("keys"), tail_pair, row_pair, spread,
+                    after=token, cost=0.3 * p.groups, scratch=[scaled],
                 )
             put(kept=(keep, keep_decay, across(send, 0)))
             token = (keep_decay,)
@@ -560,7 +587,7 @@
             put(
                 mixed=call(
                     functools.partial(inside, p), [vmem(SPAN, p.width, F32)] * 2,
-                    get("values"), get("keys"), reads, both, both_t, carry_pair, row_pair, gate_input,
+                    get("values"), get("keys"), reads, both, both_t, carry_pair, row_pair, spread, gate_input,
                     after=token, cost=0.42 * p.groups,
                 )
             )

time: 48.9 us -> 45.3 us (0.926)
  waiting for transfers between devices: 13.6 us -> 9.75 us
  starting transfers between devices: 19.8 us -> 22.5 us
  Pallas kernels: 14.2 us -> 11.7 us
    ppermute x12, waiting for transfers between devices: 13.6 us -> 9.75 us  [across(): lax.ppermute(value, 'seq', [(i, i ^ flipped) for i in range(devices)])]
    ppermute x12, starting transfers between devices: 17.4 us -> 20.1 us  [across(): lax.ppermute(value, 'seq', [(i, i ^ flipped) for i in range(devices)])]
    pallas_call x21, Pallas kernels: 14.2 us -> 11.7 us  [call(): pl.pallas_call(kernel, out_shape=[space(shape, kind) for shape, kind, spa...]
  transfers between devices with their start and end apart: 13 -> 13, of which waited for: 8 -> 5; matrix products, arithmetic and copies ran while one was open for 0% -> 0% of each run, Pallas kernels for 24% -> 22%
where the time goes in v4:
time: 45.3 us; the launch traced here: 45 us
  starting transfers between devices  22.5 us (50%)
  Pallas kernels  11.7 us (26%)
  waiting for transfers between devices  9.75 us (22%)
  local copies, waits for them, and re-layouts  0.93 us (2%)
    ppermute x12, starting transfers between devices, across(): lax.ppermute(value, 'seq', [(i, i ^ flipped) for i in range(devices)])  20.1 us
    pallas_call x21, Pallas kernels, call(): pl.pallas_call(kernel, out_shape=[space(shape, kind) for shape, kind, spa...  11.7 us
    ppermute x12, waiting for transfers between devices, across(): lax.ppermute(value, 'seq', [(i, i ^ flipped) for i in range(devices)])  9.75 us
    ppermute x1, starting transfers between devices, shards(): lax.ppermute(mixer_input[SPAN - 3:], 'seq', [(i, i + 1) for i in range(de...  2.36 us
    slice x1, local copies, waits for them, and re-layouts, shards(): mixer_input[SPAN - 3:]  0.92 us
  transfers between devices with their start and end apart: 13, of which 5 were waited for; matrix products, arithmetic and copies ran while one was open for 0% of the time, Pallas kernels for 22%

profile of v4, /device:TPU:0, one launch (start us, length us, event | category | flops | bytes accessed | tf_op | source)
XLA Modules:
  0.0 45.0 jit_solution(2028650506686796861)
XLA Ops:
  0.0 0.9 %slice.3 = bf16[3,6144]{1,0:T(4,128)(2,1)S(1)} slice(bf16[128,6144]{1,0:T(8,128)(2,1)} %refs_0_.1), slice={[125:128], [0:6144]} | slice | bytes 73728 | tf_op jit(solution)/shard_map/slice | solution.py:474
  0.9 2.4 %collective-permute-start = (bf16[3,6144]{1,0:T(4,128)(2,1)S(1)}, bf16[3,6144]{1,0:T(4,128)(2,1)S(1)}, u32[]{:S(2)}, u32[]{:S(2)}) collective-permute-start(bf16[3,6144]{1,0:T(4,128)(2,1)S(1)} %slice.3), channel_id=1, source_target_pairs={{0,1},{1,2},{2,3},{3,4},{4,5},{5,6},{6,7},{7,8},{8,9},{9,10},{10,1... | collective-permute-start | bytes 110600 | tf_op jit(solution)/shard_map/ppermute | solution.py:474
  3.3 2.2 %shard_map.91 = (bf16[128,6144]{1,0:T(8,128)(2,1)S(1)}, bf16[4,6144]{1,0:T(4,128)(2,1)S(1)}, f32[1,6144]{1,0:T(1,128)S(1)}, bf16[128,2048]{1,0:T(8,128)(2,1)S(1)...) custom-call(bf16[128,6144]{1,0:T(8,128)(2,1)} %refs_0_.1, ...), custom_call_target="tpu_custom_call" | custom-call | flops 2500000000 | bytes 7500000 | tf_op jit(solution)/shard_map/pallas_call | solution.py:65
  5.5 0.0 collective-permute-done.refs_1_
  5.5 0.8 %shard_map.92 = (bf16[1040,128]{1,0:T(8,128)(2,1)S(1)}, f32[1024,128]{1,0:T(8,128)S(1)}, f32[8,128]{1,0:T(8,128)S(1)}, bf16[128,2048]{1,0:T(8,128)(2,1)S(1)}, bf16[128,512]{1,0:T(8,128)(2,1)S(1)}) custom-call(bf16[128,6144]{1,0:T(8,128)(2,1)S(1)} %get-tuple-element.56.refs_0_, bf16[3,6144]{1,0:T(4,128)(2,1)S(1)} %collective-permute-done.refs_1_, ...), custom_call_target="tpu_custom_call" | custom-call | flops 1200000000 | bytes 3600000 | tf_op jit(solution)/shard_map/pallas_call | solution.py:65
  6.3 2.7 %collective-permute-start.2 = (bf16[1040,128]{1,0:T(8,128)(2,1)S(1)}, bf16[1040,128]{1,0:T(8,128)(2,1)S(1)}, u32[]{:S(2)}, u32[]{:S(2)}) collective-permute-start(bf16[1040,128]{1,0:T(8,128)(2,1)S(1)} %get-tuple-element.71), channel_id=1, source_target_pairs={{0,1},{1,0},{2,3},{3,2},{4,5},{5,4},{6,7},{7,6},{8,9},{9,8},{10,11... | collective-permute-start | bytes 798728 | tf_op jit(solution)/shard_map/ppermute | solution.py:452
  9.0 1.2 %shard_map.93 = (bf16[128,2048]{1,0:T(8,128)(2,1)S(1)}, bf16[128,512]{1,0:T(8,128)(2,1)S(1)}) custom-call(bf16[128,6144]{1,0:T(8,128)(2,1)S(1)} %get-tuple-element.56.refs_0_, bf16[3,6144]{1,0:T(4,128)(2,1)S(1)} %collective-permute-done.refs_1_, bf16[4,6144]{1,0:T(4,128)(2,1)S(1)} %get-tuple-element.57.refs_2_, f32[1,6144]{1,0:T(1,128)S(1)} %get-tuple-element.58.refs_3_, ...), custom_call_target="tpu_custom_call" | custom-call | flops 1600000000 | bytes 4800000 | tf_op jit(solution)/shard_map/pallas_call | solution.py:65
  10.2 0.5 %shard_map.94 = (bf16[1040,128]{1,0:T(8,128)(2,1)S(1)}, f32[1024,128]{1,0:T(8,128)S(1)}, f32[8,128]{1,0:T(8,128)S(1)}) custom-call(bf16[128,2048]{1,0:T(8,128)(2,1)S(1)} %get-tuple-element.65.refs_0_, bf16[128,512]{1,0:T(8,128)(2,1)S(1)} %get-tuple-element.66.refs_1_.refs_5_, bf16[128,128]{1,0:T(8,128)(2,1)S(1)} %get-tuple-element.61.refs_6_.refs_2_, ...), custom_call_target="tpu_custom_call" | custom-call | flops 1200000000 | bytes 3600000 | tf_op jit(solution)/shard_map/pallas_call | solution.py:65
  10.7 0.1 collective-permute-start.1
  10.8 0.0 collective-permute-done.2.refs_2_.refs_4_
  10.8 0.1 shard_map.95
  11.0 1.7 %collective-permute-start.4 = (bf16[528,128]{1,0:T(8,128)(2,1)S(1)}, bf16[528,128]{1,0:T(8,128)(2,1)S(1)}, u32[]{:S(2)}, u32[]{:S(2)}) collective-permute-start(bf16[528,128]{1,0:T(8,128)(2,1)S(1)} %get-tuple-element.77), channel_id=1, source_target_pairs={{0,2},{1,3},{2,0},{3,1},{4,6},{5,7},{6,4},{7,5},{8,10},{9,11},{10,... | collective-permute-start | bytes 405512 | tf_op jit(solution)/shard_map/ppermute | solution.py:452
  12.6 0.0 collective-permute-done.1.refs_2_.refs_4_
  12.6 0.1 shard_map.96
  12.7 1.3 %collective-permute-start.3 = (bf16[528,128]{1,0:T(8,128)(2,1)S(1)}, bf16[528,128]{1,0:T(8,128)(2,1)S(1)}, u32[]{:S(2)}, u32[]{:S(2)}) collective-permute-start(bf16[528,128]{1,0:T(8,128)(2,1)S(1)} %get-tuple-element.75), channel_id=1, source_target_pairs={{0,2},{1,3},{2,0},{3,1},{4,6},{5,7},{6,4},{7,5},{8,10},{9,11},{10,... | collective-permute-start | bytes 405512 | tf_op jit(solution)/shard_map/ppermute | solution.py:452
  14.0 3.4 %collective-permute-done.4.refs_2_.refs_5_ = bf16[528,128]{1,0:T(8,128)(2,1)S(1)} collective-permute-done((bf16[528,128]{1,0:T(8,128)(2,1)S(1)}, bf16[528,128]{1,0:T(8,128)(2,1)S(1)}, u32[]{:S(2)}, u32[]{:S(2)}) %collective-permute-start.4) | collective-permute-done | bytes 135200 | tf_op jit(solution)/shard_map/ppermute | solution.py:452
  17.4 0.1 shard_map.97
  17.5 2.7 %collective-permute-start.6 = (bf16[528,128]{1,0:T(8,128)(2,1)S(1)}, bf16[528,128]{1,0:T(8,128)(2,1)S(1)}, u32[]{:S(2)}, u32[]{:S(2)}) collective-permute-start(bf16[528,128]{1,0:T(8,128)(2,1)S(1)} %get-tuple-element.83), channel_id=1, source_target_pairs={{0,4},{1,5},{2,6},{3,7},{4,0},{5,1},{6,2},{7,3},{8,12},{9,13},{10,... | collective-permute-start | bytes 405512 | tf_op jit(solution)/shard_map/ppermute | solution.py:452
  20.2 0.0 collective-permute-done.3.refs_2_.refs_5_
  20.2 0.1 shard_map.98
  20.3 0.0 copy-start.1
  20.3 1.9 %collective-permute-start.5 = (bf16[528,128]{1,0:T(8,128)(2,1)S(1)}, bf16[528,128]{1,0:T(8,128)(2,1)S(1)}, u32[]{:S(2)}, u32[]{:S(2)}) collective-permute-start(bf16[528,128]{1,0:T(8,128)(2,1)S(1)} %get-tuple-element.81), channel_id=1, source_target_pairs={{0,4},{1,5},{2,6},{3,7},{4,0},{5,1},{6,2},{7,3},{8,12},{9,13},{10,... | collective-permute-start | bytes 405512 | tf_op jit(solution)/shard_map/ppermute | solution.py:452
  22.2 1.9 %collective-permute-done.6.refs_2_ = bf16[528,128]{1,0:T(8,128)(2,1)S(1)} collective-permute-done((bf16[528,128]{1,0:T(8,128)(2,1)S(1)}, bf16[528,128]{1,0:T(8,128)(2,1)S(1)}, u32[]{:S(2)}, u32[]{:S(2)}) %collective-permute-start.6) | collective-permute-done | bytes 135200 | tf_op jit(solution)/shard_map/ppermute | solution.py:452
  24.1 0.1 shard_map.99
  24.2 4.4 %collective-permute-start.7 = (bf16[528,128]{1,0:T(8,128)(2,1)S(1)}, bf16[528,128]{1,0:T(8,128)(2,1)S(1)}, u32[]{:S(2)}, u32[]{:S(2)}) collective-permute-start(bf16[528,128]{1,0:T(8,128)(2,1)S(1)} %get-tuple-element.86), channel_id=1, source_target_pairs={{0,12},{1,13},{2,14},{3,15},{4,8},{5,9},{6,10},{7,11},{8,4},{9,5},... | collective-permute-start | bytes 405512 | tf_op jit(solution)/shard_map/ppermute | solution.py:452
  28.6 0.0 collective-permute-done.5.refs_2_
  28.6 0.1 shard_map.100
  28.7 3.0 %collective-permute-start.9 = (bf16[528,128]{1,0:T(8,128)(2,1)S(1)}, bf16[528,128]{1,0:T(8,128)(2,1)S(1)}, u32[]{:S(2)}, u32[]{:S(2)}) collective-permute-start(bf16[528,128]{1,0:T(8,128)(2,1)S(1)} %get-tuple-element.97), channel_id=1, source_target_pairs={{0,12},{1,13},{2,14},{3,15},{4,8},{5,9},{6,10},{7,11},{8,4},{9,5},... | collective-permute-start | bytes 405512 | tf_op jit(solution)/shard_map/ppermute | solution.py:452
  31.7 0.5 %shard_map.101.refs_2_.refs_9_.refs_0_.refs_3_ = bf16[128,1024]{1,0:T(8,128)(2,1)S(1)} custom-call(bf16[128,6144]{1,0:T(8,128)(2,1)S(1)} %get-tuple-element.56.refs_0_, bf16[3,6144]{1,0:T(4,128)(2,1)S(1)} %collective-permute-done.refs_1_, bf16[4,6144]{1,0:T(4,128)(2,1)S(1)} %get-tuple-element.57.refs_2_, f32[1,6144]{1,0:T(1,128)S(1)} %get-tuple-element.58.refs_3_, ...), custom_call_target="tpu_custom_call" | custom-call | flops 600000000 | bytes 1800000 | tf_op jit(solution)/shard_map/pallas_call | solution.py:65
  32.2 0.0 copy-done.1
  32.2 1.7 %shard_map.102 = (f32[128,2048]{1,0:T(8,128)S(1)}, f32[128,2048]{1,0:T(8,128)S(1)}) custom-call(bf16[128,2048]{1,0:T(8,128)(2,1)S(1)} %get-tuple-element.91.refs_0_, bf16[128,512]{1,0:T(8,128)(2,1)S(1)} %get-tuple-element.92.refs_1_, bf16[128,1024]{1,0:T(8,128)(2,1)S(1)} %shard_map.101.refs_2_.refs_9_.refs_0_.refs_3_, ...), custom_call_target="tpu_custom_call" | custom-call | flops 1680000000 | bytes 5040000 | tf_op jit(solution)/shard_map/pallas_call | solution.py:65
  33.9 1.7 %shard_map.103 = (f32[128,2048]{1,0:T(8,128)S(1)}, f32[128,2048]{1,0:T(8,128)S(1)}) custom-call(bf16[128,2048]{1,0:T(8,128)(2,1)S(1)} %get-tuple-element.65.refs_0_, bf16[128,512]{1,0:T(8,128)(2,1)S(1)} %get-tuple-element.66.refs_1_.refs_5_, bf16[128,1024]{1,0:T(8,128)(2,1)S(1)} %shard_map.101.refs_2_.refs_9_.refs_0_.refs_3_, ...), custom_call_target="tpu_custom_call" | custom-call | flops 1680000000 | bytes 5040000 | tf_op jit(solution)/shard_map/pallas_call | solution.py:65
  35.5 0.0 collective-permute-done.7.refs_0_
  35.6 0.1 shard_map.104
  35.7 0.7 %collective-permute-start.8 = (bf16[512,128]{1,0:T(8,128)(2,1)S(1)}, bf16[512,128]{1,0:T(8,128)(2,1)S(1)}, u32[]{:S(2)}, u32[]{:S(2)}) collective-permute-start(bf16[512,128]{1,0:T(8,128)(2,1)S(1)} %get-tuple-element.96), channel_id=1, source_target_pairs={{0,2},{1,3},{2,0},{3,1},{4,6},{5,7},{6,4},{7,5},{8,10},{9,11},{10,... | collective-permute-start | bytes 393224 | tf_op jit(solution)/shard_map/ppermute | solution.py:452
  36.4 0.0 collective-permute-done.9.refs_0_
  36.4 0.1 shard_map.105
  36.5 0.0 copy-start
  36.5 1.5 %collective-permute-start.10 = (bf16[512,128]{1,0:T(8,128)(2,1)S(1)}, bf16[512,128]{1,0:T(8,128)(2,1)S(1)}, u32[]{:S(2)}, u32[]{:S(2)}) collective-permute-start(bf16[512,128]{1,0:T(8,128)(2,1)S(1)} %get-tuple-element.102), channel_id=1, source_target_pairs={{0,2},{1,3},{2,0},{3,1},{4,6},{5,7},{6,4},{7,5},{8,10},{9,11},{10,... | collective-permute-start | bytes 393224 | tf_op jit(solution)/shard_map/ppermute | solution.py:452
  37.9 2.8 %collective-permute-done.8.refs_1_ = bf16[512,128]{1,0:T(8,128)(2,1)S(1)} collective-permute-done((bf16[512,128]{1,0:T(8,128)(2,1)S(1)}, bf16[512,128]{1,0:T(8,128)(2,1)S(1)}, u32[]{:S(2)}, u32[]{:S(2)}) %collective-permute-start.8) | collective-permute-done | bytes 131104 | tf_op jit(solution)/shard_map/ppermute | solution.py:452
  40.7 0.2 shard_map.106
  40.9 0.1 collective-permute-start.11
  40.9 1.2 %collective-permute-done.10.refs_1_ = bf16[512,128]{1,0:T(8,128)(2,1)S(1)} collective-permute-done((bf16[512,128]{1,0:T(8,128)(2,1)S(1)}, bf16[512,128]{1,0:T(8,128)(2,1)S(1)}, u32[]{:S(2)}, u32[]{:S(2)}) %collective-permute-start.10) | collective-permute-done | bytes 131104 | tf_op jit(solution)/shard_map/ppermute | solution.py:452
  42.1 0.2 shard_map.107
  42.3 0.1 collective-permute-start.12
  42.3 0.0 copy-done
  42.3 0.3 shard_map.108.refs_5_.refs_0_
  42.7 0.0 collective-permute-done.11.refs_1_
  42.7 0.3 shard_map.109.refs_5_.refs_1_
  43.0 0.3 shard_map.110.refs_2_.refs_8_
  43.3 0.5 %collective-permute-done.12.refs_4_ = bf16[1024,128]{1,0:T(8,128)(2,1)S(1)} collective-permute-done((bf16[1024,128]{1,0:T(8,128)(2,1)S(1)}, bf16[1024,128]{1,0:T(8,128)(2,1)S(1)}, u32[]{:S(2)}, u32[]{:S(2)}) %collective-permute-start.12) | collective-permute-done | bytes 262176 | tf_op jit(solution)/shard_map/ppermute | solution.py:452
  43.9 1.2 %shard_map.111 = bf16[128,4096]{1,0:T(8,128)(2,1)} custom-call(bf16[128,1024]{1,0:T(8,128)(2,1)S(1)} %shard_map.108.refs_5_.refs_0_, bf16[128,1024]{1,0:T(8,128)(2,1)S(1)} %shard_map.109.refs_5_.refs_1_, bf16[128,1024]{1,0:T(8,128)(2,1)S(1)} %shard_map.110.refs_2_.refs_8_, bf16[128,1024]{1,0:T(8,128)(2,1)S(1)} %shard_map.101.refs_2_.refs_9_.refs_0_.refs_3_, ...), custom_call_target="tpu_custom_call" | custom-call | flops 400000000 | bytes 1200000 | tf_op jit(solution)/shard_map/pallas_call | solution.py:65
Async XLA Ops:
  0.9 4.6 %collective-permute-start = (bf16[3,6144]{1,0:T(4,128)(2,1)S(1)}, bf16[3,6144]{1,0:T(4,128)(2,1)S(1)}, u32[]{:S(2)}, u32[]{:S(2)}) collective-permute-start(bf16[3,6144]{1,0:T(4,128)(2,1)S(1)} %slice.3), channel_id=1, source_target_pairs={{0,1},{1,2},{2,3},{3,4},{4,5},{5,6},{6,7},{7,8},{8,9},{9,10},{10,1... | collective-permute-start | bytes 110600 | tf_op jit(solution)/shard_map/ppermute | solution.py:474
  6.3 4.5 %collective-permute-start.2 = (bf16[1040,128]{1,0:T(8,128)(2,1)S(1)}, bf16[1040,128]{1,0:T(8,128)(2,1)S(1)}, u32[]{:S(2)}, u32[]{:S(2)}) collective-permute-start(bf16[1040,128]{1,0:T(8,128)(2,1)S(1)} %get-tuple-element.71), channel_id=1, source_target_pairs={{0,1},{1,0},{2,3},{3,2},{4,5},{5,4},{6,7},{7,6},{8,9},{9,8},{10,11... | collective-permute-start | bytes 798728 | tf_op jit(solution)/shard_map/ppermute | solution.py:452
  10.7 1.9 %collective-permute-start.1 = (bf16[1040,128]{1,0:T(8,128)(2,1)S(1)}, bf16[1040,128]{1,0:T(8,128)(2,1)S(1)}, u32[]{:S(2)}, u32[]{:S(2)}) collective-permute-start(bf16[1040,128]{1,0:T(8,128)(2,1)S(1)} %get-tuple-element.69), channel_id=1, source_target_pairs={{0,1},{1,0},{2,3},{3,2},{4,5},{5,4},{6,7},{7,6},{8,9},{9,8},{10,11... | collective-permute-start | bytes 798728 | tf_op jit(solution)/shard_map/ppermute | solution.py:452
  11.0 6.4 %collective-permute-start.4 = (bf16[528,128]{1,0:T(8,128)(2,1)S(1)}, bf16[528,128]{1,0:T(8,128)(2,1)S(1)}, u32[]{:S(2)}, u32[]{:S(2)}) collective-permute-start(bf16[528,128]{1,0:T(8,128)(2,1)S(1)} %get-tuple-element.77), channel_id=1, source_target_pairs={{0,2},{1,3},{2,0},{3,1},{4,6},{5,7},{6,4},{7,5},{8,10},{9,11},{10,... | collective-permute-start | bytes 405512 | tf_op jit(solution)/shard_map/ppermute | solution.py:452
  12.7 7.4 %collective-permute-start.3 = (bf16[528,128]{1,0:T(8,128)(2,1)S(1)}, bf16[528,128]{1,0:T(8,128)(2,1)S(1)}, u32[]{:S(2)}, u32[]{:S(2)}) collective-permute-start(bf16[528,128]{1,0:T(8,128)(2,1)S(1)} %get-tuple-element.75), channel_id=1, source_target_pairs={{0,2},{1,3},{2,0},{3,1},{4,6},{5,7},{6,4},{7,5},{8,10},{9,11},{10,... | collective-permute-start | bytes 405512 | tf_op jit(solution)/shard_map/ppermute | solution.py:452
  17.5 6.6 %collective-permute-start.6 = (bf16[528,128]{1,0:T(8,128)(2,1)S(1)}, bf16[528,128]{1,0:T(8,128)(2,1)S(1)}, u32[]{:S(2)}, u32[]{:S(2)}) collective-permute-start(bf16[528,128]{1,0:T(8,128)(2,1)S(1)} %get-tuple-element.83), channel_id=1, source_target_pairs={{0,4},{1,5},{2,6},{3,7},{4,0},{5,1},{6,2},{7,3},{8,12},{9,13},{10,... | collective-permute-start | bytes 405512 | tf_op jit(solution)/shard_map/ppermute | solution.py:452
  20.3 11.9 %copy-start.1 = (bf16[128,4096]{1,0:T(8,128)(2,1)S(1)}, bf16[128,4096]{1,0:T(8,128)(2,1)}, u32[]{:S(2)}) copy-start(bf16[128,4096]{1,0:T(8,128)(2,1)} %refs_8_.3) | copy-start | bytes 3145732
  20.3 8.3 %collective-permute-start.5 = (bf16[528,128]{1,0:T(8,128)(2,1)S(1)}, bf16[528,128]{1,0:T(8,128)(2,1)S(1)}, u32[]{:S(2)}, u32[]{:S(2)}) collective-permute-start(bf16[528,128]{1,0:T(8,128)(2,1)S(1)} %get-tuple-element.81), channel_id=1, source_target_pairs={{0,4},{1,5},{2,6},{3,7},{4,0},{5,1},{6,2},{7,3},{8,12},{9,13},{10,... | collective-permute-start | bytes 405512 | tf_op jit(solution)/shard_map/ppermute | solution.py:452
  24.2 11.4 %collective-permute-start.7 = (bf16[528,128]{1,0:T(8,128)(2,1)S(1)}, bf16[528,128]{1,0:T(8,128)(2,1)S(1)}, u32[]{:S(2)}, u32[]{:S(2)}) collective-permute-start(bf16[528,128]{1,0:T(8,128)(2,1)S(1)} %get-tuple-element.86), channel_id=1, source_target_pairs={{0,12},{1,13},{2,14},{3,15},{4,8},{5,9},{6,10},{7,11},{8,4},{9,5},... | collective-permute-start | bytes 405512 | tf_op jit(solution)/shard_map/ppermute | solution.py:452
  28.7 7.7 %collective-permute-start.9 = (bf16[528,128]{1,0:T(8,128)(2,1)S(1)}, bf16[528,128]{1,0:T(8,128)(2,1)S(1)}, u32[]{:S(2)}, u32[]{:S(2)}) collective-permute-start(bf16[528,128]{1,0:T(8,128)(2,1)S(1)} %get-tuple-element.97), channel_id=1, source_target_pairs={{0,12},{1,13},{2,14},{3,15},{4,8},{5,9},{6,10},{7,11},{8,4},{9,5},... | collective-permute-start | bytes 405512 | tf_op jit(solution)/shard_map/ppermute | solution.py:452
  35.7 5.0 %collective-permute-start.8 = (bf16[512,128]{1,0:T(8,128)(2,1)S(1)}, bf16[512,128]{1,0:T(8,128)(2,1)S(1)}, u32[]{:S(2)}, u32[]{:S(2)}) collective-permute-start(bf16[512,128]{1,0:T(8,128)(2,1)S(1)} %get-tuple-element.96), channel_id=1, source_target_pairs={{0,2},{1,3},{2,0},{3,1},{4,6},{5,7},{6,4},{7,5},{8,10},{9,11},{10,... | collective-permute-start | bytes 393224 | tf_op jit(solution)/shard_map/ppermute | solution.py:452
  36.5 5.9 %copy-start = (f32[4096]{0:T(1024)S(1)}, f32[4096]{0:T(1024)}, u32[]{:S(2)}) copy-start(f32[4096]{0:T(1024)} %param.17) | copy-start | bytes 49156
  36.5 5.6 %collective-permute-start.10 = (bf16[512,128]{1,0:T(8,128)(2,1)S(1)}, bf16[512,128]{1,0:T(8,128)(2,1)S(1)}, u32[]{:S(2)}, u32[]{:S(2)}) collective-permute-start(bf16[512,128]{1,0:T(8,128)(2,1)S(1)} %get-tuple-element.102), channel_id=1, source_target_pairs={{0,2},{1,3},{2,0},{3,1},{4,6},{5,7},{6,4},{7,5},{8,10},{9,11},{10,... | collective-permute-start | bytes 393224 | tf_op jit(solution)/shard_map/ppermute | solution.py:452
  40.9 1.8 %collective-permute-start.11 = (bf16[1024,128]{1,0:T(8,128)(2,1)S(1)}, bf16[1024,128]{1,0:T(8,128)(2,1)S(1)}, u32[]{:S(2)}, u32[]{:S(2)}) collective-permute-start(bf16[1024,128]{1,0:T(8,128)(2,1)S(1)} %get-tuple-element.104), channel_id=1, source_target_pairs={{0,1},{1,0},{2,3},{3,2},{4,5},{5,4},{6,7},{7,6},{8,9},{9,8},{10,11... | collective-permute-start | bytes 786440 | tf_op jit(solution)/shard_map/ppermute | solution.py:452
  42.3 1.6 %collective-permute-start.12 = (bf16[1024,128]{1,0:T(8,128)(2,1)S(1)}, bf16[1024,128]{1,0:T(8,128)(2,1)S(1)}, u32[]{:S(2)}, u32[]{:S(2)}) collective-permute-start(bf16[1024,128]{1,0:T(8,128)(2,1)S(1)} %get-tuple-element.106), channel_id=1, source_target_pairs={{0,1},{1,0},{2,3},{3,2},{4,5},{5,4},{6,7},{7,6},{8,9},{9,8},{10,11... | collective-permute-start | bytes 786440 | tf_op jit(solution)/shard_map/ppermute | solution.py:452

commit v5 on v4

--- a/solution.py
+++ b/solution.py
@@ -134,6 +134,7 @@
 
 
 def convolve_head(source, halo, weight, bias, padded, spans, outs):
+    first = lax.axis_index("seq") == 0
     for (start, width), out in zip(spans, outs):
         block = min(width, 512)
 
@@ -142,23 +143,17 @@
             cols = columns(i, block, start)
             here = padded.at[:, 0:block]
             here[0:8, :] = jnp.zeros((8, block), F32)
-            here[5:8, :] = halo[:, cols].astype(F32)
+            here[5:8, :] = jnp.where(first, 0.0, halo[:, cols].astype(F32))
             here[8:24, :] = source[0:16, cols].astype(F32)
             out[0:16, columns(i, block)] = convolve_into(16, here, weight, bias, cols)
 
 
 def prepare(
-    part, x, raw_t, step_bias, decay_log, skip, weight_in, bias_in,
-    held, weight, bias, values, keys, both, both_t, tail_pair, carry_pair, row_pair, spread,
-    raw_here, small, sems,
+    parts, x, raw_t, step_bias, decay_log, skip, weight_in, bias_in,
+    held, weight, bias, both, both_t, tail_pair, carry_pair, row_pair, spread, *refs,
 ):
-    first = part.spans
-    pieces_of_x = list(first)
-    at = 0
-    for start, width in sorted(first) + [(CONV_COLS, 0)]:
-        if start > at:
-            pieces_of_x.append((at, start - at))
-        at = start + width
+    *outs, raw_here, small, sems = refs
+    spans = [span for part in parts for span in part.spans]
     copies = [
         pltpu.make_async_copy(raw_t, raw_here, sems.at[0]),
         pltpu.make_async_copy(step_bias, small.at[0:1], sems.at[1]),
@@ -167,7 +162,7 @@
         pltpu.make_async_copy(weight_in, weight, sems.at[4]),
         pltpu.make_async_copy(bias_in, bias, sems.at[5]),
     ]
-    for i, (start, width) in enumerate(pieces_of_x):
+    for i, (start, width) in enumerate(spans + [(INNER + KEYS, KEYS)]):
         cols = slice(start, start + width)
         copies.append(pltpu.make_async_copy(x.at[:, cols], held.at[:, cols], sems.at[6 + i]))
     for copy in copies:
@@ -197,16 +192,18 @@
         [jnp.broadcast_to(jnp.exp(total), (8, HEADS)), jnp.broadcast_to(small[16:17, :], (8, HEADS))], axis=0
     )
     row_pair[...] = jnp.concatenate(pieces(rows, 2), axis=1)
-    for copy in copies[4:8]:
+    for copy in copies[4:6]:
         copy.wait()
-    convolve_body(held, weight, bias, first, (values, keys))
-    for copy in copies[8:]:
-        copy.wait()
-
-
-def prepare_rest(spans, held, halo, weight, bias, *refs):
-    convolve_body(held, weight, bias, spans, refs[:-1])
-    convolve_head(held, halo, weight, bias, refs[-1], spans, refs[:-1])
+    for i, (span, out) in enumerate(zip(spans, outs)):
+        copies[6 + i].wait()
+        convolve_body(held, weight, bias, [span], [out])
+    copies[-1].wait()
+
+
+def convolve_reads(held, halo, weight, bias, reads, padded):
+    spans = [(INNER + KEYS, KEYS)]
+    convolve_body(held, weight, bias, spans, [reads])
+    convolve_head(held, halo, weight, bias, padded, spans, [reads])
 
 
 def put_decays(send, tiles, decays):
@@ -219,26 +216,20 @@
 
 
 def increments(part, *refs):
-    if part.index == 0:
-        held, halo, weight, bias, raw_values, raw_keys = refs[:6]
-        tail_pair, row_pair, spread, send, keep, keep_decay, values_ref, keys_ref = refs[6:14]
-        scaled, padded, value_fix, key_fix = refs[14:]
-        convolve_head(held, halo, weight, bias, padded, part.spans, (value_fix, key_fix))
-        keys_ref[0:16, :] = key_fix[...]
-        keys_ref[16:, :] = raw_keys[16:, :]
-    else:
-        values_ref, keys_ref, tail_pair, row_pair, spread, send, keep, keep_decay, scaled = refs
+    held, halo, weight, bias, raw_values, raw_keys = refs[:6]
+    tail_pair, row_pair, spread, send, keep, keep_decay, values_ref, keys_ref = refs[6:14]
+    scaled, padded, value_fix, key_fix = refs[14:]
+    convolve_head(held, halo, weight, bias, padded, part.spans, (value_fix, key_fix))
+    keys_ref[0:16, :] = key_fix[...]
+    keys_ref[16:, :] = raw_keys[16:, :]
     core = lax.axis_index("seq") & 1
     targets = ((send, 1 - core), (keep, core))
     order = [(target, side * part.half_groups + j, j) for target, side in targets for j in range(part.half_groups)]
     for i, (_, local, _) in enumerate(order):
         cols = columns(local, GROUP_COLS)
         scale = dot(tail_pair[...], spread[:, columns(part.first + local, GROUP_COLS)])
-        if part.index == 0:
-            values = jnp.concatenate([value_fix[:, cols], raw_values[16:, cols]], axis=0)
-            values_ref[:, cols] = values
-        else:
-            values = values_ref[:, cols]
+        values = jnp.concatenate([value_fix[:, cols], raw_values[16:, cols]], axis=0)
+        values_ref[:, cols] = values
         scaled[i] = (values.astype(F32) * scale).astype(BF16)
     for target, side in targets:
         decay = dot(
@@ -328,7 +319,8 @@
             else:
                 new_before[rows, :] = jnp.where(upper, theirs, 0.0)
                 new_before_decay[t : t + 1, :] = jnp.where(upper, d_theirs, 1.0)
-    put_decays(send, part.quarter_tiles, decays)
+    if totals:
+        put_decays(send, part.quarter_tiles, decays)
 
 
 def to_planes(part, bit, carried, *refs):
@@ -437,7 +429,7 @@
 
 
 ORDER = (
-    "I0", "P1", "I1", "A0", "A1", "B0", "B1", "C0", "C1", "R0", "W0", "W1", "S0", "S1",
+    "I0", "I1", "R0", "A0", "A1", "W0", "B0", "W1", "B1", "C0", "C1", "S0", "S1",
     "H0", "H1", "E0", "F0", "E1", "F1",
 )
 
@@ -471,21 +463,20 @@
     def quarter(p):
         return [vmem(p.quarter_rows, LANES, F32), decays_of(p.quarter_tiles)]
 
-    halo = lax.ppermute(mixer_input[SPAN - 3 :], "seq", [(i, i + 1) for i in range(devices - 1)])
-    p = parts[0]
-    held, weight, bias, raw_values, raw_keys, both, both_t, tail_pair, carry_pair, row_pair, spread = call(
-        functools.partial(prepare, p),
+    halo = lax.ppermute(mixer_input[SPAN - 3 :], "seq", [(i, (i + 1) % devices) for i in range(devices)])
+    held, weight, bias, both, both_t, tail_pair, carry_pair, row_pair, spread, *raw = call(
+        functools.partial(prepare, parts),
         [
             vmem(SPAN, CONV_COLS, BF16),
             vmem(4, CONV_COLS, BF16),
             vmem(1, CONV_COLS, F32),
-            *rows_of(p),
             vmem(SPAN, 2 * HEADS, F32),
             vmem(2 * HEADS, SPAN, F32),
             vmem(SPAN, 2 * HEADS, BF16),
             vmem(SPAN, 2 * HEADS, BF16),
             vmem(16, 2 * HEADS, BF16),
             vmem(2 * HEADS, INNER, BF16),
+            *[shape for p in parts for shape in rows_of(p)],
         ],
         mixer_input, step_raw.T, step_bias[None, :], decay_log[None, :], skip_gain[None, :],
         conv_weight, conv_bias[None, :],
@@ -494,7 +485,7 @@
         scratch=[
             pltpu.VMEM((HEADS, SPAN), BF16),
             pltpu.VMEM((24, HEADS), F32),
-            pltpu.SemaphoreType.DMA((12,)),
+            pltpu.SemaphoreType.DMA((7 + 2 * len(parts),)),
         ],
     )
     gain = norm_gain[None, :]
@@ -509,41 +500,26 @@
         def put(**values):
             have.update({(name, n): value for name, value in values.items()})
 
-        if kind == "P":
-            values, keys = call(
-                functools.partial(prepare_rest, p.spans), rows_of(p), held, halo, weight, bias,
-                after=token, cost=0.4 * p.groups, scratch=[padded],
-            )
-            put(values=values, keys=keys)
-            token = (keys,)
-        elif kind == "R":
+        if kind == "R":
             (reads,) = call(
-                functools.partial(prepare_rest, [(INNER + KEYS, KEYS)]), [vmem(SPAN, KEYS, BF16)],
-                held, halo, weight, bias, after=token, cost=0.6, scratch=[padded],
+                convolve_reads, [vmem(SPAN, KEYS, BF16)], held, halo, weight, bias,
+                after=token, cost=0.6, scratch=[padded],
             )
             token = (reads,)
         elif kind == "I":
-            outs = [half_send(p), vmem(p.half_rows, LANES, F32), decays_of(p.half_tiles)]
-            scaled = pltpu.VMEM((p.groups, SPAN, GROUP_COLS), BF16)
-            if n == 0:
-                send, keep, keep_decay, values, keys = call(
-                    functools.partial(increments, p), outs + rows_of(p),
-                    held, halo, weight, bias, raw_values, raw_keys, tail_pair, row_pair, spread,
-                    cost=0.3 * p.groups,
-                    scratch=[
-                        scaled,
-                        padded,
-                        pltpu.VMEM((16, p.width), BF16),
-                        pltpu.VMEM((16, p.groups * STATE), BF16),
-                    ],
-                )
-                put(values=values, keys=keys)
-            else:
-                send, keep, keep_decay = call(
-                    functools.partial(increments, p), outs, get("values"), get("keys"), tail_pair, row_pair, spread,
-                    after=token, cost=0.3 * p.groups, scratch=[scaled],
-                )
-            put(kept=(keep, keep_decay, across(send, 0)))
+            send, keep, keep_decay, values, keys = call(
+                functools.partial(increments, p),
+                [half_send(p), vmem(p.half_rows, LANES, F32), decays_of(p.half_tiles), *rows_of(p)],
+                held, halo, weight, bias, *raw[2 * n : 2 * n + 2], tail_pair, row_pair, spread,
+                after=token, cost=0.2 * p.groups,
+                scratch=[
+                    pltpu.VMEM((p.groups, SPAN, GROUP_COLS), BF16),
+                    padded,
+                    pltpu.VMEM((16, p.width), BF16),
+                    pltpu.VMEM((16, p.groups * STATE), BF16),
+                ],
+            )
+            put(values=values, keys=keys, kept=(keep, keep_decay, across(send, 0)))
             token = (keep_decay,)
         elif kind == "A":
             send, own, own_decay = call(
@@ -558,7 +534,7 @@
                 totals, carried = bit + 1 < bits - 1, get("carried")
                 outs = call(
                     functools.partial(join_pair, p, bit, bool(carried), totals),
-                    [quarter_send(p)] + quarter(p) * totals + quarter(p) * (bit >= 2),
+                    [quarter_send(p) if totals else vmem(p.quarter_rows, LANES, BF16)] + quarter(p) * totals + quarter(p) * (bit >= 2),
                     *get("state"), *carried, after=token, scratch=decay_scratch(p.quarter_tiles),
                 )
                 recv = across(outs[0], bit + 1)

time: 45.3 us -> 42.3 us (0.934)
  starting transfers between devices: 22.5 us -> 8.48 us
  waiting for transfers between devices: 9.75 us -> 20.8 us
    ppermute x12, starting transfers between devices: 20.1 us -> 7.97 us  [across(): lax.ppermute(value, 'seq', [(i, i ^ flipped) for i in range(devices)])]
    ppermute x12, waiting for transfers between devices: 9.75 us -> 17.2 us  [across(): lax.ppermute(value, 'seq', [(i, i ^ flipped) for i in range(devices)])]
    ppermute x1, waiting for transfers between devices: 0.01 us -> 3.66 us  [shards(): lax.ppermute(mixer_input[SPAN - 3:], 'seq', [(i, (i + 1) % devices) for i...]
    ppermute x1, starting transfers between devices: 2.36 us -> 0.5 us  [shards(): lax.ppermute(mixer_input[SPAN - 3:], 'seq', [(i, (i + 1) % devices) for i...]
    pallas_call x21 -> x20, Pallas kernels: 11.7 us -> 11.6 us  [call(): pl.pallas_call(kernel, out_shape=[space(shape, kind) for shape, kind, spa...]
  transfers between devices with their start and end apart: 13 -> 13, of which waited for: 5 -> 10; matrix products, arithmetic and copies ran while one was open for 0% -> 0% of each run, Pallas kernels for 22% -> 23%
where the time goes in v5:
time: 42.3 us; the launch traced here: 42 us
  waiting for transfers between devices  20.8 us (49%)
  Pallas kernels  11.6 us (27%)
  starting transfers between devices  8.48 us (20%)
  local copies, waits for them, and re-layouts  0.93 us (2%)
    ppermute x12, waiting for transfers between devices, across(): lax.ppermute(value, 'seq', [(i, i ^ flipped) for i in range(devices)])  17.2 us
    pallas_call x20, Pallas kernels, call(): pl.pallas_call(kernel, out_shape=[space(shape, kind) for shape, kind, spa...  11.6 us
    ppermute x12, starting transfers between devices, across(): lax.ppermute(value, 'seq', [(i, i ^ flipped) for i in range(devices)])  7.97 us
    ppermute x1, waiting for transfers between devices, shards(): lax.ppermute(mixer_input[SPAN - 3:], 'seq', [(i, (i + 1) % devices) for i...  3.66 us
    slice x1, local copies, waits for them, and re-layouts, shards(): mixer_input[SPAN - 3:]  0.92 us
  transfers between devices with their start and end apart: 13, of which 10 were waited for; matrix products, arithmetic and copies ran while one was open for 0% of the time, Pallas kernels for 23%

profile of v5, /device:TPU:0, one launch (start us, length us, event | category | flops | bytes accessed | tf_op | source)
XLA Modules:
  0.0 42.0 jit_solution(2992777809007150117)
XLA Ops:
  0.0 0.9 %slice.3 = bf16[3,6144]{1,0:T(4,128)(2,1)S(1)} slice(bf16[128,6144]{1,0:T(8,128)(2,1)} %refs_0_.1), slice={[125:128], [0:6144]} | slice | bytes 73728 | tf_op jit(solution)/shard_map/slice | solution.py:466
  0.9 0.5 %collective-permute-start = (bf16[3,6144]{1,0:T(4,128)(2,1)S(1)}, bf16[3,6144]{1,0:T(4,128)(2,1)S(1)}, u32[]{:S(2)}, u32[]{:S(2)}) collective-permute-start(bf16[3,6144]{1,0:T(4,128)(2,1)S(1)} %slice.3), channel_id=1, source_target_pairs={{0,1},{1,2},{2,3},{3,4},{4,5},{5,6},{6,7},{7,8},{8,9},{9,10},{10,1... | collective-permute-start | bytes 110600 | tf_op jit(solution)/shard_map/ppermute | solution.py:466
  1.4 3.1 %shard_map.91 = (bf16[128,6144]{1,0:T(8,128)(2,1)S(1)}, bf16[4,6144]{1,0:T(4,128)(2,1)S(1)}, f32[1,6144]{1,0:T(1,128)S(1)}, f32[128,128]{1,0:T(8,128)S(1)}, f32[...) custom-call(bf16[128,6144]{1,0:T(8,128)(2,1)} %refs_0_.1, ...), custom_call_target="tpu_custom_call" | custom-call | flops 2500000000 | bytes 7500000 | tf_op jit(solution)/shard_map/pallas_call | solution.py:65
  4.5 3.7 %collective-permute-done.refs_1_ = bf16[3,6144]{1,0:T(4,128)(2,1)S(1)} collective-permute-done((bf16[3,6144]{1,0:T(4,128)(2,1)S(1)}, bf16[3,6144]{1,0:T(4,128)(2,1)S(1)}, u32[]{:S(2)}, u32[]{:S(2)}) %collective-permute-start) | collective-permute-done | bytes 36896 | tf_op jit(solution)/shard_map/ppermute | solution.py:466
  8.2 0.8 %shard_map.92 = (bf16[1040,128]{1,0:T(8,128)(2,1)S(1)}, f32[1024,128]{1,0:T(8,128)S(1)}, f32[8,128]{1,0:T(8,128)S(1)}, bf16[128,2048]{1,0:T(8,128)(2,1)S(1)}, bf16[128,512]{1,0:T(8,128)(2,1)S(1)}) custom-call(bf16[128,6144]{1,0:T(8,128)(2,1)S(1)} %get-tuple-element.58.refs_0_, bf16[3,6144]{1,0:T(4,128)(2,1)S(1)} %collective-permute-done.refs_1_, ...), custom_call_target="tpu_custom_call" | custom-call | flops 800000000 | bytes 2400000 | tf_op jit(solution)/shard_map/pallas_call | solution.py:65
  9.0 0.1 collective-permute-start.1
  9.0 0.8 %shard_map.93 = (bf16[1040,128]{1,0:T(8,128)(2,1)S(1)}, f32[1024,128]{1,0:T(8,128)S(1)}, f32[8,128]{1,0:T(8,128)S(1)}, bf16[128,2048]{1,0:T(8,128)(2,1)S(1)}, bf16[128,512]{1,0:T(8,128)(2,1)S(1)}) custom-call(bf16[128,6144]{1,0:T(8,128)(2,1)S(1)} %get-tuple-element.58.refs_0_, bf16[3,6144]{1,0:T(4,128)(2,1)S(1)} %collective-permute-done.refs_1_, ...), custom_call_target="tpu_custom_call" | custom-call | flops 800000000 | bytes 2400000 | tf_op jit(solution)/shard_map/pallas_call | solution.py:65
  9.8 0.5 %collective-permute-start.3 = (bf16[1040,128]{1,0:T(8,128)(2,1)S(1)}, bf16[1040,128]{1,0:T(8,128)(2,1)S(1)}, u32[]{:S(2)}, u32[]{:S(2)}) collective-permute-start(bf16[1040,128]{1,0:T(8,128)(2,1)S(1)} %get-tuple-element.81), channel_id=1, source_target_pairs={{0,1},{1,0},{2,3},{3,2},{4,5},{5,4},{6,7},{7,6},{8,9},{9,8},{10,11... | collective-permute-start | bytes 798728 | tf_op jit(solution)/shard_map/ppermute | solution.py:444
  10.4 0.0 copy-start.1
  10.4 0.5 %shard_map.94.refs_3_.refs_2_.refs_0_ = bf16[128,1024]{1,0:T(8,128)(2,1)S(1)} custom-call(bf16[128,6144]{1,0:T(8,128)(2,1)S(1)} %get-tuple-element.58.refs_0_, bf16[3,6144]{1,0:T(4,128)(2,1)S(1)} %collective-permute-done.refs_1_, bf16[4,6144]{1,0:T(4,128)(2,1)S(1)} %get-tuple-element.59.refs_2_, f32[1,6144]{1,0:T(1,128)S(1)} %get-tuple-element.60.refs_3_, ...), custom_call_target="tpu_custom_call" | custom-call | flops 600000000 | bytes 1800000 | tf_op jit(solution)/shard_map/pallas_call | solution.py:65
  10.9 0.0 collective-permute-done.1.refs_2_.refs_4_
  10.9 0.1 shard_map.95
  11.0 0.1 collective-permute-start.2
  11.1 0.4 %collective-permute-done.3.refs_2_.refs_4_ = bf16[1040,128]{1,0:T(8,128)(2,1)S(1)} collective-permute-done((bf16[1040,128]{1,0:T(8,128)(2,1)S(1)}, bf16[1040,128]{1,0:T(8,128)(2,1)S(1)}, u32[]{:S(2)}, u32[]{:S(2)}) %collective-permute-start.3) | collective-permute-done | bytes 266272 | tf_op jit(solution)/shard_map/ppermute | solution.py:444
  11.5 0.1 shard_map.96
  11.7 1.6 %collective-permute-start.5 = (bf16[528,128]{1,0:T(8,128)(2,1)S(1)}, bf16[528,128]{1,0:T(8,128)(2,1)S(1)}, u32[]{:S(2)}, u32[]{:S(2)}) collective-permute-start(bf16[528,128]{1,0:T(8,128)(2,1)S(1)} %get-tuple-element.88), channel_id=1, source_target_pairs={{0,2},{1,3},{2,0},{3,1},{4,6},{5,7},{6,4},{7,5},{8,10},{9,11},{10,... | collective-permute-start | bytes 405512 | tf_op jit(solution)/shard_map/ppermute | solution.py:444
  13.3 0.0 copy-done.1
  13.3 1.6 %shard_map.97 = (f32[128,2048]{1,0:T(8,128)S(1)}, f32[128,2048]{1,0:T(8,128)S(1)}) custom-call(bf16[128,2048]{1,0:T(8,128)(2,1)S(1)} %get-tuple-element.75.refs_0_, bf16[128,512]{1,0:T(8,128)(2,1)S(1)} %get-tuple-element.76.refs_1_, bf16[128,1024]{1,0:T(8,128)(2,1)S(1)} %shard_map.94.refs_3_.refs_2_.refs_0_, f32[128,128]{1,0:T(8,128)S(1)} %get-tuple-element.77.refs_3_, ...), custom_call_target="tpu_custom_call" | custom-call | flops 1680000000 | bytes 5040000 | tf_op jit(solution)/shard_map/pallas_call | solution.py:65
  14.9 2.6 %collective-permute-done.2.refs_2_.refs_5_ = bf16[528,128]{1,0:T(8,128)(2,1)S(1)} collective-permute-done((bf16[528,128]{1,0:T(8,128)(2,1)S(1)}, bf16[528,128]{1,0:T(8,128)(2,1)S(1)}, u32[]{:S(2)}, u32[]{:S(2)}) %collective-permute-start.2) | collective-permute-done | bytes 135200 | tf_op jit(solution)/shard_map/ppermute | solution.py:444
  17.5 0.1 shard_map.98
  17.6 0.2 collective-permute-start.4
  17.8 1.7 %shard_map.99 = (f32[128,2048]{1,0:T(8,128)S(1)}, f32[128,2048]{1,0:T(8,128)S(1)}) custom-call(bf16[128,2048]{1,0:T(8,128)(2,1)S(1)} %get-tuple-element.89.refs_0_, bf16[128,512]{1,0:T(8,128)(2,1)S(1)} %get-tuple-element.90.refs_1_, bf16[128,1024]{1,0:T(8,128)(2,1)S(1)} %shard_map.94.refs_3_.refs_2_.refs_0_, f32[128,128]{1,0:T(8,128)S(1)} %get-tuple-element.77.refs_3_, ...), custom_call_target="tpu_custom_call" | custom-call | flops 1680000000 | bytes 5040000 | tf_op jit(solution)/shard_map/pallas_call | solution.py:65
  19.5 0.0 collective-permute-done.5.refs_2_.refs_5_
  19.5 0.1 shard_map.100
  19.6 1.9 %collective-permute-start.7 = (bf16[528,128]{1,0:T(8,128)(2,1)S(1)}, bf16[528,128]{1,0:T(8,128)(2,1)S(1)}, u32[]{:S(2)}, u32[]{:S(2)}) collective-permute-start(bf16[528,128]{1,0:T(8,128)(2,1)S(1)} %get-tuple-element.97), channel_id=1, source_target_pairs={{0,4},{1,5},{2,6},{3,7},{4,0},{5,1},{6,2},{7,3},{8,12},{9,13},{10,... | collective-permute-start | bytes 405512 | tf_op jit(solution)/shard_map/ppermute | solution.py:444
  21.5 2.4 %collective-permute-done.4.refs_2_ = bf16[528,128]{1,0:T(8,128)(2,1)S(1)} collective-permute-done((bf16[528,128]{1,0:T(8,128)(2,1)S(1)}, bf16[528,128]{1,0:T(8,128)(2,1)S(1)}, u32[]{:S(2)}, u32[]{:S(2)}) %collective-permute-start.4) | collective-permute-done | bytes 135200 | tf_op jit(solution)/shard_map/ppermute | solution.py:444
  23.9 0.1 shard_map.101
  24.0 1.6 %collective-permute-start.6 = (bf16[512,128]{1,0:T(8,128)(2,1)S(1)}, bf16[512,128]{1,0:T(8,128)(2,1)S(1)}, u32[]{:S(2)}, u32[]{:S(2)}) collective-permute-start(bf16[512,128]{1,0:T(8,128)(2,1)S(1)} %get-tuple-element.93), channel_id=1, source_target_pairs={{0,12},{1,13},{2,14},{3,15},{4,8},{5,9},{6,10},{7,11},{8,4},{9,5},... | collective-permute-start | bytes 393224 | tf_op jit(solution)/shard_map/ppermute | solution.py:444
  25.6 1.4 %collective-permute-done.7.refs_2_ = bf16[528,128]{1,0:T(8,128)(2,1)S(1)} collective-permute-done((bf16[528,128]{1,0:T(8,128)(2,1)S(1)}, bf16[528,128]{1,0:T(8,128)(2,1)S(1)}, u32[]{:S(2)}, u32[]{:S(2)}) %collective-permute-start.7) | collective-permute-done | bytes 135200 | tf_op jit(solution)/shard_map/ppermute | solution.py:444
  26.9 0.1 shard_map.102
  27.0 1.5 %collective-permute-start.9 = (bf16[512,128]{1,0:T(8,128)(2,1)S(1)}, bf16[512,128]{1,0:T(8,128)(2,1)S(1)}, u32[]{:S(2)}, u32[]{:S(2)}) collective-permute-start(bf16[512,128]{1,0:T(8,128)(2,1)S(1)} %get-tuple-element.101), channel_id=1, source_target_pairs={{0,12},{1,13},{2,14},{3,15},{4,8},{5,9},{6,10},{7,11},{8,4},{9,5},... | collective-permute-start | bytes 393224 | tf_op jit(solution)/shard_map/ppermute | solution.py:444
  28.5 3.3 %collective-permute-done.6.refs_0_ = bf16[512,128]{1,0:T(8,128)(2,1)S(1)} collective-permute-done((bf16[512,128]{1,0:T(8,128)(2,1)S(1)}, bf16[512,128]{1,0:T(8,128)(2,1)S(1)}, u32[]{:S(2)}, u32[]{:S(2)}) %collective-permute-start.6) | collective-permute-done | bytes 131104 | tf_op jit(solution)/shard_map/ppermute | solution.py:444
  31.9 0.1 shard_map.103
  32.0 0.1 collective-permute-start.8
  32.0 1.9 %collective-permute-done.9.refs_0_ = bf16[512,128]{1,0:T(8,128)(2,1)S(1)} collective-permute-done((bf16[512,128]{1,0:T(8,128)(2,1)S(1)}, bf16[512,128]{1,0:T(8,128)(2,1)S(1)}, u32[]{:S(2)}, u32[]{:S(2)}) %collective-permute-start.9) | collective-permute-done | bytes 131104 | tf_op jit(solution)/shard_map/ppermute | solution.py:444
  33.9 0.1 shard_map.104
  34.0 0.0 copy-start
  34.1 0.2 collective-permute-start.10
  34.3 2.9 %collective-permute-done.8.refs_1_ = bf16[512,128]{1,0:T(8,128)(2,1)S(1)} collective-permute-done((bf16[512,128]{1,0:T(8,128)(2,1)S(1)}, bf16[512,128]{1,0:T(8,128)(2,1)S(1)}, u32[]{:S(2)}, u32[]{:S(2)}) %collective-permute-start.8) | collective-permute-done | bytes 131104 | tf_op jit(solution)/shard_map/ppermute | solution.py:444
  37.1 0.2 shard_map.105
  37.3 0.1 collective-permute-start.11
  37.3 1.7 %collective-permute-done.10.refs_1_ = bf16[512,128]{1,0:T(8,128)(2,1)S(1)} collective-permute-done((bf16[512,128]{1,0:T(8,128)(2,1)S(1)}, bf16[512,128]{1,0:T(8,128)(2,1)S(1)}, u32[]{:S(2)}, u32[]{:S(2)}) %collective-permute-start.10) | collective-permute-done | bytes 131104 | tf_op jit(solution)/shard_map/ppermute | solution.py:444
  39.1 0.2 shard_map.106
  39.3 0.1 collective-permute-start.12
  39.3 0.0 copy-done
  39.3 0.3 shard_map.107.refs_5_.refs_0_
  39.7 0.0 collective-permute-done.11.refs_1_
  39.7 0.3 shard_map.108.refs_5_.refs_1_
  40.0 0.3 shard_map.109.refs_2_.refs_8_
  40.3 0.5 %collective-permute-done.12.refs_4_ = bf16[1024,128]{1,0:T(8,128)(2,1)S(1)} collective-permute-done((bf16[1024,128]{1,0:T(8,128)(2,1)S(1)}, bf16[1024,128]{1,0:T(8,128)(2,1)S(1)}, u32[]{:S(2)}, u32[]{:S(2)}) %collective-permute-start.12) | collective-permute-done | bytes 262176 | tf_op jit(solution)/shard_map/ppermute | solution.py:444
  40.9 1.2 %shard_map.110 = bf16[128,4096]{1,0:T(8,128)(2,1)} custom-call(bf16[128,1024]{1,0:T(8,128)(2,1)S(1)} %shard_map.107.refs_5_.refs_0_, bf16[128,1024]{1,0:T(8,128)(2,1)S(1)} %shard_map.108.refs_5_.refs_1_, bf16[128,1024]{1,0:T(8,128)(2,1)S(1)} %shard_map.109.refs_2_.refs_8_, bf16[128,1024]{1,0:T(8,128)(2,1)S(1)} %shard_map.94.refs_3_.refs_2_.refs_0_, ...), custom_call_target="tpu_custom_call" | custom-call | flops 400000000 | bytes 1200000 | tf_op jit(solution)/shard_map/pallas_call | solution.py:65
Async XLA Ops:
  0.9 7.3 %collective-permute-start = (bf16[3,6144]{1,0:T(4,128)(2,1)S(1)}, bf16[3,6144]{1,0:T(4,128)(2,1)S(1)}, u32[]{:S(2)}, u32[]{:S(2)}) collective-permute-start(bf16[3,6144]{1,0:T(4,128)(2,1)S(1)} %slice.3), channel_id=1, source_target_pairs={{0,1},{1,2},{2,3},{3,4},{4,5},{5,6},{6,7},{7,8},{8,9},{9,10},{10,1... | collective-permute-start | bytes 110600 | tf_op jit(solution)/shard_map/ppermute | solution.py:466
  9.0 1.9 %collective-permute-start.1 = (bf16[1040,128]{1,0:T(8,128)(2,1)S(1)}, bf16[1040,128]{1,0:T(8,128)(2,1)S(1)}, u32[]{:S(2)}, u32[]{:S(2)}) collective-permute-start(bf16[1040,128]{1,0:T(8,128)(2,1)S(1)} %get-tuple-element.71), channel_id=1, source_target_pairs={{0,1},{1,0},{2,3},{3,2},{4,5},{5,4},{6,7},{7,6},{8,9},{9,8},{10,11... | collective-permute-start | bytes 798728 | tf_op jit(solution)/shard_map/ppermute | solution.py:444
  9.8 1.7 %collective-permute-start.3 = (bf16[1040,128]{1,0:T(8,128)(2,1)S(1)}, bf16[1040,128]{1,0:T(8,128)(2,1)S(1)}, u32[]{:S(2)}, u32[]{:S(2)}) collective-permute-start(bf16[1040,128]{1,0:T(8,128)(2,1)S(1)} %get-tuple-element.81), channel_id=1, source_target_pairs={{0,1},{1,0},{2,3},{3,2},{4,5},{5,4},{6,7},{7,6},{8,9},{9,8},{10,11... | collective-permute-start | bytes 798728 | tf_op jit(solution)/shard_map/ppermute | solution.py:444
  10.4 2.9 %copy-start.1 = (bf16[128,4096]{1,0:T(8,128)(2,1)S(1)}, bf16[128,4096]{1,0:T(8,128)(2,1)}, u32[]{:S(2)}) copy-start(bf16[128,4096]{1,0:T(8,128)(2,1)} %refs_8_.3) | copy-start | bytes 3145732
  11.0 6.5 %collective-permute-start.2 = (bf16[528,128]{1,0:T(8,128)(2,1)S(1)}, bf16[528,128]{1,0:T(8,128)(2,1)S(1)}, u32[]{:S(2)}, u32[]{:S(2)}) collective-permute-start(bf16[528,128]{1,0:T(8,128)(2,1)S(1)} %get-tuple-element.74), channel_id=1, source_target_pairs={{0,2},{1,3},{2,0},{3,1},{4,6},{5,7},{6,4},{7,5},{8,10},{9,11},{10,... | collective-permute-start | bytes 405512 | tf_op jit(solution)/shard_map/ppermute | solution.py:444
  11.7 7.9 %collective-permute-start.5 = (bf16[528,128]{1,0:T(8,128)(2,1)S(1)}, bf16[528,128]{1,0:T(8,128)(2,1)S(1)}, u32[]{:S(2)}, u32[]{:S(2)}) collective-permute-start(bf16[528,128]{1,0:T(8,128)(2,1)S(1)} %get-tuple-element.88), channel_id=1, source_target_pairs={{0,2},{1,3},{2,0},{3,1},{4,6},{5,7},{6,4},{7,5},{8,10},{9,11},{10,... | collective-permute-start | bytes 405512 | tf_op jit(solution)/shard_map/ppermute | solution.py:444
  17.6 6.3 %collective-permute-start.4 = (bf16[528,128]{1,0:T(8,128)(2,1)S(1)}, bf16[528,128]{1,0:T(8,128)(2,1)S(1)}, u32[]{:S(2)}, u32[]{:S(2)}) collective-permute-start(bf16[528,128]{1,0:T(8,128)(2,1)S(1)} %get-tuple-element.86), channel_id=1, source_target_pairs={{0,4},{1,5},{2,6},{3,7},{4,0},{5,1},{6,2},{7,3},{8,12},{9,13},{10,... | collective-permute-start | bytes 405512 | tf_op jit(solution)/shard_map/ppermute | solution.py:444
  19.6 7.3 %collective-permute-start.7 = (bf16[528,128]{1,0:T(8,128)(2,1)S(1)}, bf16[528,128]{1,0:T(8,128)(2,1)S(1)}, u32[]{:S(2)}, u32[]{:S(2)}) collective-permute-start(bf16[528,128]{1,0:T(8,128)(2,1)S(1)} %get-tuple-element.97), channel_id=1, source_target_pairs={{0,4},{1,5},{2,6},{3,7},{4,0},{5,1},{6,2},{7,3},{8,12},{9,13},{10,... | collective-permute-start | bytes 405512 | tf_op jit(solution)/shard_map/ppermute | solution.py:444
  24.0 7.9 %collective-permute-start.6 = (bf16[512,128]{1,0:T(8,128)(2,1)S(1)}, bf16[512,128]{1,0:T(8,128)(2,1)S(1)}, u32[]{:S(2)}, u32[]{:S(2)}) collective-permute-start(bf16[512,128]{1,0:T(8,128)(2,1)S(1)} %get-tuple-element.93), channel_id=1, source_target_pairs={{0,12},{1,13},{2,14},{3,15},{4,8},{5,9},{6,10},{7,11},{8,4},{9,5},... | collective-permute-start | bytes 393224 | tf_op jit(solution)/shard_map/ppermute | solution.py:444
  27.0 6.9 %collective-permute-start.9 = (bf16[512,128]{1,0:T(8,128)(2,1)S(1)}, bf16[512,128]{1,0:T(8,128)(2,1)S(1)}, u32[]{:S(2)}, u32[]{:S(2)}) collective-permute-start(bf16[512,128]{1,0:T(8,128)(2,1)S(1)} %get-tuple-element.101), channel_id=1, source_target_pairs={{0,12},{1,13},{2,14},{3,15},{4,8},{5,9},{6,10},{7,11},{8,4},{9,5},... | collective-permute-start | bytes 393224 | tf_op jit(solution)/shard_map/ppermute | solution.py:444
  32.0 5.1 %collective-permute-start.8 = (bf16[512,128]{1,0:T(8,128)(2,1)S(1)}, bf16[512,128]{1,0:T(8,128)(2,1)S(1)}, u32[]{:S(2)}, u32[]{:S(2)}) collective-permute-start(bf16[512,128]{1,0:T(8,128)(2,1)S(1)} %get-tuple-element.100), channel_id=1, source_target_pairs={{0,2},{1,3},{2,0},{3,1},{4,6},{5,7},{6,4},{7,5},{8,10},{9,11},{10,... | collective-permute-start | bytes 393224 | tf_op jit(solution)/shard_map/ppermute | solution.py:444
  34.0 5.3 %copy-start = (f32[4096]{0:T(1024)S(1)}, f32[4096]{0:T(1024)}, u32[]{:S(2)}) copy-start(f32[4096]{0:T(1024)} %param.17) | copy-start | bytes 49156
  34.1 5.0 %collective-permute-start.10 = (bf16[512,128]{1,0:T(8,128)(2,1)S(1)}, bf16[512,128]{1,0:T(8,128)(2,1)S(1)}, u32[]{:S(2)}, u32[]{:S(2)}) collective-permute-start(bf16[512,128]{1,0:T(8,128)(2,1)S(1)} %get-tuple-element.106), channel_id=1, source_target_pairs={{0,2},{1,3},{2,0},{3,1},{4,6},{5,7},{6,4},{7,5},{8,10},{9,11},{10,... | collective-permute-start | bytes 393224 | tf_op jit(solution)/shard_map/ppermute | solution.py:444
  37.3 2.4 %collective-permute-start.11 = (bf16[1024,128]{1,0:T(8,128)(2,1)S(1)}, bf16[1024,128]{1,0:T(8,128)(2,1)S(1)}, u32[]{:S(2)}, u32[]{:S(2)}) collective-permute-start(bf16[1024,128]{1,0:T(8,128)(2,1)S(1)} %get-tuple-element.108), channel_id=1, source_target_pairs={{0,1},{1,0},{2,3},{3,2},{4,5},{5,4},{6,7},{7,6},{8,9},{9,8},{10,11... | collective-permute-start | bytes 786440 | tf_op jit(solution)/shard_map/ppermute | solution.py:444
  39.3 1.6 %collective-permute-start.12 = (bf16[1024,128]{1,0:T(8,128)(2,1)S(1)}, bf16[1024,128]{1,0:T(8,128)(2,1)S(1)}, u32[]{:S(2)}, u32[]{:S(2)}) collective-permute-start(bf16[1024,128]{1,0:T(8,128)(2,1)S(1)} %get-tuple-element.110), channel_id=1, source_target_pairs={{0,1},{1,0},{2,3},{3,2},{4,5},{5,4},{6,7},{7,6},{8,9},{9,8},{10,11... | collective-permute-start | bytes 786440 | tf_op jit(solution)/shard_map/ppermute | solution.py:444

commit v6 on v5

--- a/solution.py
+++ b/solution.py
@@ -429,7 +429,7 @@
 
 
 ORDER = (
-    "I0", "I1", "R0", "A0", "A1", "W0", "B0", "W1", "B1", "C0", "C1", "S0", "S1",
+    "I0", "I1", "A0", "A1", "B0", "R0", "W0", "B1", "C0", "C1", "W1", "S0", "S1",
     "H0", "H1", "E0", "F0", "E1", "F1",
 )
 

time: 42.3 us -> 42 us (level)
  waiting for transfers between devices: 20.8 us -> 19.9 us
  starting transfers between devices: 8.48 us -> 9.07 us
    ppermute x12, waiting for transfers between devices: 17.2 us -> 16.2 us  [across(): lax.ppermute(value, 'seq', [(i, i ^ flipped) for i in range(devices)])]
    ppermute x12, starting transfers between devices: 7.97 us -> 8.56 us  [across(): lax.ppermute(value, 'seq', [(i, i ^ flipped) for i in range(devices)])]
  transfers between devices with their start and end apart: 13 -> 13, of which waited for: 10 -> 11; matrix products, arithmetic and copies ran while one was open for 0% -> 0% of each run, Pallas kernels for 23% -> 23%
where the time goes in v6:
time: 42 us; the launch traced here: 41.7 us
  waiting for transfers between devices  19.9 us (47%)
  Pallas kernels  11.6 us (28%)
  starting transfers between devices  9.07 us (22%)
  local copies, waits for them, and re-layouts  0.93 us (2%)
    ppermute x12, waiting for transfers between devices, across(): lax.ppermute(value, 'seq', [(i, i ^ flipped) for i in range(devices)])  16.2 us
    pallas_call x20, Pallas kernels, call(): pl.pallas_call(kernel, out_shape=[space(shape, kind) for shape, kind, spa...  11.6 us
    ppermute x12, starting transfers between devices, across(): lax.ppermute(value, 'seq', [(i, i ^ flipped) for i in range(devices)])  8.56 us
    ppermute x1, waiting for transfers between devices, shards(): lax.ppermute(mixer_input[SPAN - 3:], 'seq', [(i, (i + 1) % devices) for i...  3.66 us
    slice x1, local copies, waits for them, and re-layouts, shards(): mixer_input[SPAN - 3:]  0.92 us
  transfers between devices with their start and end apart: 13, of which 11 were waited for; matrix products, arithmetic and copies ran while one was open for 0% of the time, Pallas kernels for 23%

profile of v6, /device:TPU:0, one launch (start us, length us, event | category | flops | bytes accessed | tf_op | source)
XLA Modules:
  0.0 41.7 jit_solution(1510798695590325809)
XLA Ops:
  0.0 0.9 %slice.3 = bf16[3,6144]{1,0:T(4,128)(2,1)S(1)} slice(bf16[128,6144]{1,0:T(8,128)(2,1)} %refs_0_.1), slice={[125:128], [0:6144]} | slice | bytes 73728 | tf_op jit(solution)/shard_map/slice | solution.py:466
  0.9 0.5 %collective-permute-start = (bf16[3,6144]{1,0:T(4,128)(2,1)S(1)}, bf16[3,6144]{1,0:T(4,128)(2,1)S(1)}, u32[]{:S(2)}, u32[]{:S(2)}) collective-permute-start(bf16[3,6144]{1,0:T(4,128)(2,1)S(1)} %slice.3), channel_id=1, source_target_pairs={{0,1},{1,2},{2,3},{3,4},{4,5},{5,6},{6,7},{7,8},{8,9},{9,10},{10,1... | collective-permute-start | bytes 110600 | tf_op jit(solution)/shard_map/ppermute | solution.py:466
  1.4 3.1 %shard_map.91 = (bf16[128,6144]{1,0:T(8,128)(2,1)S(1)}, bf16[4,6144]{1,0:T(4,128)(2,1)S(1)}, f32[1,6144]{1,0:T(1,128)S(1)}, f32[128,128]{1,0:T(8,128)S(1)}, f32[...) custom-call(bf16[128,6144]{1,0:T(8,128)(2,1)} %refs_0_.1, ...), custom_call_target="tpu_custom_call" | custom-call | flops 2500000000 | bytes 7500000 | tf_op jit(solution)/shard_map/pallas_call | solution.py:65
  4.5 3.7 %collective-permute-done.refs_1_ = bf16[3,6144]{1,0:T(4,128)(2,1)S(1)} collective-permute-done((bf16[3,6144]{1,0:T(4,128)(2,1)S(1)}, bf16[3,6144]{1,0:T(4,128)(2,1)S(1)}, u32[]{:S(2)}, u32[]{:S(2)}) %collective-permute-start) | collective-permute-done | bytes 36896 | tf_op jit(solution)/shard_map/ppermute | solution.py:466
  8.2 0.8 %shard_map.92 = (bf16[1040,128]{1,0:T(8,128)(2,1)S(1)}, f32[1024,128]{1,0:T(8,128)S(1)}, f32[8,128]{1,0:T(8,128)S(1)}, bf16[128,2048]{1,0:T(8,128)(2,1)S(1)}, bf16[128,512]{1,0:T(8,128)(2,1)S(1)}) custom-call(bf16[128,6144]{1,0:T(8,128)(2,1)S(1)} %get-tuple-element.58.refs_0_, bf16[3,6144]{1,0:T(4,128)(2,1)S(1)} %collective-permute-done.refs_1_, ...), custom_call_target="tpu_custom_call" | custom-call | flops 800000000 | bytes 2400000 | tf_op jit(solution)/shard_map/pallas_call | solution.py:65
  9.0 0.1 collective-permute-start.1
  9.0 0.8 %shard_map.93 = (bf16[1040,128]{1,0:T(8,128)(2,1)S(1)}, f32[1024,128]{1,0:T(8,128)S(1)}, f32[8,128]{1,0:T(8,128)S(1)}, bf16[128,2048]{1,0:T(8,128)(2,1)S(1)}, bf16[128,512]{1,0:T(8,128)(2,1)S(1)}) custom-call(bf16[128,6144]{1,0:T(8,128)(2,1)S(1)} %get-tuple-element.58.refs_0_, bf16[3,6144]{1,0:T(4,128)(2,1)S(1)} %collective-permute-done.refs_1_, ...), custom_call_target="tpu_custom_call" | custom-call | flops 800000000 | bytes 2400000 | tf_op jit(solution)/shard_map/pallas_call | solution.py:65
  9.8 0.5 %collective-permute-start.3 = (bf16[1040,128]{1,0:T(8,128)(2,1)S(1)}, bf16[1040,128]{1,0:T(8,128)(2,1)S(1)}, u32[]{:S(2)}, u32[]{:S(2)}) collective-permute-start(bf16[1040,128]{1,0:T(8,128)(2,1)S(1)} %get-tuple-element.76), channel_id=1, source_target_pairs={{0,1},{1,0},{2,3},{3,2},{4,5},{5,4},{6,7},{7,6},{8,9},{9,8},{10,11... | collective-permute-start | bytes 798728 | tf_op jit(solution)/shard_map/ppermute | solution.py:444
  10.4 0.2 collective-permute-done.1.refs_2_.refs_4_
  10.6 0.1 shard_map.94
  10.7 0.2 collective-permute-start.2
  10.9 0.6 %collective-permute-done.3.refs_2_.refs_4_ = bf16[1040,128]{1,0:T(8,128)(2,1)S(1)} collective-permute-done((bf16[1040,128]{1,0:T(8,128)(2,1)S(1)}, bf16[1040,128]{1,0:T(8,128)(2,1)S(1)}, u32[]{:S(2)}, u32[]{:S(2)}) %collective-permute-start.3) | collective-permute-done | bytes 266272 | tf_op jit(solution)/shard_map/ppermute | solution.py:444
  11.5 0.0 copy-start.1
  11.6 0.1 shard_map.95
  11.7 1.3 %collective-permute-start.5 = (bf16[528,128]{1,0:T(8,128)(2,1)S(1)}, bf16[528,128]{1,0:T(8,128)(2,1)S(1)}, u32[]{:S(2)}, u32[]{:S(2)}) collective-permute-start(bf16[528,128]{1,0:T(8,128)(2,1)S(1)} %get-tuple-element.82), channel_id=1, source_target_pairs={{0,2},{1,3},{2,0},{3,1},{4,6},{5,7},{6,4},{7,5},{8,10},{9,11},{10,... | collective-permute-start | bytes 405512 | tf_op jit(solution)/shard_map/ppermute | solution.py:444
  13.0 4.2 %collective-permute-done.2.refs_2_.refs_5_ = bf16[528,128]{1,0:T(8,128)(2,1)S(1)} collective-permute-done((bf16[528,128]{1,0:T(8,128)(2,1)S(1)}, bf16[528,128]{1,0:T(8,128)(2,1)S(1)}, u32[]{:S(2)}, u32[]{:S(2)}) %collective-permute-start.2) | collective-permute-done | bytes 135200 | tf_op jit(solution)/shard_map/ppermute | solution.py:444
  17.2 0.1 shard_map.96
  17.3 0.3 collective-permute-start.4
  17.5 0.5 %shard_map.97.refs_2_.refs_9_.refs_0_.refs_3_ = bf16[128,1024]{1,0:T(8,128)(2,1)S(1)} custom-call(bf16[128,6144]{1,0:T(8,128)(2,1)S(1)} %get-tuple-element.58.refs_0_, bf16[3,6144]{1,0:T(4,128)(2,1)S(1)} %collective-permute-done.refs_1_, bf16[4,6144]{1,0:T(4,128)(2,1)S(1)} %get-tuple-element.59.refs_2_, f32[1,6144]{1,0:T(1,128)S(1)} %get-tuple-element.60.refs_3_, ...), custom_call_target="tpu_custom_call" | custom-call | flops 600000000 | bytes 1800000 | tf_op jit(solution)/shard_map/pallas_call | solution.py:65
  18.0 0.0 copy-done.1
  18.0 1.7 %shard_map.98 = (f32[128,2048]{1,0:T(8,128)S(1)}, f32[128,2048]{1,0:T(8,128)S(1)}) custom-call(bf16[128,2048]{1,0:T(8,128)(2,1)S(1)} %get-tuple-element.83.refs_0_, bf16[128,512]{1,0:T(8,128)(2,1)S(1)} %get-tuple-element.84.refs_1_, bf16[128,1024]{1,0:T(8,128)(2,1)S(1)} %shard_map.97.refs_2_.refs_9_.refs_0_.refs_3_, ...), custom_call_target="tpu_custom_call" | custom-call | flops 1680000000 | bytes 5040000 | tf_op jit(solution)/shard_map/pallas_call | solution.py:65
  19.7 0.0 collective-permute-done.5.refs_2_.refs_5_
  19.7 0.1 shard_map.99
  19.8 1.9 %collective-permute-start.7 = (bf16[528,128]{1,0:T(8,128)(2,1)S(1)}, bf16[528,128]{1,0:T(8,128)(2,1)S(1)}, u32[]{:S(2)}, u32[]{:S(2)}) collective-permute-start(bf16[528,128]{1,0:T(8,128)(2,1)S(1)} %get-tuple-element.96), channel_id=1, source_target_pairs={{0,4},{1,5},{2,6},{3,7},{4,0},{5,1},{6,2},{7,3},{8,12},{9,13},{10,... | collective-permute-start | bytes 405512 | tf_op jit(solution)/shard_map/ppermute | solution.py:444
  21.7 1.8 %collective-permute-done.4.refs_2_ = bf16[528,128]{1,0:T(8,128)(2,1)S(1)} collective-permute-done((bf16[528,128]{1,0:T(8,128)(2,1)S(1)}, bf16[528,128]{1,0:T(8,128)(2,1)S(1)}, u32[]{:S(2)}, u32[]{:S(2)}) %collective-permute-start.4) | collective-permute-done | bytes 135200 | tf_op jit(solution)/shard_map/ppermute | solution.py:444
  23.4 0.1 shard_map.100
  23.5 1.7 %collective-permute-start.6 = (bf16[512,128]{1,0:T(8,128)(2,1)S(1)}, bf16[512,128]{1,0:T(8,128)(2,1)S(1)}, u32[]{:S(2)}, u32[]{:S(2)}) collective-permute-start(bf16[512,128]{1,0:T(8,128)(2,1)S(1)} %get-tuple-element.90), channel_id=1, source_target_pairs={{0,12},{1,13},{2,14},{3,15},{4,8},{5,9},{6,10},{7,11},{8,4},{9,5},... | collective-permute-start | bytes 393224 | tf_op jit(solution)/shard_map/ppermute | solution.py:444
  25.2 1.4 %collective-permute-done.7.refs_2_ = bf16[528,128]{1,0:T(8,128)(2,1)S(1)} collective-permute-done((bf16[528,128]{1,0:T(8,128)(2,1)S(1)}, bf16[528,128]{1,0:T(8,128)(2,1)S(1)}, u32[]{:S(2)}, u32[]{:S(2)}) %collective-permute-start.7) | collective-permute-done | bytes 135200 | tf_op jit(solution)/shard_map/ppermute | solution.py:444
  26.6 0.1 shard_map.101
  26.7 1.5 %collective-permute-start.9 = (bf16[512,128]{1,0:T(8,128)(2,1)S(1)}, bf16[512,128]{1,0:T(8,128)(2,1)S(1)}, u32[]{:S(2)}, u32[]{:S(2)}) collective-permute-start(bf16[512,128]{1,0:T(8,128)(2,1)S(1)} %get-tuple-element.101), channel_id=1, source_target_pairs={{0,12},{1,13},{2,14},{3,15},{4,8},{5,9},{6,10},{7,11},{8,4},{9,5},... | collective-permute-start | bytes 393224 | tf_op jit(solution)/shard_map/ppermute | solution.py:444
  28.2 1.7 %shard_map.102 = (f32[128,2048]{1,0:T(8,128)S(1)}, f32[128,2048]{1,0:T(8,128)S(1)}) custom-call(bf16[128,2048]{1,0:T(8,128)(2,1)S(1)} %get-tuple-element.93.refs_0_, bf16[128,512]{1,0:T(8,128)(2,1)S(1)} %get-tuple-element.94.refs_1_, bf16[128,1024]{1,0:T(8,128)(2,1)S(1)} %shard_map.97.refs_2_.refs_9_.refs_0_.refs_3_, ...), custom_call_target="tpu_custom_call" | custom-call | flops 1680000000 | bytes 5040000 | tf_op jit(solution)/shard_map/pallas_call | solution.py:65
  29.9 1.8 %collective-permute-done.6.refs_0_ = bf16[512,128]{1,0:T(8,128)(2,1)S(1)} collective-permute-done((bf16[512,128]{1,0:T(8,128)(2,1)S(1)}, bf16[512,128]{1,0:T(8,128)(2,1)S(1)}, u32[]{:S(2)}, u32[]{:S(2)}) %collective-permute-start.6) | collective-permute-done | bytes 131104 | tf_op jit(solution)/shard_map/ppermute | solution.py:444
  31.7 0.1 shard_map.103
  31.8 0.4 %collective-permute-start.8 = (bf16[512,128]{1,0:T(8,128)(2,1)S(1)}, bf16[512,128]{1,0:T(8,128)(2,1)S(1)}, u32[]{:S(2)}, u32[]{:S(2)}) collective-permute-start(bf16[512,128]{1,0:T(8,128)(2,1)S(1)} %get-tuple-element.100), channel_id=1, source_target_pairs={{0,2},{1,3},{2,0},{3,1},{4,6},{5,7},{6,4},{7,5},{8,10},{9,11},{10,... | collective-permute-start | bytes 393224 | tf_op jit(solution)/shard_map/ppermute | solution.py:444
  32.2 1.4 %collective-permute-done.9.refs_0_ = bf16[512,128]{1,0:T(8,128)(2,1)S(1)} collective-permute-done((bf16[512,128]{1,0:T(8,128)(2,1)S(1)}, bf16[512,128]{1,0:T(8,128)(2,1)S(1)}, u32[]{:S(2)}, u32[]{:S(2)}) %collective-permute-start.9) | collective-permute-done | bytes 131104 | tf_op jit(solution)/shard_map/ppermute | solution.py:444
  33.6 0.1 shard_map.104
  33.7 0.0 copy-start
  33.7 0.4 %collective-permute-start.10 = (bf16[512,128]{1,0:T(8,128)(2,1)S(1)}, bf16[512,128]{1,0:T(8,128)(2,1)S(1)}, u32[]{:S(2)}, u32[]{:S(2)}) collective-permute-start(bf16[512,128]{1,0:T(8,128)(2,1)S(1)} %get-tuple-element.106), channel_id=1, source_target_pairs={{0,2},{1,3},{2,0},{3,1},{4,6},{5,7},{6,4},{7,5},{8,10},{9,11},{10,... | collective-permute-start | bytes 393224 | tf_op jit(solution)/shard_map/ppermute | solution.py:444
  34.2 3.0 %collective-permute-done.8.refs_1_ = bf16[512,128]{1,0:T(8,128)(2,1)S(1)} collective-permute-done((bf16[512,128]{1,0:T(8,128)(2,1)S(1)}, bf16[512,128]{1,0:T(8,128)(2,1)S(1)}, u32[]{:S(2)}, u32[]{:S(2)}) %collective-permute-start.8) | collective-permute-done | bytes 131104 | tf_op jit(solution)/shard_map/ppermute | solution.py:444
  37.2 0.2 shard_map.105
  37.4 0.1 collective-permute-start.11
  37.4 1.3 %collective-permute-done.10.refs_1_ = bf16[512,128]{1,0:T(8,128)(2,1)S(1)} collective-permute-done((bf16[512,128]{1,0:T(8,128)(2,1)S(1)}, bf16[512,128]{1,0:T(8,128)(2,1)S(1)}, u32[]{:S(2)}, u32[]{:S(2)}) %collective-permute-start.10) | collective-permute-done | bytes 131104 | tf_op jit(solution)/shard_map/ppermute | solution.py:444
  38.8 0.2 shard_map.106
  38.9 0.1 collective-permute-start.12
  39.0 0.0 copy-done
  39.0 0.3 shard_map.107.refs_5_.refs_0_
  39.3 0.0 collective-permute-done.11.refs_1_
  39.3 0.3 shard_map.108.refs_5_.refs_1_
  39.7 0.3 shard_map.109.refs_2_.refs_8_
  40.0 0.5 %collective-permute-done.12.refs_4_ = bf16[1024,128]{1,0:T(8,128)(2,1)S(1)} collective-permute-done((bf16[1024,128]{1,0:T(8,128)(2,1)S(1)}, bf16[1024,128]{1,0:T(8,128)(2,1)S(1)}, u32[]{:S(2)}, u32[]{:S(2)}) %collective-permute-start.12) | collective-permute-done | bytes 262176 | tf_op jit(solution)/shard_map/ppermute | solution.py:444
  40.5 1.2 %shard_map.110 = bf16[128,4096]{1,0:T(8,128)(2,1)} custom-call(bf16[128,1024]{1,0:T(8,128)(2,1)S(1)} %shard_map.107.refs_5_.refs_0_, bf16[128,1024]{1,0:T(8,128)(2,1)S(1)} %shard_map.108.refs_5_.refs_1_, bf16[128,1024]{1,0:T(8,128)(2,1)S(1)} %shard_map.109.refs_2_.refs_8_, bf16[128,1024]{1,0:T(8,128)(2,1)S(1)} %shard_map.97.refs_2_.refs_9_.refs_0_.refs_3_, ...), custom_call_target="tpu_custom_call" | custom-call | flops 400000000 | bytes 1200000 | tf_op jit(solution)/shard_map/pallas_call | solution.py:65
Async XLA Ops:
  0.9 7.3 %collective-permute-start = (bf16[3,6144]{1,0:T(4,128)(2,1)S(1)}, bf16[3,6144]{1,0:T(4,128)(2,1)S(1)}, u32[]{:S(2)}, u32[]{:S(2)}) collective-permute-start(bf16[3,6144]{1,0:T(4,128)(2,1)S(1)} %slice.3), channel_id=1, source_target_pairs={{0,1},{1,2},{2,3},{3,4},{4,5},{5,6},{6,7},{7,8},{8,9},{9,10},{10,1... | collective-permute-start | bytes 110600 | tf_op jit(solution)/shard_map/ppermute | solution.py:466
  9.0 1.6 %collective-permute-start.1 = (bf16[1040,128]{1,0:T(8,128)(2,1)S(1)}, bf16[1040,128]{1,0:T(8,128)(2,1)S(1)}, u32[]{:S(2)}, u32[]{:S(2)}) collective-permute-start(bf16[1040,128]{1,0:T(8,128)(2,1)S(1)} %get-tuple-element.68), channel_id=1, source_target_pairs={{0,1},{1,0},{2,3},{3,2},{4,5},{5,4},{6,7},{7,6},{8,9},{9,8},{10,11... | collective-permute-start | bytes 798728 | tf_op jit(solution)/shard_map/ppermute | solution.py:444
  9.8 1.7 %collective-permute-start.3 = (bf16[1040,128]{1,0:T(8,128)(2,1)S(1)}, bf16[1040,128]{1,0:T(8,128)(2,1)S(1)}, u32[]{:S(2)}, u32[]{:S(2)}) collective-permute-start(bf16[1040,128]{1,0:T(8,128)(2,1)S(1)} %get-tuple-element.76), channel_id=1, source_target_pairs={{0,1},{1,0},{2,3},{3,2},{4,5},{5,4},{6,7},{7,6},{8,9},{9,8},{10,11... | collective-permute-start | bytes 798728 | tf_op jit(solution)/shard_map/ppermute | solution.py:444
  10.7 6.5 %collective-permute-start.2 = (bf16[528,128]{1,0:T(8,128)(2,1)S(1)}, bf16[528,128]{1,0:T(8,128)(2,1)S(1)}, u32[]{:S(2)}, u32[]{:S(2)}) collective-permute-start(bf16[528,128]{1,0:T(8,128)(2,1)S(1)} %get-tuple-element.74), channel_id=1, source_target_pairs={{0,2},{1,3},{2,0},{3,1},{4,6},{5,7},{6,4},{7,5},{8,10},{9,11},{10,... | collective-permute-start | bytes 405512 | tf_op jit(solution)/shard_map/ppermute | solution.py:444
  11.5 6.5 %copy-start.1 = (bf16[128,4096]{1,0:T(8,128)(2,1)S(1)}, bf16[128,4096]{1,0:T(8,128)(2,1)}, u32[]{:S(2)}) copy-start(bf16[128,4096]{1,0:T(8,128)(2,1)} %refs_8_.3) | copy-start | bytes 3145732
  11.7 8.0 %collective-permute-start.5 = (bf16[528,128]{1,0:T(8,128)(2,1)S(1)}, bf16[528,128]{1,0:T(8,128)(2,1)S(1)}, u32[]{:S(2)}, u32[]{:S(2)}) collective-permute-start(bf16[528,128]{1,0:T(8,128)(2,1)S(1)} %get-tuple-element.82), channel_id=1, source_target_pairs={{0,2},{1,3},{2,0},{3,1},{4,6},{5,7},{6,4},{7,5},{8,10},{9,11},{10,... | collective-permute-start | bytes 405512 | tf_op jit(solution)/shard_map/ppermute | solution.py:444
  17.3 6.2 %collective-permute-start.4 = (bf16[528,128]{1,0:T(8,128)(2,1)S(1)}, bf16[528,128]{1,0:T(8,128)(2,1)S(1)}, u32[]{:S(2)}, u32[]{:S(2)}) collective-permute-start(bf16[528,128]{1,0:T(8,128)(2,1)S(1)} %get-tuple-element.80), channel_id=1, source_target_pairs={{0,4},{1,5},{2,6},{3,7},{4,0},{5,1},{6,2},{7,3},{8,12},{9,13},{10,... | collective-permute-start | bytes 405512 | tf_op jit(solution)/shard_map/ppermute | solution.py:444
  19.8 6.9 %collective-permute-start.7 = (bf16[528,128]{1,0:T(8,128)(2,1)S(1)}, bf16[528,128]{1,0:T(8,128)(2,1)S(1)}, u32[]{:S(2)}, u32[]{:S(2)}) collective-permute-start(bf16[528,128]{1,0:T(8,128)(2,1)S(1)} %get-tuple-element.96), channel_id=1, source_target_pairs={{0,4},{1,5},{2,6},{3,7},{4,0},{5,1},{6,2},{7,3},{8,12},{9,13},{10,... | collective-permute-start | bytes 405512 | tf_op jit(solution)/shard_map/ppermute | solution.py:444
  23.5 8.2 %collective-permute-start.6 = (bf16[512,128]{1,0:T(8,128)(2,1)S(1)}, bf16[512,128]{1,0:T(8,128)(2,1)S(1)}, u32[]{:S(2)}, u32[]{:S(2)}) collective-permute-start(bf16[512,128]{1,0:T(8,128)(2,1)S(1)} %get-tuple-element.90), channel_id=1, source_target_pairs={{0,12},{1,13},{2,14},{3,15},{4,8},{5,9},{6,10},{7,11},{8,4},{9,5},... | collective-permute-start | bytes 393224 | tf_op jit(solution)/shard_map/ppermute | solution.py:444
  26.7 6.9 %collective-permute-start.9 = (bf16[512,128]{1,0:T(8,128)(2,1)S(1)}, bf16[512,128]{1,0:T(8,128)(2,1)S(1)}, u32[]{:S(2)}, u32[]{:S(2)}) collective-permute-start(bf16[512,128]{1,0:T(8,128)(2,1)S(1)} %get-tuple-element.101), channel_id=1, source_target_pairs={{0,12},{1,13},{2,14},{3,15},{4,8},{5,9},{6,10},{7,11},{8,4},{9,5},... | collective-permute-start | bytes 393224 | tf_op jit(solution)/shard_map/ppermute | solution.py:444
  31.8 5.4 %collective-permute-start.8 = (bf16[512,128]{1,0:T(8,128)(2,1)S(1)}, bf16[512,128]{1,0:T(8,128)(2,1)S(1)}, u32[]{:S(2)}, u32[]{:S(2)}) collective-permute-start(bf16[512,128]{1,0:T(8,128)(2,1)S(1)} %get-tuple-element.100), channel_id=1, source_target_pairs={{0,2},{1,3},{2,0},{3,1},{4,6},{5,7},{6,4},{7,5},{8,10},{9,11},{10,... | collective-permute-start | bytes 393224 | tf_op jit(solution)/shard_map/ppermute | solution.py:444
  33.7 5.3 %copy-start = (f32[4096]{0:T(1024)S(1)}, f32[4096]{0:T(1024)}, u32[]{:S(2)}) copy-start(f32[4096]{0:T(1024)} %param.17) | copy-start | bytes 49156
  33.7 5.0 %collective-permute-start.10 = (bf16[512,128]{1,0:T(8,128)(2,1)S(1)}, bf16[512,128]{1,0:T(8,128)(2,1)S(1)}, u32[]{:S(2)}, u32[]{:S(2)}) collective-permute-start(bf16[512,128]{1,0:T(8,128)(2,1)S(1)} %get-tuple-element.106), channel_id=1, source_target_pairs={{0,2},{1,3},{2,0},{3,1},{4,6},{5,7},{6,4},{7,5},{8,10},{9,11},{10,... | collective-permute-start | bytes 393224 | tf_op jit(solution)/shard_map/ppermute | solution.py:444
  37.4 2.0 %collective-permute-start.11 = (bf16[1024,128]{1,0:T(8,128)(2,1)S(1)}, bf16[1024,128]{1,0:T(8,128)(2,1)S(1)}, u32[]{:S(2)}, u32[]{:S(2)}) collective-permute-start(bf16[1024,128]{1,0:T(8,128)(2,1)S(1)} %get-tuple-element.108), channel_id=1, source_target_pairs={{0,1},{1,0},{2,3},{3,2},{4,5},{5,4},{6,7},{7,6},{8,9},{9,8},{10,11... | collective-permute-start | bytes 786440 | tf_op jit(solution)/shard_map/ppermute | solution.py:444
  38.9 1.6 %collective-permute-start.12 = (bf16[1024,128]{1,0:T(8,128)(2,1)S(1)}, bf16[1024,128]{1,0:T(8,128)(2,1)S(1)}, u32[]{:S(2)}, u32[]{:S(2)}) collective-permute-start(bf16[1024,128]{1,0:T(8,128)(2,1)S(1)} %get-tuple-element.110), channel_id=1, source_target_pairs={{0,1},{1,0},{2,3},{3,2},{4,5},{5,4},{6,7},{7,6},{8,9},{9,8},{10,11... | collective-permute-start | bytes 786440 | tf_op jit(solution)/shard_map/ppermute | solution.py:444

commit v7 on v6

--- a/solution.py
+++ b/solution.py
@@ -146,6 +146,13 @@
             here[5:8, :] = jnp.where(first, 0.0, halo[:, cols].astype(F32))
             here[8:24, :] = source[0:16, cols].astype(F32)
             out[0:16, columns(i, block)] = convolve_into(16, here, weight, bias, cols)
+
+
+def take_last_rows(x, out, rows, sems):
+    copy = pltpu.make_async_copy(x.at[SPAN - 16 : SPAN, :], rows, sems.at[0])
+    copy.start()
+    copy.wait()
+    out[...] = rows[...].astype(F32)[13:16, :].astype(BF16)
 
 
 def prepare(
@@ -463,7 +470,11 @@
     def quarter(p):
         return [vmem(p.quarter_rows, LANES, F32), decays_of(p.quarter_tiles)]
 
-    halo = lax.ppermute(mixer_input[SPAN - 3 :], "seq", [(i, (i + 1) % devices) for i in range(devices)])
+    (last_rows,) = call(
+        take_last_rows, [vmem(3, CONV_COLS, BF16)], mixer_input, hbm=(0,),
+        scratch=[pltpu.VMEM((16, CONV_COLS), BF16), pltpu.SemaphoreType.DMA((1,))],
+    )
+    halo = lax.ppermute(last_rows, "seq", [(i, (i + 1) % devices) for i in range(devices)])
     held, weight, bias, both, both_t, tail_pair, carry_pair, row_pair, spread, *raw = call(
         functools.partial(prepare, parts),
         [

time: 42 us -> 42 us (level)
  Pallas kernels: 11.6 us -> 12.6 us
  local copies, waits for them, and re-layouts: 0.93 us -> 0.01 us
    pallas_call x20 -> x21, Pallas kernels: 11.6 us -> 12.6 us  [call(): pl.pallas_call(kernel, out_shape=[space(shape, kind) for shape, kind, spa...]
    slice x1 -> x0, local copies, waits for them, and re-layouts: 0.92 us -> none  [shards(): mixer_input[SPAN - 3:]]
where the time goes in v7:
time: 42 us; the launch traced here: 41.7 us
  waiting for transfers between devices  20 us (48%)
  Pallas kernels  12.6 us (30%)
  starting transfers between devices  9.01 us (21%)
    ppermute x12, waiting for transfers between devices, across(): lax.ppermute(value, 'seq', [(i, i ^ flipped) for i in range(devices)])  16.3 us
    pallas_call x21, Pallas kernels, call(): pl.pallas_call(kernel, out_shape=[space(shape, kind) for shape, kind, spa...  12.6 us
    ppermute x12, starting transfers between devices, across(): lax.ppermute(value, 'seq', [(i, i ^ flipped) for i in range(devices)])  8.51 us
    ppermute x1, waiting for transfers between devices, shards(): lax.ppermute(last_rows, 'seq', [(i, (i + 1) % devices) for i in range(dev...  3.66 us
  transfers between devices with their start and end apart: 13, of which 11 were waited for; matrix products, arithmetic and copies ran while one was open for 0% of the time, Pallas kernels for 23%

profile of v7, /device:TPU:0, one launch (start us, length us, event | category | flops | bytes accessed | tf_op | source)
XLA Modules:
  0.0 41.7 jit_solution(477515749516945831)
XLA Ops:
  0.0 1.0 %shard_map.92 = bf16[3,6144]{1,0:T(4,128)(2,1)S(1)} custom-call(bf16[128,6144]{1,0:T(8,128)(2,1)} %refs_0_.3), custom_call_target="tpu_custom_call" | custom-call | flops 100000000 | bytes 300000 | tf_op jit(solution)/shard_map/pallas_call | solution.py:65
  1.0 0.5 %collective-permute-start = (bf16[3,6144]{1,0:T(4,128)(2,1)S(1)}, bf16[3,6144]{1,0:T(4,128)(2,1)S(1)}, u32[]{:S(2)}, u32[]{:S(2)}) collective-permute-start(bf16[3,6144]{1,0:T(4,128)(2,1)S(1)} %shard_map.92), channel_id=1, source_target_pairs={{0,1},{1,2},{2,3},{3,4},{4,5},{5,6},{6,7},{7,8},{8,9},{9,10},{10,1... | collective-permute-start | bytes 110600 | tf_op jit(solution)/shard_map/ppermute | solution.py:477
  1.5 3.1 %shard_map.91 = (bf16[128,6144]{1,0:T(8,128)(2,1)S(1)}, bf16[4,6144]{1,0:T(4,128)(2,1)S(1)}, f32[1,6144]{1,0:T(1,128)S(1)}, f32[128,128]{1,0:T(8,128)S(1)}, f32[...) custom-call(bf16[128,6144]{1,0:T(8,128)(2,1)} %refs_0_.3, ...), custom_call_target="tpu_custom_call" | custom-call | flops 2500000000 | bytes 7500000 | tf_op jit(solution)/shard_map/pallas_call | solution.py:65
  4.6 3.7 %collective-permute-done.refs_1_ = bf16[3,6144]{1,0:T(4,128)(2,1)S(1)} collective-permute-done((bf16[3,6144]{1,0:T(4,128)(2,1)S(1)}, bf16[3,6144]{1,0:T(4,128)(2,1)S(1)}, u32[]{:S(2)}, u32[]{:S(2)}) %collective-permute-start) | collective-permute-done | bytes 36896 | tf_op jit(solution)/shard_map/ppermute | solution.py:477
  8.2 0.8 %shard_map.93 = (bf16[1040,128]{1,0:T(8,128)(2,1)S(1)}, f32[1024,128]{1,0:T(8,128)S(1)}, f32[8,128]{1,0:T(8,128)S(1)}, bf16[128,2048]{1,0:T(8,128)(2,1)S(1)}, bf16[128,512]{1,0:T(8,128)(2,1)S(1)}) custom-call(bf16[128,6144]{1,0:T(8,128)(2,1)S(1)} %get-tuple-element.58.refs_0_, bf16[3,6144]{1,0:T(4,128)(2,1)S(1)} %collective-permute-done.refs_1_, ...), custom_call_target="tpu_custom_call" | custom-call | flops 800000000 | bytes 2400000 | tf_op jit(solution)/shard_map/pallas_call | solution.py:65
  9.0 0.1 collective-permute-start.1
  9.1 0.8 %shard_map.94 = (bf16[1040,128]{1,0:T(8,128)(2,1)S(1)}, f32[1024,128]{1,0:T(8,128)S(1)}, f32[8,128]{1,0:T(8,128)S(1)}, bf16[128,2048]{1,0:T(8,128)(2,1)S(1)}, bf16[128,512]{1,0:T(8,128)(2,1)S(1)}) custom-call(bf16[128,6144]{1,0:T(8,128)(2,1)S(1)} %get-tuple-element.58.refs_0_, bf16[3,6144]{1,0:T(4,128)(2,1)S(1)} %collective-permute-done.refs_1_, ...), custom_call_target="tpu_custom_call" | custom-call | flops 800000000 | bytes 2400000 | tf_op jit(solution)/shard_map/pallas_call | solution.py:65
  9.9 0.6 %collective-permute-start.3 = (bf16[1040,128]{1,0:T(8,128)(2,1)S(1)}, bf16[1040,128]{1,0:T(8,128)(2,1)S(1)}, u32[]{:S(2)}, u32[]{:S(2)}) collective-permute-start(bf16[1040,128]{1,0:T(8,128)(2,1)S(1)} %get-tuple-element.76), channel_id=1, source_target_pairs={{0,1},{1,0},{2,3},{3,2},{4,5},{5,4},{6,7},{7,6},{8,9},{9,8},{10,11... | collective-permute-start | bytes 798728 | tf_op jit(solution)/shard_map/ppermute | solution.py:451
  10.4 0.2 collective-permute-done.1.refs_2_.refs_4_
  10.6 0.1 shard_map.95
  10.7 0.2 collective-permute-start.2
  11.0 0.6 %collective-permute-done.3.refs_2_.refs_4_ = bf16[1040,128]{1,0:T(8,128)(2,1)S(1)} collective-permute-done((bf16[1040,128]{1,0:T(8,128)(2,1)S(1)}, bf16[1040,128]{1,0:T(8,128)(2,1)S(1)}, u32[]{:S(2)}, u32[]{:S(2)}) %collective-permute-start.3) | collective-permute-done | bytes 266272 | tf_op jit(solution)/shard_map/ppermute | solution.py:451
  11.6 0.0 copy-start.1
  11.6 0.1 shard_map.96
  11.7 1.3 %collective-permute-start.5 = (bf16[528,128]{1,0:T(8,128)(2,1)S(1)}, bf16[528,128]{1,0:T(8,128)(2,1)S(1)}, u32[]{:S(2)}, u32[]{:S(2)}) collective-permute-start(bf16[528,128]{1,0:T(8,128)(2,1)S(1)} %get-tuple-element.82), channel_id=1, source_target_pairs={{0,2},{1,3},{2,0},{3,1},{4,6},{5,7},{6,4},{7,5},{8,10},{9,11},{10,... | collective-permute-start | bytes 405512 | tf_op jit(solution)/shard_map/ppermute | solution.py:451
  13.0 4.2 %collective-permute-done.2.refs_2_.refs_5_ = bf16[528,128]{1,0:T(8,128)(2,1)S(1)} collective-permute-done((bf16[528,128]{1,0:T(8,128)(2,1)S(1)}, bf16[528,128]{1,0:T(8,128)(2,1)S(1)}, u32[]{:S(2)}, u32[]{:S(2)}) %collective-permute-start.2) | collective-permute-done | bytes 135200 | tf_op jit(solution)/shard_map/ppermute | solution.py:451
  17.2 0.1 shard_map.97
  17.3 0.3 collective-permute-start.4
  17.6 0.5 %shard_map.98.refs_2_.refs_9_.refs_0_.refs_3_ = bf16[128,1024]{1,0:T(8,128)(2,1)S(1)} custom-call(bf16[128,6144]{1,0:T(8,128)(2,1)S(1)} %get-tuple-element.58.refs_0_, bf16[3,6144]{1,0:T(4,128)(2,1)S(1)} %collective-permute-done.refs_1_, bf16[4,6144]{1,0:T(4,128)(2,1)S(1)} %get-tuple-element.59.refs_2_, f32[1,6144]{1,0:T(1,128)S(1)} %get-tuple-element.60.refs_3_, ...), custom_call_target="tpu_custom_call" | custom-call | flops 600000000 | bytes 1800000 | tf_op jit(solution)/shard_map/pallas_call | solution.py:65
  18.0 0.0 copy-done.1
  18.1 1.7 %shard_map.99 = (f32[128,2048]{1,0:T(8,128)S(1)}, f32[128,2048]{1,0:T(8,128)S(1)}) custom-call(bf16[128,2048]{1,0:T(8,128)(2,1)S(1)} %get-tuple-element.83.refs_0_, bf16[128,512]{1,0:T(8,128)(2,1)S(1)} %get-tuple-element.84.refs_1_, bf16[128,1024]{1,0:T(8,128)(2,1)S(1)} %shard_map.98.refs_2_.refs_9_.refs_0_.refs_3_, ...), custom_call_target="tpu_custom_call" | custom-call | flops 1680000000 | bytes 5040000 | tf_op jit(solution)/shard_map/pallas_call | solution.py:65
  19.7 0.0 collective-permute-done.5.refs_2_.refs_5_
  19.7 0.1 shard_map.100
  19.8 1.9 %collective-permute-start.7 = (bf16[528,128]{1,0:T(8,128)(2,1)S(1)}, bf16[528,128]{1,0:T(8,128)(2,1)S(1)}, u32[]{:S(2)}, u32[]{:S(2)}) collective-permute-start(bf16[528,128]{1,0:T(8,128)(2,1)S(1)} %get-tuple-element.96), channel_id=1, source_target_pairs={{0,4},{1,5},{2,6},{3,7},{4,0},{5,1},{6,2},{7,3},{8,12},{9,13},{10,... | collective-permute-start | bytes 405512 | tf_op jit(solution)/shard_map/ppermute | solution.py:451
  21.7 1.8 %collective-permute-done.4.refs_2_ = bf16[528,128]{1,0:T(8,128)(2,1)S(1)} collective-permute-done((bf16[528,128]{1,0:T(8,128)(2,1)S(1)}, bf16[528,128]{1,0:T(8,128)(2,1)S(1)}, u32[]{:S(2)}, u32[]{:S(2)}) %collective-permute-start.4) | collective-permute-done | bytes 135200 | tf_op jit(solution)/shard_map/ppermute | solution.py:451
  23.5 0.1 shard_map.101
  23.5 1.7 %collective-permute-start.6 = (bf16[512,128]{1,0:T(8,128)(2,1)S(1)}, bf16[512,128]{1,0:T(8,128)(2,1)S(1)}, u32[]{:S(2)}, u32[]{:S(2)}) collective-permute-start(bf16[512,128]{1,0:T(8,128)(2,1)S(1)} %get-tuple-element.90), channel_id=1, source_target_pairs={{0,12},{1,13},{2,14},{3,15},{4,8},{5,9},{6,10},{7,11},{8,4},{9,5},... | collective-permute-start | bytes 393224 | tf_op jit(solution)/shard_map/ppermute | solution.py:451
  25.3 1.4 %collective-permute-done.7.refs_2_ = bf16[528,128]{1,0:T(8,128)(2,1)S(1)} collective-permute-done((bf16[528,128]{1,0:T(8,128)(2,1)S(1)}, bf16[528,128]{1,0:T(8,128)(2,1)S(1)}, u32[]{:S(2)}, u32[]{:S(2)}) %collective-permute-start.7) | collective-permute-done | bytes 135200 | tf_op jit(solution)/shard_map/ppermute | solution.py:451
  26.7 0.1 shard_map.102
  26.8 1.5 %collective-permute-start.9 = (bf16[512,128]{1,0:T(8,128)(2,1)S(1)}, bf16[512,128]{1,0:T(8,128)(2,1)S(1)}, u32[]{:S(2)}, u32[]{:S(2)}) collective-permute-start(bf16[512,128]{1,0:T(8,128)(2,1)S(1)} %get-tuple-element.101), channel_id=1, source_target_pairs={{0,12},{1,13},{2,14},{3,15},{4,8},{5,9},{6,10},{7,11},{8,4},{9,5},... | collective-permute-start | bytes 393224 | tf_op jit(solution)/shard_map/ppermute | solution.py:451
  28.2 1.7 %shard_map.103 = (f32[128,2048]{1,0:T(8,128)S(1)}, f32[128,2048]{1,0:T(8,128)S(1)}) custom-call(bf16[128,2048]{1,0:T(8,128)(2,1)S(1)} %get-tuple-element.93.refs_0_, bf16[128,512]{1,0:T(8,128)(2,1)S(1)} %get-tuple-element.94.refs_1_, bf16[128,1024]{1,0:T(8,128)(2,1)S(1)} %shard_map.98.refs_2_.refs_9_.refs_0_.refs_3_, ...), custom_call_target="tpu_custom_call" | custom-call | flops 1680000000 | bytes 5040000 | tf_op jit(solution)/shard_map/pallas_call | solution.py:65
  29.9 1.8 %collective-permute-done.6.refs_0_ = bf16[512,128]{1,0:T(8,128)(2,1)S(1)} collective-permute-done((bf16[512,128]{1,0:T(8,128)(2,1)S(1)}, bf16[512,128]{1,0:T(8,128)(2,1)S(1)}, u32[]{:S(2)}, u32[]{:S(2)}) %collective-permute-start.6) | collective-permute-done | bytes 131104 | tf_op jit(solution)/shard_map/ppermute | solution.py:451
  31.7 0.1 shard_map.104
  31.8 0.4 %collective-permute-start.8 = (bf16[512,128]{1,0:T(8,128)(2,1)S(1)}, bf16[512,128]{1,0:T(8,128)(2,1)S(1)}, u32[]{:S(2)}, u32[]{:S(2)}) collective-permute-start(bf16[512,128]{1,0:T(8,128)(2,1)S(1)} %get-tuple-element.100), channel_id=1, source_target_pairs={{0,2},{1,3},{2,0},{3,1},{4,6},{5,7},{6,4},{7,5},{8,10},{9,11},{10,... | collective-permute-start | bytes 393224 | tf_op jit(solution)/shard_map/ppermute | solution.py:451
  32.3 1.4 %collective-permute-done.9.refs_0_ = bf16[512,128]{1,0:T(8,128)(2,1)S(1)} collective-permute-done((bf16[512,128]{1,0:T(8,128)(2,1)S(1)}, bf16[512,128]{1,0:T(8,128)(2,1)S(1)}, u32[]{:S(2)}, u32[]{:S(2)}) %collective-permute-start.9) | collective-permute-done | bytes 131104 | tf_op jit(solution)/shard_map/ppermute | solution.py:451
  33.6 0.1 shard_map.105
  33.8 0.0 copy-start
  33.8 0.4 %collective-permute-start.10 = (bf16[512,128]{1,0:T(8,128)(2,1)S(1)}, bf16[512,128]{1,0:T(8,128)(2,1)S(1)}, u32[]{:S(2)}, u32[]{:S(2)}) collective-permute-start(bf16[512,128]{1,0:T(8,128)(2,1)S(1)} %get-tuple-element.106), channel_id=1, source_target_pairs={{0,2},{1,3},{2,0},{3,1},{4,6},{5,7},{6,4},{7,5},{8,10},{9,11},{10,... | collective-permute-start | bytes 393224 | tf_op jit(solution)/shard_map/ppermute | solution.py:451
  34.2 3.0 %collective-permute-done.8.refs_1_ = bf16[512,128]{1,0:T(8,128)(2,1)S(1)} collective-permute-done((bf16[512,128]{1,0:T(8,128)(2,1)S(1)}, bf16[512,128]{1,0:T(8,128)(2,1)S(1)}, u32[]{:S(2)}, u32[]{:S(2)}) %collective-permute-start.8) | collective-permute-done | bytes 131104 | tf_op jit(solution)/shard_map/ppermute | solution.py:451
  37.2 0.2 shard_map.106
  37.4 0.1 collective-permute-start.11
  37.5 1.3 %collective-permute-done.10.refs_1_ = bf16[512,128]{1,0:T(8,128)(2,1)S(1)} collective-permute-done((bf16[512,128]{1,0:T(8,128)(2,1)S(1)}, bf16[512,128]{1,0:T(8,128)(2,1)S(1)}, u32[]{:S(2)}, u32[]{:S(2)}) %collective-permute-start.10) | collective-permute-done | bytes 131104 | tf_op jit(solution)/shard_map/ppermute | solution.py:451
  38.8 0.2 shard_map.107
  39.0 0.1 collective-permute-start.12
  39.0 0.0 copy-done
  39.0 0.3 shard_map.108.refs_5_.refs_0_
  39.4 0.0 collective-permute-done.11.refs_1_
  39.4 0.3 shard_map.109.refs_5_.refs_1_
  39.7 0.3 shard_map.110.refs_2_.refs_8_
  40.0 0.5 %collective-permute-done.12.refs_4_ = bf16[1024,128]{1,0:T(8,128)(2,1)S(1)} collective-permute-done((bf16[1024,128]{1,0:T(8,128)(2,1)S(1)}, bf16[1024,128]{1,0:T(8,128)(2,1)S(1)}, u32[]{:S(2)}, u32[]{:S(2)}) %collective-permute-start.12) | collective-permute-done | bytes 262176 | tf_op jit(solution)/shard_map/ppermute | solution.py:451
  40.6 1.2 %shard_map.111 = bf16[128,4096]{1,0:T(8,128)(2,1)} custom-call(bf16[128,1024]{1,0:T(8,128)(2,1)S(1)} %shard_map.108.refs_5_.refs_0_, bf16[128,1024]{1,0:T(8,128)(2,1)S(1)} %shard_map.109.refs_5_.refs_1_, bf16[128,1024]{1,0:T(8,128)(2,1)S(1)} %shard_map.110.refs_2_.refs_8_, bf16[128,1024]{1,0:T(8,128)(2,1)S(1)} %shard_map.98.refs_2_.refs_9_.refs_0_.refs_3_, ...), custom_call_target="tpu_custom_call" | custom-call | flops 400000000 | bytes 1200000 | tf_op jit(solution)/shard_map/pallas_call | solution.py:65
Async XLA Ops:
  1.0 7.3 %collective-permute-start = (bf16[3,6144]{1,0:T(4,128)(2,1)S(1)}, bf16[3,6144]{1,0:T(4,128)(2,1)S(1)}, u32[]{:S(2)}, u32[]{:S(2)}) collective-permute-start(bf16[3,6144]{1,0:T(4,128)(2,1)S(1)} %shard_map.92), channel_id=1, source_target_pairs={{0,1},{1,2},{2,3},{3,4},{4,5},{5,6},{6,7},{7,8},{8,9},{9,10},{10,1... | collective-permute-start | bytes 110600 | tf_op jit(solution)/shard_map/ppermute | solution.py:477
  9.0 1.6 %collective-permute-start.1 = (bf16[1040,128]{1,0:T(8,128)(2,1)S(1)}, bf16[1040,128]{1,0:T(8,128)(2,1)S(1)}, u32[]{:S(2)}, u32[]{:S(2)}) collective-permute-start(bf16[1040,128]{1,0:T(8,128)(2,1)S(1)} %get-tuple-element.68), channel_id=1, source_target_pairs={{0,1},{1,0},{2,3},{3,2},{4,5},{5,4},{6,7},{7,6},{8,9},{9,8},{10,11... | collective-permute-start | bytes 798728 | tf_op jit(solution)/shard_map/ppermute | solution.py:451
  9.9 1.7 %collective-permute-start.3 = (bf16[1040,128]{1,0:T(8,128)(2,1)S(1)}, bf16[1040,128]{1,0:T(8,128)(2,1)S(1)}, u32[]{:S(2)}, u32[]{:S(2)}) collective-permute-start(bf16[1040,128]{1,0:T(8,128)(2,1)S(1)} %get-tuple-element.76), channel_id=1, source_target_pairs={{0,1},{1,0},{2,3},{3,2},{4,5},{5,4},{6,7},{7,6},{8,9},{9,8},{10,11... | collective-permute-start | bytes 798728 | tf_op jit(solution)/shard_map/ppermute | solution.py:451
  10.7 6.5 %collective-permute-start.2 = (bf16[528,128]{1,0:T(8,128)(2,1)S(1)}, bf16[528,128]{1,0:T(8,128)(2,1)S(1)}, u32[]{:S(2)}, u32[]{:S(2)}) collective-permute-start(bf16[528,128]{1,0:T(8,128)(2,1)S(1)} %get-tuple-element.74), channel_id=1, source_target_pairs={{0,2},{1,3},{2,0},{3,1},{4,6},{5,7},{6,4},{7,5},{8,10},{9,11},{10,... | collective-permute-start | bytes 405512 | tf_op jit(solution)/shard_map/ppermute | solution.py:451
  11.6 6.5 %copy-start.1 = (bf16[128,4096]{1,0:T(8,128)(2,1)S(1)}, bf16[128,4096]{1,0:T(8,128)(2,1)}, u32[]{:S(2)}) copy-start(bf16[128,4096]{1,0:T(8,128)(2,1)} %refs_8_.3) | copy-start | bytes 3145732
  11.7 8.0 %collective-permute-start.5 = (bf16[528,128]{1,0:T(8,128)(2,1)S(1)}, bf16[528,128]{1,0:T(8,128)(2,1)S(1)}, u32[]{:S(2)}, u32[]{:S(2)}) collective-permute-start(bf16[528,128]{1,0:T(8,128)(2,1)S(1)} %get-tuple-element.82), channel_id=1, source_target_pairs={{0,2},{1,3},{2,0},{3,1},{4,6},{5,7},{6,4},{7,5},{8,10},{9,11},{10,... | collective-permute-start | bytes 405512 | tf_op jit(solution)/shard_map/ppermute | solution.py:451
  17.3 6.2 %collective-permute-start.4 = (bf16[528,128]{1,0:T(8,128)(2,1)S(1)}, bf16[528,128]{1,0:T(8,128)(2,1)S(1)}, u32[]{:S(2)}, u32[]{:S(2)}) collective-permute-start(bf16[528,128]{1,0:T(8,128)(2,1)S(1)} %get-tuple-element.80), channel_id=1, source_target_pairs={{0,4},{1,5},{2,6},{3,7},{4,0},{5,1},{6,2},{7,3},{8,12},{9,13},{10,... | collective-permute-start | bytes 405512 | tf_op jit(solution)/shard_map/ppermute | solution.py:451
  19.8 6.9 %collective-permute-start.7 = (bf16[528,128]{1,0:T(8,128)(2,1)S(1)}, bf16[528,128]{1,0:T(8,128)(2,1)S(1)}, u32[]{:S(2)}, u32[]{:S(2)}) collective-permute-start(bf16[528,128]{1,0:T(8,128)(2,1)S(1)} %get-tuple-element.96), channel_id=1, source_target_pairs={{0,4},{1,5},{2,6},{3,7},{4,0},{5,1},{6,2},{7,3},{8,12},{9,13},{10,... | collective-permute-start | bytes 405512 | tf_op jit(solution)/shard_map/ppermute | solution.py:451
  23.5 8.2 %collective-permute-start.6 = (bf16[512,128]{1,0:T(8,128)(2,1)S(1)}, bf16[512,128]{1,0:T(8,128)(2,1)S(1)}, u32[]{:S(2)}, u32[]{:S(2)}) collective-permute-start(bf16[512,128]{1,0:T(8,128)(2,1)S(1)} %get-tuple-element.90), channel_id=1, source_target_pairs={{0,12},{1,13},{2,14},{3,15},{4,8},{5,9},{6,10},{7,11},{8,4},{9,5},... | collective-permute-start | bytes 393224 | tf_op jit(solution)/shard_map/ppermute | solution.py:451
  26.8 6.9 %collective-permute-start.9 = (bf16[512,128]{1,0:T(8,128)(2,1)S(1)}, bf16[512,128]{1,0:T(8,128)(2,1)S(1)}, u32[]{:S(2)}, u32[]{:S(2)}) collective-permute-start(bf16[512,128]{1,0:T(8,128)(2,1)S(1)} %get-tuple-element.101), channel_id=1, source_target_pairs={{0,12},{1,13},{2,14},{3,15},{4,8},{5,9},{6,10},{7,11},{8,4},{9,5},... | collective-permute-start | bytes 393224 | tf_op jit(solution)/shard_map/ppermute | solution.py:451
  31.8 5.4 %collective-permute-start.8 = (bf16[512,128]{1,0:T(8,128)(2,1)S(1)}, bf16[512,128]{1,0:T(8,128)(2,1)S(1)}, u32[]{:S(2)}, u32[]{:S(2)}) collective-permute-start(bf16[512,128]{1,0:T(8,128)(2,1)S(1)} %get-tuple-element.100), channel_id=1, source_target_pairs={{0,2},{1,3},{2,0},{3,1},{4,6},{5,7},{6,4},{7,5},{8,10},{9,11},{10,... | collective-permute-start | bytes 393224 | tf_op jit(solution)/shard_map/ppermute | solution.py:451
  33.8 5.3 %copy-start = (f32[4096]{0:T(1024)S(1)}, f32[4096]{0:T(1024)}, u32[]{:S(2)}) copy-start(f32[4096]{0:T(1024)} %param.17) | copy-start | bytes 49156
  33.8 5.0 %collective-permute-start.10 = (bf16[512,128]{1,0:T(8,128)(2,1)S(1)}, bf16[512,128]{1,0:T(8,128)(2,1)S(1)}, u32[]{:S(2)}, u32[]{:S(2)}) collective-permute-start(bf16[512,128]{1,0:T(8,128)(2,1)S(1)} %get-tuple-element.106), channel_id=1, source_target_pairs={{0,2},{1,3},{2,0},{3,1},{4,6},{5,7},{6,4},{7,5},{8,10},{9,11},{10,... | collective-permute-start | bytes 393224 | tf_op jit(solution)/shard_map/ppermute | solution.py:451
  37.4 2.0 %collective-permute-start.11 = (bf16[1024,128]{1,0:T(8,128)(2,1)S(1)}, bf16[1024,128]{1,0:T(8,128)(2,1)S(1)}, u32[]{:S(2)}, u32[]{:S(2)}) collective-permute-start(bf16[1024,128]{1,0:T(8,128)(2,1)S(1)} %get-tuple-element.108), channel_id=1, source_target_pairs={{0,1},{1,0},{2,3},{3,2},{4,5},{5,4},{6,7},{7,6},{8,9},{9,8},{10,11... | collective-permute-start | bytes 786440 | tf_op jit(solution)/shard_map/ppermute | solution.py:451
  39.0 1.6 %collective-permute-start.12 = (bf16[1024,128]{1,0:T(8,128)(2,1)S(1)}, bf16[1024,128]{1,0:T(8,128)(2,1)S(1)}, u32[]{:S(2)}, u32[]{:S(2)}) collective-permute-start(bf16[1024,128]{1,0:T(8,128)(2,1)S(1)} %get-tuple-element.110), channel_id=1, source_target_pairs={{0,1},{1,0},{2,3},{3,2},{4,5},{5,4},{6,7},{7,6},{8,9},{9,8},{10,11... | collective-permute-start | bytes 786440 | tf_op jit(solution)/shard_map/ppermute | solution.py:451

commit v8 on v6

--- a/solution.py
+++ b/solution.py
@@ -120,17 +120,14 @@
 
 def convolve_body(source, weight, bias, spans, outs):
     for (start, width), out in zip(spans, outs):
-        block = min(width, 256)
-
-        @pl.loop(0, width // block)
-        def _(i, start=start, out=out, block=block):
-            cols = columns(i, block, start)
+        for i in range(width // LANES):
+            cols = slice(start + i * LANES, start + (i + 1) * LANES)
             here = source[:, cols].astype(F32)
             taps, total = halved_taps(weight, bias, cols)
             total = total + taps[3:4] * here
             for back in range(1, 4):
                 total = total + taps[3 - back : 4 - back] * pltpu.roll(here, back, 0)
-            out[:, columns(i, block)] = silu_of_twice(total).astype(BF16)
+            out[:, i * LANES : (i + 1) * LANES] = silu_of_twice(total).astype(BF16)
 
 
 def convolve_head(source, halo, weight, bias, padded, spans, outs):

time: 42 us -> 42 us (level)
  starting transfers between devices: 9.07 us -> 9.66 us
    ppermute x12, starting transfers between devices: 8.56 us -> 9.15 us  [across(): lax.ppermute(value, 'seq', [(i, i ^ flipped) for i in range(devices)])]
    ppermute x12, waiting for transfers between devices: 16.2 us -> 15.7 us  [across(): lax.ppermute(value, 'seq', [(i, i ^ flipped) for i in range(devices)])]
where the time goes in v8:
time: 42 us; the launch traced here: 41.7 us
  waiting for transfers between devices  19.5 us (46%)
  Pallas kernels  11.5 us (27%)
  starting transfers between devices  9.66 us (23%)
  local copies, waits for them, and re-layouts  0.93 us (2%)
    ppermute x12, waiting for transfers between devices, across(): lax.ppermute(value, 'seq', [(i, i ^ flipped) for i in range(devices)])  15.7 us
    pallas_call x20, Pallas kernels, call(): pl.pallas_call(kernel, out_shape=[space(shape, kind) for shape, kind, spa...  11.5 us
    ppermute x12, starting transfers between devices, across(): lax.ppermute(value, 'seq', [(i, i ^ flipped) for i in range(devices)])  9.15 us
    ppermute x1, waiting for transfers between devices, shards(): lax.ppermute(mixer_input[SPAN - 3:], 'seq', [(i, (i + 1) % devices) for i...  3.81 us
    slice x1, local copies, waits for them, and re-layouts, shards(): mixer_input[SPAN - 3:]  0.92 us
  transfers between devices with their start and end apart: 13, of which 11 were waited for; matrix products, arithmetic and copies ran while one was open for 0% of the time, Pallas kernels for 23%

profile of v8, /device:TPU:0, one launch (start us, length us, event | category | flops | bytes accessed | tf_op | source)
XLA Modules:
  0.0 41.7 jit_solution(13528907323988316892)
XLA Ops:
  0.0 0.9 %slice.3 = bf16[3,6144]{1,0:T(4,128)(2,1)S(1)} slice(bf16[128,6144]{1,0:T(8,128)(2,1)} %refs_0_.1), slice={[125:128], [0:6144]} | slice | bytes 73728 | tf_op jit(solution)/shard_map/slice | solution.py:463
  0.9 0.5 %collective-permute-start = (bf16[3,6144]{1,0:T(4,128)(2,1)S(1)}, bf16[3,6144]{1,0:T(4,128)(2,1)S(1)}, u32[]{:S(2)}, u32[]{:S(2)}) collective-permute-start(bf16[3,6144]{1,0:T(4,128)(2,1)S(1)} %slice.3), channel_id=1, source_target_pairs={{0,1},{1,2},{2,3},{3,4},{4,5},{5,6},{6,7},{7,8},{8,9},{9,10},{10,1... | collective-permute-start | bytes 110600 | tf_op jit(solution)/shard_map/ppermute | solution.py:463
  1.4 2.9 %shard_map.91 = (bf16[128,6144]{1,0:T(8,128)(2,1)S(1)}, bf16[4,6144]{1,0:T(4,128)(2,1)S(1)}, f32[1,6144]{1,0:T(1,128)S(1)}, f32[128,128]{1,0:T(8,128)S(1)}, f32[...) custom-call(bf16[128,6144]{1,0:T(8,128)(2,1)} %refs_0_.1, ...), custom_call_target="tpu_custom_call" | custom-call | flops 2500000000 | bytes 7500000 | tf_op jit(solution)/shard_map/pallas_call | solution.py:65
  4.4 3.8 %collective-permute-done.refs_1_ = bf16[3,6144]{1,0:T(4,128)(2,1)S(1)} collective-permute-done((bf16[3,6144]{1,0:T(4,128)(2,1)S(1)}, bf16[3,6144]{1,0:T(4,128)(2,1)S(1)}, u32[]{:S(2)}, u32[]{:S(2)}) %collective-permute-start) | collective-permute-done | bytes 36896 | tf_op jit(solution)/shard_map/ppermute | solution.py:463
  8.2 0.8 %shard_map.92 = (bf16[1040,128]{1,0:T(8,128)(2,1)S(1)}, f32[1024,128]{1,0:T(8,128)S(1)}, f32[8,128]{1,0:T(8,128)S(1)}, bf16[128,2048]{1,0:T(8,128)(2,1)S(1)}, bf16[128,512]{1,0:T(8,128)(2,1)S(1)}) custom-call(bf16[128,6144]{1,0:T(8,128)(2,1)S(1)} %get-tuple-element.58.refs_0_, bf16[3,6144]{1,0:T(4,128)(2,1)S(1)} %collective-permute-done.refs_1_, ...), custom_call_target="tpu_custom_call" | custom-call | flops 800000000 | bytes 2400000 | tf_op jit(solution)/shard_map/pallas_call | solution.py:65
  9.0 0.1 collective-permute-start.1
  9.0 0.8 %shard_map.93 = (bf16[1040,128]{1,0:T(8,128)(2,1)S(1)}, f32[1024,128]{1,0:T(8,128)S(1)}, f32[8,128]{1,0:T(8,128)S(1)}, bf16[128,2048]{1,0:T(8,128)(2,1)S(1)}, bf16[128,512]{1,0:T(8,128)(2,1)S(1)}) custom-call(bf16[128,6144]{1,0:T(8,128)(2,1)S(1)} %get-tuple-element.58.refs_0_, bf16[3,6144]{1,0:T(4,128)(2,1)S(1)} %collective-permute-done.refs_1_, ...), custom_call_target="tpu_custom_call" | custom-call | flops 800000000 | bytes 2400000 | tf_op jit(solution)/shard_map/pallas_call | solution.py:65
  9.8 0.5 %collective-permute-start.3 = (bf16[1040,128]{1,0:T(8,128)(2,1)S(1)}, bf16[1040,128]{1,0:T(8,128)(2,1)S(1)}, u32[]{:S(2)}, u32[]{:S(2)}) collective-permute-start(bf16[1040,128]{1,0:T(8,128)(2,1)S(1)} %get-tuple-element.76), channel_id=1, source_target_pairs={{0,1},{1,0},{2,3},{3,2},{4,5},{5,4},{6,7},{7,6},{8,9},{9,8},{10,11... | collective-permute-start | bytes 798728 | tf_op jit(solution)/shard_map/ppermute | solution.py:441
  10.4 0.2 collective-permute-done.1.refs_2_.refs_4_
  10.6 0.1 shard_map.94
  10.7 0.1 collective-permute-start.2
  10.8 0.8 %collective-permute-done.3.refs_2_.refs_4_ = bf16[1040,128]{1,0:T(8,128)(2,1)S(1)} collective-permute-done((bf16[1040,128]{1,0:T(8,128)(2,1)S(1)}, bf16[1040,128]{1,0:T(8,128)(2,1)S(1)}, u32[]{:S(2)}, u32[]{:S(2)}) %collective-permute-start.3) | collective-permute-done | bytes 266272 | tf_op jit(solution)/shard_map/ppermute | solution.py:441
  11.5 0.0 copy-start.1
  11.6 0.1 shard_map.95
  11.7 1.3 %collective-permute-start.5 = (bf16[528,128]{1,0:T(8,128)(2,1)S(1)}, bf16[528,128]{1,0:T(8,128)(2,1)S(1)}, u32[]{:S(2)}, u32[]{:S(2)}) collective-permute-start(bf16[528,128]{1,0:T(8,128)(2,1)S(1)} %get-tuple-element.82), channel_id=1, source_target_pairs={{0,2},{1,3},{2,0},{3,1},{4,6},{5,7},{6,4},{7,5},{8,10},{9,11},{10,... | collective-permute-start | bytes 405512 | tf_op jit(solution)/shard_map/ppermute | solution.py:441
  13.0 4.2 %collective-permute-done.2.refs_2_.refs_5_ = bf16[528,128]{1,0:T(8,128)(2,1)S(1)} collective-permute-done((bf16[528,128]{1,0:T(8,128)(2,1)S(1)}, bf16[528,128]{1,0:T(8,128)(2,1)S(1)}, u32[]{:S(2)}, u32[]{:S(2)}) %collective-permute-start.2) | collective-permute-done | bytes 135200 | tf_op jit(solution)/shard_map/ppermute | solution.py:441
  17.2 0.1 shard_map.96
  17.3 0.3 collective-permute-start.4
  17.5 0.4 %shard_map.97.refs_2_.refs_9_.refs_0_.refs_3_ = bf16[128,1024]{1,0:T(8,128)(2,1)S(1)} custom-call(bf16[128,6144]{1,0:T(8,128)(2,1)S(1)} %get-tuple-element.58.refs_0_, bf16[3,6144]{1,0:T(4,128)(2,1)S(1)} %collective-permute-done.refs_1_, bf16[4,6144]{1,0:T(4,128)(2,1)S(1)} %get-tuple-element.59.refs_2_, f32[1,6144]{1,0:T(1,128)S(1)} %get-tuple-element.60.refs_3_, ...), custom_call_target="tpu_custom_call" | custom-call | flops 600000000 | bytes 1800000 | tf_op jit(solution)/shard_map/pallas_call | solution.py:65
  18.0 0.0 copy-done.1
  18.0 1.7 %shard_map.98 = (f32[128,2048]{1,0:T(8,128)S(1)}, f32[128,2048]{1,0:T(8,128)S(1)}) custom-call(bf16[128,2048]{1,0:T(8,128)(2,1)S(1)} %get-tuple-element.83.refs_0_, bf16[128,512]{1,0:T(8,128)(2,1)S(1)} %get-tuple-element.84.refs_1_, bf16[128,1024]{1,0:T(8,128)(2,1)S(1)} %shard_map.97.refs_2_.refs_9_.refs_0_.refs_3_, ...), custom_call_target="tpu_custom_call" | custom-call | flops 1680000000 | bytes 5040000 | tf_op jit(solution)/shard_map/pallas_call | solution.py:65
  19.7 0.0 collective-permute-done.5.refs_2_.refs_5_
  19.7 0.1 shard_map.99
  19.8 1.9 %collective-permute-start.7 = (bf16[528,128]{1,0:T(8,128)(2,1)S(1)}, bf16[528,128]{1,0:T(8,128)(2,1)S(1)}, u32[]{:S(2)}, u32[]{:S(2)}) collective-permute-start(bf16[528,128]{1,0:T(8,128)(2,1)S(1)} %get-tuple-element.96), channel_id=1, source_target_pairs={{0,4},{1,5},{2,6},{3,7},{4,0},{5,1},{6,2},{7,3},{8,12},{9,13},{10,... | collective-permute-start | bytes 405512 | tf_op jit(solution)/shard_map/ppermute | solution.py:441
  21.6 1.8 %collective-permute-done.4.refs_2_ = bf16[528,128]{1,0:T(8,128)(2,1)S(1)} collective-permute-done((bf16[528,128]{1,0:T(8,128)(2,1)S(1)}, bf16[528,128]{1,0:T(8,128)(2,1)S(1)}, u32[]{:S(2)}, u32[]{:S(2)}) %collective-permute-start.4) | collective-permute-done | bytes 135200 | tf_op jit(solution)/shard_map/ppermute | solution.py:441
  23.4 0.1 shard_map.100
  23.5 2.2 %collective-permute-start.6 = (bf16[512,128]{1,0:T(8,128)(2,1)S(1)}, bf16[512,128]{1,0:T(8,128)(2,1)S(1)}, u32[]{:S(2)}, u32[]{:S(2)}) collective-permute-start(bf16[512,128]{1,0:T(8,128)(2,1)S(1)} %get-tuple-element.90), channel_id=1, source_target_pairs={{0,12},{1,13},{2,14},{3,15},{4,8},{5,9},{6,10},{7,11},{8,4},{9,5},... | collective-permute-start | bytes 393224 | tf_op jit(solution)/shard_map/ppermute | solution.py:441
  25.7 1.0 %collective-permute-done.7.refs_2_ = bf16[528,128]{1,0:T(8,128)(2,1)S(1)} collective-permute-done((bf16[528,128]{1,0:T(8,128)(2,1)S(1)}, bf16[528,128]{1,0:T(8,128)(2,1)S(1)}, u32[]{:S(2)}, u32[]{:S(2)}) %collective-permute-start.7) | collective-permute-done | bytes 135200 | tf_op jit(solution)/shard_map/ppermute | solution.py:441
  26.6 0.1 shard_map.101
  26.7 2.1 %collective-permute-start.9 = (bf16[512,128]{1,0:T(8,128)(2,1)S(1)}, bf16[512,128]{1,0:T(8,128)(2,1)S(1)}, u32[]{:S(2)}, u32[]{:S(2)}) collective-permute-start(bf16[512,128]{1,0:T(8,128)(2,1)S(1)} %get-tuple-element.101), channel_id=1, source_target_pairs={{0,12},{1,13},{2,14},{3,15},{4,8},{5,9},{6,10},{7,11},{8,4},{9,5},... | collective-permute-start | bytes 393224 | tf_op jit(solution)/shard_map/ppermute | solution.py:441
  28.8 1.7 %shard_map.102 = (f32[128,2048]{1,0:T(8,128)S(1)}, f32[128,2048]{1,0:T(8,128)S(1)}) custom-call(bf16[128,2048]{1,0:T(8,128)(2,1)S(1)} %get-tuple-element.93.refs_0_, bf16[128,512]{1,0:T(8,128)(2,1)S(1)} %get-tuple-element.94.refs_1_, bf16[128,1024]{1,0:T(8,128)(2,1)S(1)} %shard_map.97.refs_2_.refs_9_.refs_0_.refs_3_, ...), custom_call_target="tpu_custom_call" | custom-call | flops 1680000000 | bytes 5040000 | tf_op jit(solution)/shard_map/pallas_call | solution.py:65
  30.5 1.2 %collective-permute-done.6.refs_0_ = bf16[512,128]{1,0:T(8,128)(2,1)S(1)} collective-permute-done((bf16[512,128]{1,0:T(8,128)(2,1)S(1)}, bf16[512,128]{1,0:T(8,128)(2,1)S(1)}, u32[]{:S(2)}, u32[]{:S(2)}) %collective-permute-start.6) | collective-permute-done | bytes 131104 | tf_op jit(solution)/shard_map/ppermute | solution.py:441
  31.7 0.1 shard_map.103
  31.8 0.3 collective-permute-start.8
  32.1 1.5 %collective-permute-done.9.refs_0_ = bf16[512,128]{1,0:T(8,128)(2,1)S(1)} collective-permute-done((bf16[512,128]{1,0:T(8,128)(2,1)S(1)}, bf16[512,128]{1,0:T(8,128)(2,1)S(1)}, u32[]{:S(2)}, u32[]{:S(2)}) %collective-permute-start.9) | collective-permute-done | bytes 131104 | tf_op jit(solution)/shard_map/ppermute | solution.py:441
  33.6 0.1 shard_map.104
  33.7 0.0 copy-start
  33.7 0.4 collective-permute-start.10
  34.1 3.1 %collective-permute-done.8.refs_1_ = bf16[512,128]{1,0:T(8,128)(2,1)S(1)} collective-permute-done((bf16[512,128]{1,0:T(8,128)(2,1)S(1)}, bf16[512,128]{1,0:T(8,128)(2,1)S(1)}, u32[]{:S(2)}, u32[]{:S(2)}) %collective-permute-start.8) | collective-permute-done | bytes 131104 | tf_op jit(solution)/shard_map/ppermute | solution.py:441
  37.2 0.2 shard_map.105
  37.4 0.1 collective-permute-start.11
  37.4 1.3 %collective-permute-done.10.refs_1_ = bf16[512,128]{1,0:T(8,128)(2,1)S(1)} collective-permute-done((bf16[512,128]{1,0:T(8,128)(2,1)S(1)}, bf16[512,128]{1,0:T(8,128)(2,1)S(1)}, u32[]{:S(2)}, u32[]{:S(2)}) %collective-permute-start.10) | collective-permute-done | bytes 131104 | tf_op jit(solution)/shard_map/ppermute | solution.py:441
  38.8 0.2 shard_map.106
  38.9 0.1 collective-permute-start.12
  39.0 0.0 copy-done
  39.0 0.3 shard_map.107.refs_5_.refs_0_
  39.3 0.0 collective-permute-done.11.refs_1_
  39.3 0.3 shard_map.108.refs_5_.refs_1_
  39.7 0.3 shard_map.109.refs_2_.refs_8_
  40.0 0.5 %collective-permute-done.12.refs_4_ = bf16[1024,128]{1,0:T(8,128)(2,1)S(1)} collective-permute-done((bf16[1024,128]{1,0:T(8,128)(2,1)S(1)}, bf16[1024,128]{1,0:T(8,128)(2,1)S(1)}, u32[]{:S(2)}, u32[]{:S(2)}) %collective-permute-start.12) | collective-permute-done | bytes 262176 | tf_op jit(solution)/shard_map/ppermute | solution.py:441
  40.5 1.2 %shard_map.110 = bf16[128,4096]{1,0:T(8,128)(2,1)} custom-call(bf16[128,1024]{1,0:T(8,128)(2,1)S(1)} %shard_map.107.refs_5_.refs_0_, bf16[128,1024]{1,0:T(8,128)(2,1)S(1)} %shard_map.108.refs_5_.refs_1_, bf16[128,1024]{1,0:T(8,128)(2,1)S(1)} %shard_map.109.refs_2_.refs_8_, bf16[128,1024]{1,0:T(8,128)(2,1)S(1)} %shard_map.97.refs_2_.refs_9_.refs_0_.refs_3_, ...), custom_call_target="tpu_custom_call" | custom-call | flops 400000000 | bytes 1200000 | tf_op jit(solution)/shard_map/pallas_call | solution.py:65
Async XLA Ops:
  0.9 7.3 %collective-permute-start = (bf16[3,6144]{1,0:T(4,128)(2,1)S(1)}, bf16[3,6144]{1,0:T(4,128)(2,1)S(1)}, u32[]{:S(2)}, u32[]{:S(2)}) collective-permute-start(bf16[3,6144]{1,0:T(4,128)(2,1)S(1)} %slice.3), channel_id=1, source_target_pairs={{0,1},{1,2},{2,3},{3,4},{4,5},{5,6},{6,7},{7,8},{8,9},{9,10},{10,1... | collective-permute-start | bytes 110600 | tf_op jit(solution)/shard_map/ppermute | solution.py:463
  9.0 1.6 %collective-permute-start.1 = (bf16[1040,128]{1,0:T(8,128)(2,1)S(1)}, bf16[1040,128]{1,0:T(8,128)(2,1)S(1)}, u32[]{:S(2)}, u32[]{:S(2)}) collective-permute-start(bf16[1040,128]{1,0:T(8,128)(2,1)S(1)} %get-tuple-element.68), channel_id=1, source_target_pairs={{0,1},{1,0},{2,3},{3,2},{4,5},{5,4},{6,7},{7,6},{8,9},{9,8},{10,11... | collective-permute-start | bytes 798728 | tf_op jit(solution)/shard_map/ppermute | solution.py:441
  9.8 1.7 %collective-permute-start.3 = (bf16[1040,128]{1,0:T(8,128)(2,1)S(1)}, bf16[1040,128]{1,0:T(8,128)(2,1)S(1)}, u32[]{:S(2)}, u32[]{:S(2)}) collective-permute-start(bf16[1040,128]{1,0:T(8,128)(2,1)S(1)} %get-tuple-element.76), channel_id=1, source_target_pairs={{0,1},{1,0},{2,3},{3,2},{4,5},{5,4},{6,7},{7,6},{8,9},{9,8},{10,11... | collective-permute-start | bytes 798728 | tf_op jit(solution)/shard_map/ppermute | solution.py:441
  10.7 6.5 %collective-permute-start.2 = (bf16[528,128]{1,0:T(8,128)(2,1)S(1)}, bf16[528,128]{1,0:T(8,128)(2,1)S(1)}, u32[]{:S(2)}, u32[]{:S(2)}) collective-permute-start(bf16[528,128]{1,0:T(8,128)(2,1)S(1)} %get-tuple-element.74), channel_id=1, source_target_pairs={{0,2},{1,3},{2,0},{3,1},{4,6},{5,7},{6,4},{7,5},{8,10},{9,11},{10,... | collective-permute-start | bytes 405512 | tf_op jit(solution)/shard_map/ppermute | solution.py:441
  11.5 6.4 %copy-start.1 = (bf16[128,4096]{1,0:T(8,128)(2,1)S(1)}, bf16[128,4096]{1,0:T(8,128)(2,1)}, u32[]{:S(2)}) copy-start(bf16[128,4096]{1,0:T(8,128)(2,1)} %refs_8_.3) | copy-start | bytes 3145732
  11.7 8.0 %collective-permute-start.5 = (bf16[528,128]{1,0:T(8,128)(2,1)S(1)}, bf16[528,128]{1,0:T(8,128)(2,1)S(1)}, u32[]{:S(2)}, u32[]{:S(2)}) collective-permute-start(bf16[528,128]{1,0:T(8,128)(2,1)S(1)} %get-tuple-element.82), channel_id=1, source_target_pairs={{0,2},{1,3},{2,0},{3,1},{4,6},{5,7},{6,4},{7,5},{8,10},{9,11},{10,... | collective-permute-start | bytes 405512 | tf_op jit(solution)/shard_map/ppermute | solution.py:441
  17.3 6.2 %collective-permute-start.4 = (bf16[528,128]{1,0:T(8,128)(2,1)S(1)}, bf16[528,128]{1,0:T(8,128)(2,1)S(1)}, u32[]{:S(2)}, u32[]{:S(2)}) collective-permute-start(bf16[528,128]{1,0:T(8,128)(2,1)S(1)} %get-tuple-element.80), channel_id=1, source_target_pairs={{0,4},{1,5},{2,6},{3,7},{4,0},{5,1},{6,2},{7,3},{8,12},{9,13},{10,... | collective-permute-start | bytes 405512 | tf_op jit(solution)/shard_map/ppermute | solution.py:441
  19.8 6.9 %collective-permute-start.7 = (bf16[528,128]{1,0:T(8,128)(2,1)S(1)}, bf16[528,128]{1,0:T(8,128)(2,1)S(1)}, u32[]{:S(2)}, u32[]{:S(2)}) collective-permute-start(bf16[528,128]{1,0:T(8,128)(2,1)S(1)} %get-tuple-element.96), channel_id=1, source_target_pairs={{0,4},{1,5},{2,6},{3,7},{4,0},{5,1},{6,2},{7,3},{8,12},{9,13},{10,... | collective-permute-start | bytes 405512 | tf_op jit(solution)/shard_map/ppermute | solution.py:441
  23.5 8.2 %collective-permute-start.6 = (bf16[512,128]{1,0:T(8,128)(2,1)S(1)}, bf16[512,128]{1,0:T(8,128)(2,1)S(1)}, u32[]{:S(2)}, u32[]{:S(2)}) collective-permute-start(bf16[512,128]{1,0:T(8,128)(2,1)S(1)} %get-tuple-element.90), channel_id=1, source_target_pairs={{0,12},{1,13},{2,14},{3,15},{4,8},{5,9},{6,10},{7,11},{8,4},{9,5},... | collective-permute-start | bytes 393224 | tf_op jit(solution)/shard_map/ppermute | solution.py:441
  26.7 6.9 %collective-permute-start.9 = (bf16[512,128]{1,0:T(8,128)(2,1)S(1)}, bf16[512,128]{1,0:T(8,128)(2,1)S(1)}, u32[]{:S(2)}, u32[]{:S(2)}) collective-permute-start(bf16[512,128]{1,0:T(8,128)(2,1)S(1)} %get-tuple-element.101), channel_id=1, source_target_pairs={{0,12},{1,13},{2,14},{3,15},{4,8},{5,9},{6,10},{7,11},{8,4},{9,5},... | collective-permute-start | bytes 393224 | tf_op jit(solution)/shard_map/ppermute | solution.py:441
  31.8 5.4 %collective-permute-start.8 = (bf16[512,128]{1,0:T(8,128)(2,1)S(1)}, bf16[512,128]{1,0:T(8,128)(2,1)S(1)}, u32[]{:S(2)}, u32[]{:S(2)}) collective-permute-start(bf16[512,128]{1,0:T(8,128)(2,1)S(1)} %get-tuple-element.100), channel_id=1, source_target_pairs={{0,2},{1,3},{2,0},{3,1},{4,6},{5,7},{6,4},{7,5},{8,10},{9,11},{10,... | collective-permute-start | bytes 393224 | tf_op jit(solution)/shard_map/ppermute | solution.py:441
  33.7 5.3 %copy-start = (f32[4096]{0:T(1024)S(1)}, f32[4096]{0:T(1024)}, u32[]{:S(2)}) copy-start(f32[4096]{0:T(1024)} %param.17) | copy-start | bytes 49156
  33.7 5.0 %collective-permute-start.10 = (bf16[512,128]{1,0:T(8,128)(2,1)S(1)}, bf16[512,128]{1,0:T(8,128)(2,1)S(1)}, u32[]{:S(2)}, u32[]{:S(2)}) collective-permute-start(bf16[512,128]{1,0:T(8,128)(2,1)S(1)} %get-tuple-element.106), channel_id=1, source_target_pairs={{0,2},{1,3},{2,0},{3,1},{4,6},{5,7},{6,4},{7,5},{8,10},{9,11},{10,... | collective-permute-start | bytes 393224 | tf_op jit(solution)/shard_map/ppermute | solution.py:441
  37.4 2.0 %collective-permute-start.11 = (bf16[1024,128]{1,0:T(8,128)(2,1)S(1)}, bf16[1024,128]{1,0:T(8,128)(2,1)S(1)}, u32[]{:S(2)}, u32[]{:S(2)}) collective-permute-start(bf16[1024,128]{1,0:T(8,128)(2,1)S(1)} %get-tuple-element.108), channel_id=1, source_target_pairs={{0,1},{1,0},{2,3},{3,2},{4,5},{5,4},{6,7},{7,6},{8,9},{9,8},{10,11... | collective-permute-start | bytes 786440 | tf_op jit(solution)/shard_map/ppermute | solution.py:441
  38.9 1.6 %collective-permute-start.12 = (bf16[1024,128]{1,0:T(8,128)(2,1)S(1)}, bf16[1024,128]{1,0:T(8,128)(2,1)S(1)}, u32[]{:S(2)}, u32[]{:S(2)}) collective-permute-start(bf16[1024,128]{1,0:T(8,128)(2,1)S(1)} %get-tuple-element.110), channel_id=1, source_target_pairs={{0,1},{1,0},{2,3},{3,2},{4,5},{5,4},{6,7},{7,6},{8,9},{9,8},{10,11... | collective-permute-start | bytes 786440 | tf_op jit(solution)/shard_map/ppermute | solution.py:441
